TPU v7x, 32 devices: a whole 2x2x4 slice. The times are simulated.
32 devices in a mesh: row: 4 (over y, core), col: 8 (over z, x).
Axes of the slice: x: 2, y: 2, z: 4, core: 2. Of those that a mesh axis runs over, the one named last changes fastest.
Arguments:
- positions: float32 [3, 32768], P(None, ('col', 'row')), may hold values from 0 to 16
- velocity: float32 [3, 32768], P(None, ('col', 'row')), may hold values from -6 to 6
- applied: float32 [3, 32768], P(None, ('col', 'row')), may hold values from -12 to 12
- suscept: float32 [32768], P(('col', 'row')), may hold values from 0.05 to 0.3
- contact_owner: int32 [8, 4, 8, 512], P('col', 'row'), may hold values from 0 to 1023
- contact_partner: int32 [8, 4, 8, 512], P('col', 'row'), may hold values from 0 to 1023
- contact_count: int32 [8, 4, 8], P('col', 'row'), may hold values from 1 to 512, as said below
Outputs:
- moments: float32 [3, 32768], P(None, ('col', 'row'))
- forces: float32 [3, 32768], P(None, ('col', 'row'))
Inputs may be any that keep to these rules, and one draw needn't show every extreme that they name: `contact_count`: in every draw one column receives full blocks of 512 live slots from every device; the other columns' blocks are filled to different depths.
All inputs are finite; a program needn't handle non-finite values.
Results may differ from a plain program's by a relative error of at most 0.0003.
Values sent between devices are 32-bit elements; how exact they have to be, the bound alone decides.
No kernel may reach another device: no remote copies, remote signals or barrier semaphores. Data moves between devices by JAX's collectives and lax.ppermute only.
A program may use at most 64 MiB of HBM per device.

v0:
```python
import math

import jax
import jax.numpy as jnp
from jax import lax
from jax.sharding import PartitionSpec as P

ITERS = 2


def dipole_block(target_pos, target_ids, source_pos, source_mom, source_ids):
    offset = target_pos[:, :, None] - source_pos[:, None, :]
    radius_sq = jnp.sum(offset * offset, axis=0) + 1.0
    inverse_r = lax.rsqrt(radius_sq)
    inverse_cube = inverse_r * inverse_r * inverse_r
    inverse_fifth = inverse_cube * inverse_r * inverse_r
    keep_mask = target_ids[:, None] != source_ids[None, :]
    projection = jnp.sum(offset * source_mom[:, None, :], axis=0)
    radial_coef = jnp.where(keep_mask, 3.0 * projection * inverse_fifth, 0.0)
    direct_coef = jnp.where(keep_mask, inverse_cube, 0.0)
    return jnp.sum(radial_coef[None] * offset, axis=2) - jnp.sum(
        direct_coef[None] * source_mom[:, None, :], axis=2
    )


def local_field(target_pos, target_ids, source_pos, source_mom, source_ids):
    target_len = target_pos.shape[1]
    source_len = source_pos.shape[1]
    target_block = math.gcd(target_len, 128)
    source_block = math.gcd(source_len, 512)
    target_count = target_len // target_block
    source_count = source_len // source_block
    source_blocks = (
        source_pos.reshape(3, source_count, source_block).transpose(1, 0, 2),
        source_mom.reshape(3, source_count, source_block).transpose(1, 0, 2),
        source_ids.reshape(source_count, source_block),
    )
    target_blocks = (
        target_pos.reshape(3, target_count, target_block).transpose(1, 0, 2),
        target_ids.reshape(target_count, target_block),
    )

    def per_target(target_pair):

        def add_block(field_sum, source_triple):
            return (
                field_sum
                + dipole_block(
                    target_pair[0],
                    target_pair[1],
                    source_triple[0],
                    source_triple[1],
                    source_triple[2],
                ),
                None,
            )

        field_sum, unused = lax.scan(
            add_block, jnp.zeros((3, target_block), jnp.float32), source_blocks
        )
        return field_sum

    result_blocks = lax.map(per_target, target_blocks)
    return result_blocks.transpose(1, 0, 2).reshape(3, target_len)


def pair_force(one_side, other_side):
    separation = one_side[0:3] - other_side[0:3]
    distance = jnp.sqrt(jnp.sum(separation * separation, axis=0) + 1.0)
    normal = separation / distance
    mom_one = one_side[6:9]
    mom_other = other_side[6:9]
    along_one = jnp.sum(mom_one * normal, axis=0)
    along_other = jnp.sum(mom_other * normal, axis=0)
    mom_dot = jnp.sum(mom_one * mom_other, axis=0)
    magnetic = 3.0 * (
        along_one * mom_other
        + along_other * mom_one
        + (mom_dot - 5.0 * along_one * along_other) * normal
    )
    spring = -0.03 * (distance - 1.0) * normal
    rel_speed = jnp.sum((one_side[3:6] - other_side[3:6]) * normal, axis=0)
    damping = -0.5 * rel_speed * normal
    return magnetic + spring + damping


def accumulate(slot_values, slot_ids, particle_count):
    flat_ids = slot_ids.reshape(-1)
    flat_values = slot_values.reshape(3, -1)
    return jnp.zeros((3, particle_count), jnp.float32).at[:, flat_ids].add(flat_values)


def on_device(positions, velocity, applied, suscept, contact_owner, contact_partner, contact_count):
    particle_count = positions.shape[1]
    row_index = lax.axis_index("row")
    own_ids = row_index * particle_count + jnp.arange(particle_count, dtype=jnp.int32)
    moments = suscept[None, :] * applied
    for iteration in range(ITERS):
        shard_pieces = (
            lax.all_gather(positions, "row", axis=1, tiled=True),
            lax.all_gather(moments, "row", axis=1, tiled=True),
        )
        piece_len = shard_pieces[0].shape[1]
        source_ids = jnp.arange(piece_len, dtype=jnp.int32)
        field_sum = local_field(positions, own_ids, shard_pieces[0], shard_pieces[1], source_ids)
        moments = suscept[None, :] * (applied + field_sum)
    col_count = contact_owner.shape[2]
    slot_count = contact_owner.shape[3]
    owner_ids = contact_owner.reshape(col_count, slot_count)
    partner_ids = contact_partner.reshape(col_count, slot_count)
    count_here = contact_count.reshape(col_count)
    live_mask = (jnp.arange(slot_count, dtype=jnp.int32)[None, :] < count_here[:, None]).astype(
        jnp.float32
    )
    state_rows = jnp.concatenate([positions, velocity, moments], axis=0)
    owner_rows = jnp.take(state_rows, owner_ids, axis=1)
    asked_ids = lax.all_to_all(partner_ids, "col", split_axis=0, concat_axis=0, tiled=True)
    looked_up = jnp.take(state_rows, asked_ids, axis=1)
    sent_rows = lax.all_to_all(looked_up, "col", split_axis=1, concat_axis=1, tiled=True)
    partner_rows, asked_ids = (sent_rows, asked_ids[None])
    slot_force = pair_force(owner_rows, partner_rows) * live_mask[None]
    owner_force = accumulate(slot_force, owner_ids, particle_count)
    returned = lax.all_to_all(slot_force, "col", split_axis=1, concat_axis=1, tiled=True)
    forces = owner_force - accumulate(returned, asked_ids[0], particle_count)
    return (moments, forces)


def solution(mesh):
    placed = (
        P(None, ("col", "row")),
        P(None, ("col", "row")),
        P(None, ("col", "row")),
        P(("col", "row")),
        P("col", "row", None, None),
        P("col", "row", None, None),
        P("col", "row", None),
    )
    return jax.shard_map(
        on_device,
        mesh=mesh,
        in_specs=placed,
        out_specs=(P(None, ("col", "row")), P(None, ("col", "row"))),
        check_vma=False,
    )
```

profile of v0, /device:TPU:0, one launch (start us, length us, event | category | flops | bytes accessed | tf_op | source)
XLA Modules:
  0.0 224.5 jit_solution(4701688283679970947)
XLA Ops:
  0.6 1.3 all_to_all.14
  2.0 7.3 %all-to-all-start = ((s32[8,1,512]{2,1,0:T(1,128)}), s32[8,1,512]{2,1,0:T(1,128)S(1)}, u32[]{:S(2)}, u32[]{:S(2)}) async-start(s32[8,1,512]{2,1,0:T(1,128)} %all_to_all.14), calls=%async_computation | async-start | bytes 32768 | tf_op jit(solution)/shard_map/all_to_all | solution.py:117
  12.2 5.2 %all_gather.11 = f32[3,4096]{1,0:T(4,128)S(1)} all-gather(f32[3,1024]{1,0:T(4,128)S(1)} %broadcast_multiply_fusion.1), channel_id=1, replica_groups=mesh['row'=4,'col'=8] {'row'}, dimensions={1}, use_global_device_ids=true | all-gather | bytes 61440 | tf_op jit(solution)/shard_map/all_gather | solution.py:101
  17.4 5.4 %all_gather.10 = f32[3,4096]{1,0:T(4,128)S(1)} all-gather(f32[3,1024]{1,0:T(4,128)} %param.17), channel_id=1, replica_groups=mesh['row'=4,'col'=8] {'row'}, dimensions={1}, use_global_device_ids=true | all-gather | bytes 61440 | tf_op jit(solution)/shard_map/all_gather | solution.py:100
  22.9 55.3 %while.47 = (s32[]{:T(128)}, f32[8,3,128]{2,1,0:T(4,128)S(1)}, f32[8,3,128]{2,1,0:T(4,128)}, s32[8,128]{1,0:T(8,128)S(1)}, f32[8,3,512]{2,1,0:T(4,128)S(1)}, /*i...) while((s32[]{:T(128)}, f32[8,3,128]{2,1,0:T(4,128)S(1)}, ...), condition=%wide.region_7.8_spmd.clone, body=%wide.region_0.7_spmd.clone.sunk | while | flops 2498949 | bytes 2190144 | solution.py:63
  23.6 6.2 %while.50 = (s32[]{:T(128)}, f32[3,128]{1,0:T(4,128)S(1)}, s32[128]{0:T(128)S(1)}, s32[8,512]{1,0:T(8,128)S(1)}, f32[3,128]{1,0:T(4,128)S(1)}, /*index=5*/f32[8,...) while((s32[]{:T(128)}, f32[3,128]{1,0:T(4,128)S(1)}, s32[128]{0:T(128)S(1)}, ...), condition=%wide.region_6.6_spmd.clone, body=%wide.region_1.5_spmd.clone.sunk | while | flops 2490755 | bytes 2165367 | solution.py:58
  30.5 6.2 %while.50 = (s32[]{:T(128)}, f32[3,128]{1,0:T(4,128)S(1)}, s32[128]{0:T(128)S(1)}, s32[8,512]{1,0:T(8,128)S(1)}, f32[3,128]{1,0:T(4,128)S(1)}, /*index=5*/f32[8,...) while((s32[]{:T(128)}, f32[3,128]{1,0:T(4,128)S(1)}, s32[128]{0:T(128)S(1)}, ...), condition=%wide.region_6.6_spmd.clone, body=%wide.region_1.5_spmd.clone.sunk | while | flops 2490755 | bytes 2165367 | solution.py:58
  37.4 6.2 %while.50 = (s32[]{:T(128)}, f32[3,128]{1,0:T(4,128)S(1)}, s32[128]{0:T(128)S(1)}, s32[8,512]{1,0:T(8,128)S(1)}, f32[3,128]{1,0:T(4,128)S(1)}, /*index=5*/f32[8,...) while((s32[]{:T(128)}, f32[3,128]{1,0:T(4,128)S(1)}, s32[128]{0:T(128)S(1)}, ...), condition=%wide.region_6.6_spmd.clone, body=%wide.region_1.5_spmd.clone.sunk | while | flops 2490755 | bytes 2165367 | solution.py:58
  44.3 6.2 %while.50 = (s32[]{:T(128)}, f32[3,128]{1,0:T(4,128)S(1)}, s32[128]{0:T(128)S(1)}, s32[8,512]{1,0:T(8,128)S(1)}, f32[3,128]{1,0:T(4,128)S(1)}, /*index=5*/f32[8,...) while((s32[]{:T(128)}, f32[3,128]{1,0:T(4,128)S(1)}, s32[128]{0:T(128)S(1)}, ...), condition=%wide.region_6.6_spmd.clone, body=%wide.region_1.5_spmd.clone.sunk | while | flops 2490755 | bytes 2165367 | solution.py:58
  51.2 6.2 %while.50 = (s32[]{:T(128)}, f32[3,128]{1,0:T(4,128)S(1)}, s32[128]{0:T(128)S(1)}, s32[8,512]{1,0:T(8,128)S(1)}, f32[3,128]{1,0:T(4,128)S(1)}, /*index=5*/f32[8,...) while((s32[]{:T(128)}, f32[3,128]{1,0:T(4,128)S(1)}, s32[128]{0:T(128)S(1)}, ...), condition=%wide.region_6.6_spmd.clone, body=%wide.region_1.5_spmd.clone.sunk | while | flops 2490755 | bytes 2165367 | solution.py:58
  58.2 6.2 %while.50 = (s32[]{:T(128)}, f32[3,128]{1,0:T(4,128)S(1)}, s32[128]{0:T(128)S(1)}, s32[8,512]{1,0:T(8,128)S(1)}, f32[3,128]{1,0:T(4,128)S(1)}, /*index=5*/f32[8,...) while((s32[]{:T(128)}, f32[3,128]{1,0:T(4,128)S(1)}, s32[128]{0:T(128)S(1)}, ...), condition=%wide.region_6.6_spmd.clone, body=%wide.region_1.5_spmd.clone.sunk | while | flops 2490755 | bytes 2165367 | solution.py:58
  65.1 6.2 %while.50 = (s32[]{:T(128)}, f32[3,128]{1,0:T(4,128)S(1)}, s32[128]{0:T(128)S(1)}, s32[8,512]{1,0:T(8,128)S(1)}, f32[3,128]{1,0:T(4,128)S(1)}, /*index=5*/f32[8,...) while((s32[]{:T(128)}, f32[3,128]{1,0:T(4,128)S(1)}, s32[128]{0:T(128)S(1)}, ...), condition=%wide.region_6.6_spmd.clone, body=%wide.region_1.5_spmd.clone.sunk | while | flops 2490755 | bytes 2165367 | solution.py:58
  72.0 6.2 %while.50 = (s32[]{:T(128)}, f32[3,128]{1,0:T(4,128)S(1)}, s32[128]{0:T(128)S(1)}, s32[8,512]{1,0:T(8,128)S(1)}, f32[3,128]{1,0:T(4,128)S(1)}, /*index=5*/f32[8,...) while((s32[]{:T(128)}, f32[3,128]{1,0:T(4,128)S(1)}, s32[128]{0:T(128)S(1)}, ...), condition=%wide.region_6.6_spmd.clone, body=%wide.region_1.5_spmd.clone.sunk | while | flops 2490755 | bytes 2165367 | solution.py:58
  78.2 5.2 %all_gather.12 = f32[3,4096]{1,0:T(4,128)S(1)} all-gather(f32[3,1024]{1,0:T(4,128)S(1)} %fusion.23), channel_id=1, replica_groups=mesh['row'=4,'col'=8] {'row'}, dimensions={1}, use_global_device_ids=true | all-gather | bytes 61440 | tf_op jit(solution)/shard_map/all_gather | solution.py:101
  83.4 55.3 %while.49 = (s32[]{:T(128)}, f32[8,3,128]{2,1,0:T(4,128)S(1)}, f32[8,3,128]{2,1,0:T(4,128)}, s32[8,128]{1,0:T(8,128)S(1)}, f32[8,3,512]{2,1,0:T(4,128)S(1)}, /*i...) while((s32[]{:T(128)}, f32[8,3,128]{2,1,0:T(4,128)S(1)}, ...), condition=%wide.region_15.16_spmd.clone, body=%wide.region_8.15_spmd.clone.sunk | while | flops 2498949 | bytes 2190144 | solution.py:63
  84.2 6.2 %while.51 = (s32[]{:T(128)}, f32[3,128]{1,0:T(4,128)S(1)}, s32[128]{0:T(128)S(1)}, s32[8,512]{1,0:T(8,128)S(1)}, f32[3,128]{1,0:T(4,128)S(1)}, /*index=5*/f32[8,...) while((s32[]{:T(128)}, f32[3,128]{1,0:T(4,128)S(1)}, s32[128]{0:T(128)S(1)}, ...), condition=%wide.region_14.14_spmd.clone, body=%wide.region_9.13_spmd.clone.sunk | while | flops 2490755 | bytes 2165367 | solution.py:58
  91.1 6.2 %while.51 = (s32[]{:T(128)}, f32[3,128]{1,0:T(4,128)S(1)}, s32[128]{0:T(128)S(1)}, s32[8,512]{1,0:T(8,128)S(1)}, f32[3,128]{1,0:T(4,128)S(1)}, /*index=5*/f32[8,...) while((s32[]{:T(128)}, f32[3,128]{1,0:T(4,128)S(1)}, s32[128]{0:T(128)S(1)}, ...), condition=%wide.region_14.14_spmd.clone, body=%wide.region_9.13_spmd.clone.sunk | while | flops 2490755 | bytes 2165367 | solution.py:58
  98.0 6.2 %while.51 = (s32[]{:T(128)}, f32[3,128]{1,0:T(4,128)S(1)}, s32[128]{0:T(128)S(1)}, s32[8,512]{1,0:T(8,128)S(1)}, f32[3,128]{1,0:T(4,128)S(1)}, /*index=5*/f32[8,...) while((s32[]{:T(128)}, f32[3,128]{1,0:T(4,128)S(1)}, s32[128]{0:T(128)S(1)}, ...), condition=%wide.region_14.14_spmd.clone, body=%wide.region_9.13_spmd.clone.sunk | while | flops 2490755 | bytes 2165367 | solution.py:58
  104.9 6.2 %while.51 = (s32[]{:T(128)}, f32[3,128]{1,0:T(4,128)S(1)}, s32[128]{0:T(128)S(1)}, s32[8,512]{1,0:T(8,128)S(1)}, f32[3,128]{1,0:T(4,128)S(1)}, /*index=5*/f32[8,...) while((s32[]{:T(128)}, f32[3,128]{1,0:T(4,128)S(1)}, s32[128]{0:T(128)S(1)}, ...), condition=%wide.region_14.14_spmd.clone, body=%wide.region_9.13_spmd.clone.sunk | while | flops 2490755 | bytes 2165367 | solution.py:58
  111.8 6.2 %while.51 = (s32[]{:T(128)}, f32[3,128]{1,0:T(4,128)S(1)}, s32[128]{0:T(128)S(1)}, s32[8,512]{1,0:T(8,128)S(1)}, f32[3,128]{1,0:T(4,128)S(1)}, /*index=5*/f32[8,...) while((s32[]{:T(128)}, f32[3,128]{1,0:T(4,128)S(1)}, s32[128]{0:T(128)S(1)}, ...), condition=%wide.region_14.14_spmd.clone, body=%wide.region_9.13_spmd.clone.sunk | while | flops 2490755 | bytes 2165367 | solution.py:58
  118.7 6.2 %while.51 = (s32[]{:T(128)}, f32[3,128]{1,0:T(4,128)S(1)}, s32[128]{0:T(128)S(1)}, s32[8,512]{1,0:T(8,128)S(1)}, f32[3,128]{1,0:T(4,128)S(1)}, /*index=5*/f32[8,...) while((s32[]{:T(128)}, f32[3,128]{1,0:T(4,128)S(1)}, s32[128]{0:T(128)S(1)}, ...), condition=%wide.region_14.14_spmd.clone, body=%wide.region_9.13_spmd.clone.sunk | while | flops 2490755 | bytes 2165367 | solution.py:58
  125.6 6.2 %while.51 = (s32[]{:T(128)}, f32[3,128]{1,0:T(4,128)S(1)}, s32[128]{0:T(128)S(1)}, s32[8,512]{1,0:T(8,128)S(1)}, f32[3,128]{1,0:T(4,128)S(1)}, /*index=5*/f32[8,...) while((s32[]{:T(128)}, f32[3,128]{1,0:T(4,128)S(1)}, s32[128]{0:T(128)S(1)}, ...), condition=%wide.region_14.14_spmd.clone, body=%wide.region_9.13_spmd.clone.sunk | while | flops 2490755 | bytes 2165367 | solution.py:58
  132.5 6.2 %while.51 = (s32[]{:T(128)}, f32[3,128]{1,0:T(4,128)S(1)}, s32[128]{0:T(128)S(1)}, s32[8,512]{1,0:T(8,128)S(1)}, f32[3,128]{1,0:T(4,128)S(1)}, /*index=5*/f32[8,...) while((s32[]{:T(128)}, f32[3,128]{1,0:T(4,128)S(1)}, s32[128]{0:T(128)S(1)}, ...), condition=%wide.region_14.14_spmd.clone, body=%wide.region_9.13_spmd.clone.sunk | while | flops 2490755 | bytes 2165367 | solution.py:58
  138.8 0.7 pad_maximum_fusion
  139.8 10.8 %gather_fusion.1 = f32[4096,9]{1,0:T(8,128)S(1)} fusion(f32[9,1024]{0,1:T(8,128)S(1)} %copy.38, s32[4096]{0:T(1024)S(1)} %broadcast_clamp_fusion), kind=kCustom, calls=%fused_computation.1.clone | custom fusion | bytes 311296 | tf_op jit(solution)/shard_map/jit(_take)/gather | solution.py:118
  152.0 6.0 %all-to-all-start.1 = ((f32[9,8,512]{2,0,1:T(8,128)}), f32[9,8,512]{2,0,1:T(8,128)S(1)}, u32[]{:S(2)}, u32[]{:S(2)}) async-start(f32[9,8,512]{2,0,1:T(8,128)} %select_bitcast_fusion), calls=%async_computation.1 | async-start | bytes 524288 | tf_op jit(solution)/shard_map/all_to_all | solution.py:119
  158.0 10.8 %gather_fusion = f32[4096,9]{1,0:T(8,128)S(1)} fusion(f32[9,1024]{0,1:T(8,128)S(1)} %copy.38, s32[4096]{0:T(1024)S(1)} %broadcast_clamp_fusion.1), kind=kCustom, calls=%fused_computation.clone | custom fusion | bytes 311296 | tf_op jit(solution)/shard_map/jit(_take)/gather | solution.py:116
  170.5 6.0 %all-to-all-start.2 = ((f32[3,8,512]{2,0,1:T(4,128)}), f32[3,8,512]{2,0,1:T(4,128)S(1)}, u32[]{:S(2)}, u32[]{:S(2)}) async-start(f32[3,8,512]{2,0,1:T(4,128)} %add_multiply_fusion), calls=%async_computation.2 | async-start | bytes 131072 | tf_op jit(solution)/shard_map/all_to_all | solution.py:123
  176.5 1.5 copy.42
  178.0 22.5 %scatter_custom_fusion = f32[3,1024]{0,1:T(8,128)S(1)} fusion(s32[4096]{0:T(1024)S(1)} %bitcast.120, f32[4096,3]{1,0:T(8,128)S(1)} %copy.42, f32[]{:T(128)} %constant.65.clone.1), kind=kCustom, calls=%fused_computation.54 | custom fusion | flops 12288 | bytes 12292 | tf_op jit(solution)/shard_map/scatter-add | solution.py:90
  201.2 22.5 %scatter_custom_fusion.1 = f32[3,1024]{0,1:T(8,128)S(1)} fusion(s32[4096]{0:T(1024)S(1)} %bitcast.121, f32[4096,3]{1,0:T(8,128)S(1)} %copy.43, f32[]{:T(128)} %constant.65.clone.1), kind=kCustom, calls=%fused_computation.52 | custom fusion | flops 12288 | bytes 12292 | tf_op jit(solution)/shard_map/scatter-add | solution.py:90
  223.7 0.8 copy.44
  (1019 shorter events, 111.6 us)
Async XLA Ops:
  2.0 137.8 %all-to-all-start = ((s32[8,1,512]{2,1,0:T(1,128)}), s32[8,1,512]{2,1,0:T(1,128)S(1)}, u32[]{:S(2)}, u32[]{:S(2)}) async-start(s32[8,1,512]{2,1,0:T(1,128)} %all_to_all.14), calls=%async_computation | async-start | bytes 32768 | tf_op jit(solution)/shard_map/all_to_all | solution.py:117
  22.9 55.3 %copy-start = (f32[3,1024]{1,0:T(4,128)S(1)}, f32[3,1024]{1,0:T(4,128)}, u32[]{:S(2)}) copy-start(f32[3,1024]{1,0:T(4,128)} %param.19) | copy-start | bytes 36868
  22.9 55.3 %copy-start.2 = (f32[1024]{0:T(1024)S(1)}, f32[1024]{0:T(1024)}, u32[]{:S(2)}) copy-start(f32[1024]{0:T(1024)} %param.20) | copy-start | bytes 12292
  83.4 55.3 %copy-start.3 = (f32[3,1024]{1,0:T(4,128)S(1)}, f32[3,1024]{1,0:T(4,128)}, u32[]{:S(2)}) copy-start(f32[3,1024]{1,0:T(4,128)} %param.18) | copy-start | bytes 36868
  138.8 12.4 %copy-start.1 = (f32[3,1024]{1,0:T(4,128)}, f32[3,1024]{1,0:T(4,128)S(1)}, u32[]{:S(2)}) copy-start(f32[3,1024]{1,0:T(4,128)S(1)} %fusion.22) | copy-start | bytes 36868
  139.8 18.2 %copy-start.4 = (s32[1,1,8]{2,1,0:T(1,128)S(1)}, s32[1,1,8]{2,1,0:T(1,128)}, u32[]{:S(2)}) copy-start(s32[1,1,8]{2,1,0:T(1,128)} %param.23) | copy-start | bytes 100
  152.0 17.5 %all-to-all-start.1 = ((f32[9,8,512]{2,0,1:T(8,128)}), f32[9,8,512]{2,0,1:T(8,128)S(1)}, u32[]{:S(2)}, u32[]{:S(2)}) async-start(f32[9,8,512]{2,0,1:T(8,128)} %select_bitcast_fusion), calls=%async_computation.1 | async-start | bytes 524288 | tf_op jit(solution)/shard_map/all_to_all | solution.py:119
  170.5 30.0 %all-to-all-start.2 = ((f32[3,8,512]{2,0,1:T(4,128)}), f32[3,8,512]{2,0,1:T(4,128)S(1)}, u32[]{:S(2)}, u32[]{:S(2)}) async-start(f32[3,8,512]{2,0,1:T(4,128)} %add_multiply_fusion), calls=%async_computation.2 | async-start | bytes 131072 | tf_op jit(solution)/shard_map/all_to_all | solution.py:123
where the time goes:
time: 226 us; the launch traced here: 225 us
  other arithmetic  140 us (62%)
  local copies, waits for them, and re-layouts  42 us (19%)
  starting transfers between devices  19.2 us (8%)
  blocking collectives  15.9 us (7%)
  loops' own time  5.98 us (3%)
    scatter-add x2, other arithmetic, accumulate(): jnp.zeros((3, particle_count), jnp.float32).at[:, flat_ids].add(flat_values)  45 us
    reduce_sum x128, other arithmetic, dipole_block(): jnp.sum(radial_coef[None] * offset, axis=2)  31.6 us
    reduce_sum x128, other arithmetic, dipole_block(): radius_sq = jnp.sum(offset * offset, axis=0) + 1.0  24.3 us
    reduce_sum x128, other arithmetic, dipole_block(): jnp.sum(direct_coef[None] * source_mom[:, None, :], axis=2)  19.3 us
    select_n x128, other arithmetic, dipole_block(): direct_coef = jnp.where(keep_mask, inverse_cube, 0.0)  13.6 us
    gather x2, local copies, waits for them, and re-layouts, on_device(): looked_up = jnp.take(state_rows, asked_ids, axis=1)  11.4 us
    gather x2, local copies, waits for them, and re-layouts, on_device(): owner_rows = jnp.take(state_rows, owner_ids, axis=1)  11.4 us
    squeeze x32, local copies, waits for them, and re-layouts, local_field(): result_blocks = lax.map(per_target, target_blocks)  11.1 us
  transfers between devices with their start and end apart: 3, of which 0 were waited for; matrix products, arithmetic and copies ran while one was open for 64% of the time, Pallas kernels for 0%

commit v1 on v0

v1 whole, which is shorter than its diff:
```python
import functools
import math

import jax
import jax.numpy as jnp
from jax import lax
from jax.experimental import pallas as pl
from jax.experimental.pallas import tpu as pltpu
from jax.sharding import PartitionSpec as P

ITERS = 2
LANES = 128
SUBS = 8
FEATURES = 16
KEEP_BYTES = 20 * 2**20
F32 = jnp.float32
BF16 = jnp.bfloat16
VMEM = pl.BlockSpec(memory_space=pltpu.VMEM)
SMEM = pl.BlockSpec(memory_space=pltpu.SMEM)


def split3(value):
    high = value.astype(BF16)
    rest = value - high.astype(F32)
    middle = rest.astype(BF16)
    return high, middle, (rest - middle.astype(F32)).astype(BF16)


def norm_sq(pos):
    return pos[0:1] * pos[0:1] + pos[1:2] * pos[1:2] + pos[2:3] * pos[2:3]


def distance_rows(pos):
    high, middle, low = split3(pos)
    norms = split3(norm_sq(pos))
    ones = tuple(jnp.ones_like(n) for n in norms)
    target = jnp.concatenate((high, high, middle, middle, high, low) + norms + ones, axis=0)
    doubled = tuple((-2.0 * p.astype(F32)).astype(BF16) for p in (high, middle, high, middle, low, high))
    source = jnp.concatenate(doubled + ones + norms, axis=0)
    return target, source


def moment_rows(pos, mom):
    outer = [mom[a : a + 1] * pos[b : b + 1] for a in range(3) for b in range(3)]
    along = outer[0] + outer[4] + outer[8]
    square = norm_sq(pos)
    mixed = [3.0 * along * pos[a : a + 1] - square * mom[a : a + 1] for a in range(3)]
    rows = jnp.concatenate([mom] + outer + mixed + [along], axis=0)
    return jnp.concatenate(split3(rows), axis=0)


def field_from_sums(sums, pos, mom):
    total = sums[0:FEATURES] + sums[FEATURES : 2 * FEATURES] + sums[2 * FEATURES : 3 * FEATURES]
    x = [pos[a : a + 1] for a in range(3)]
    m = [total[a : a + 1] for a in range(3)]

    def outer(a, b):
        return total[3 + 3 * a + b : 4 + 3 * a + b]

    trace = outer(0, 0) + outer(1, 1) + outer(2, 2)
    scale_sq = norm_sq(pos) + 1.0
    along = m[0] * x[0] + m[1] * x[1] + m[2] * x[2] - trace
    parts = []
    for a in range(3):
        by_column = outer(0, a) * x[0] + outer(1, a) * x[1] + outer(2, a) * x[2]
        by_row = outer(a, 0) * x[0] + outer(a, 1) * x[1] + outer(a, 2) * x[2]
        parts.append(
            3.0 * (along * x[a] - by_column)
            + 2.0 * by_row
            + total[12 + a : 13 + a]
            - scale_sq * m[a]
            + mom[a : a + 1]
        )
    return jnp.concatenate(parts, axis=0)


def pair_coefficient(radius_sq):
    inverse = lax.rsqrt(radius_sq)
    square = inverse * inverse
    fifth = square * square * inverse
    high = fifth.astype(BF16)
    return high, (fifth - high.astype(F32)).astype(BF16)


def center_of(pos):
    return jnp.sum(pos, axis=1, keepdims=True) * (1.0 / pos.shape[1])


def add_blocks(target_pos, source_pos, source_mom, block, high_ref, low_ref, make):
    if make:
        target_rows, unused = distance_rows(target_pos)
        unused, source_rows = distance_rows(source_pos)
    moments = moment_rows(source_pos, source_mom)
    sums = None
    for start in range(0, source_pos.shape[1], block):
        part = slice(start, start + block)
        if make:
            radius_sq = (
                lax.dot_general(
                    source_rows[:, part],
                    target_rows,
                    (((0,), (0,)), ((), ())),
                    preferred_element_type=F32,
                )
                + 1.0
            )
            high, low = pair_coefficient(radius_sq)
            if high_ref is not None:
                high_ref[part, :] = high
                low_ref[part, :] = low
        else:
            high, low = high_ref[part, :], low_ref[part, :]
        here = jnp.dot(moments[:, part], high, preferred_element_type=F32) + jnp.dot(
            moments[:, part], low, preferred_element_type=F32
        )
        sums = here if sums is None else sums + here
    return sums


def pack_kernel(pos, vel, applied, suscept, owner, partner, count, send, row_send):
    groups = pos.shape[1] // LANES
    slots = owner.shape[1] // LANES
    columns = owner.shape[0]
    row_send[0:3, :] = pos[...]
    row_send[3:6, :] = suscept[...] * applied[...]
    row_send[6:8, :] = jnp.zeros_like(row_send[6:8, :])
    for c in range(3):
        for g in range(groups):
            lanes = slice(g * LANES, (g + 1) * LANES)
            send[0, c * groups + g : c * groups + g + 1, :] = pos[c : c + 1, lanes]
            row = (3 + c) * groups + g
            send[0, row : row + 1, :] = vel[c : c + 1, lanes]
    for e in range(1, columns):
        send[e, 0 : 6 * groups, :] = send[0, 0 : 6 * groups, :]
    for q in range(slots):
        lanes = slice(q * LANES, (q + 1) * LANES)
        send[:, 6 * groups + q, :] = owner[:, lanes].astype(F32)
        send[:, 6 * groups + slots + q, :] = partner[:, lanes].astype(F32)
    tail = 6 * groups + 2 * slots
    for e in range(columns):
        send[e, tail:, :] = jnp.full((send.shape[1] - tail, LANES), count[e].astype(F32))


def first_kernel(block, own, sources, applied, suscept, moments, *kept):
    center = center_of(own[0:3, :])
    target = own[0:3, :] - center
    high_ref, low_ref = kept if kept else (None, None)
    sums = add_blocks(target, sources[0:3, :] - center, sources[3:6, :], block, high_ref, low_ref, True)
    field = field_from_sums(sums, target, own[3:6, :])
    moments[...] = suscept[...] * (applied[...] + field)


def second_kernel(block, own, sources, own_mom, source_mom, applied, suscept, *rest):
    kept, (moments, send) = rest[:-2], rest[-2:]
    center = center_of(own[0:3, :])
    target = own[0:3, :] - center
    high_ref, low_ref = kept if kept else (None, None)
    sums = add_blocks(
        target, sources[0:3, :] - center, source_mom[...], block, high_ref, low_ref, not kept
    )
    result = suscept[...] * (applied[...] + field_from_sums(sums, target, own_mom[...]))
    moments[...] = result
    groups = own.shape[1] // LANES
    for c in range(3):
        for g in range(groups):
            row = c * groups + g
            send[0, row : row + 1, :] = result[c : c + 1, g * LANES : (g + 1) * LANES]
    for e in range(1, send.shape[0]):
        send[e, :, :] = send[0, :, :]


def look_up(tables, index):
    lane = index & (LANES - 1)
    group = index >> (LANES.bit_length() - 1)
    found = None
    for g, table in enumerate(tables):
        here = jnp.take_along_axis(table, lane, axis=1, mode="promise_in_bounds")
        found = here if found is None else jnp.where(group == g, here, found)
    return found


def own_tables(ref, first, groups):
    return [
        jnp.broadcast_to(ref[0, first + g : first + g + 1, :], (SUBS, LANES)) for g in range(groups)
    ]


def their_tables(ref, rows, first, groups):
    return [ref[rows, first + g, :] for g in range(groups)]


def slot_index(sent, received, kind, rows, q, groups, slots):
    owner_row = 6 * groups + q
    partner_row = 6 * groups + slots + q
    ref = received if kind else sent
    owner = ref[rows, owner_row, :].astype(jnp.int32)
    partner = ref[rows, partner_row, :].astype(jnp.int32)
    return (partner, owner) if kind else (owner, partner)


def contact_blocks(columns, slots):
    return [
        (kind, slice(first, first + SUBS), q)
        for kind in range(2)
        for first in range(0, columns, SUBS)
        for q in range(slots)
    ]


def geometry_kernel(slots, sent, received, mom_sent, out):
    columns = sent.shape[0]
    groups = mom_sent.shape[1] // 3
    count_row = 6 * groups + 2 * slots
    for at, (kind, rows, q) in enumerate(contact_blocks(columns, slots)):
        mine, other = slot_index(sent, received, kind, rows, q, groups, slots)
        count = (received if kind else sent)[rows, count_row, :]
        slot = (lax.broadcasted_iota(jnp.int32, (SUBS, LANES), 1) + q * LANES).astype(F32)
        live = slot < count
        gap = []
        for c in range(6):
            gap.append(
                look_up(own_tables(sent, c * groups, groups), mine)
                - look_up(their_tables(received, rows, c * groups, groups), other)
            )
        radius_sq = gap[0] * gap[0] + gap[1] * gap[1] + gap[2] * gap[2] + 1.0
        inverse = lax.rsqrt(radius_sq)
        distance = radius_sq * inverse
        normal = [jnp.where(live, gap[c] * inverse, 0.0) for c in range(3)]
        speed = gap[3] * normal[0] + gap[4] * normal[1] + gap[5] * normal[2]
        for c in range(3):
            out[at, c] = normal[c]
            out[at, 4 + c] = look_up(own_tables(mom_sent, c * groups, groups), mine)
        out[at, 3] = -0.03 * (distance - 1.0) - 0.5 * speed


def force_kernel(slots, geometry, sent, received, mom_received, forces):
    columns = sent.shape[0]
    groups = mom_received.shape[1] // 3
    total = None
    for at, (kind, rows, q) in enumerate(contact_blocks(columns, slots)):
        mine, other = slot_index(sent, received, kind, rows, q, groups, slots)
        normal = [geometry[at, c] for c in range(3)]
        own = [geometry[at, 4 + c] for c in range(3)]
        their = [look_up(their_tables(mom_received, rows, c * groups, groups), other) for c in range(3)]
        along_own = own[0] * normal[0] + own[1] * normal[1] + own[2] * normal[2]
        along_their = their[0] * normal[0] + their[1] * normal[1] + their[2] * normal[2]
        product = own[0] * their[0] + own[1] * their[1] + own[2] * their[2]
        radial = 3.0 * (product - 5.0 * along_own * along_their) + geometry[at, 3]
        force = [
            3.0 * (along_own * their[c] + along_their * own[c]) + radial * normal[c] for c in range(3)
        ]
        group_of = mine >> (LANES.bit_length() - 1)
        lane_of = mine & (LANES - 1)
        for s in range(SUBS):
            place = group_of[s : s + 1, :] == lax.broadcasted_iota(jnp.int32, (groups, LANES), 0)
            rows_f32 = jnp.concatenate(
                [jnp.where(place, force[c][s : s + 1, :], 0.0) for c in range(3)], axis=0
            )
            values = jnp.concatenate(split3(rows_f32), axis=0)
            lane_hot = lane_of[s : s + 1, :] == lax.broadcasted_iota(jnp.int32, (LANES, LANES), 0)
            here = lax.dot_general(
                values,
                jnp.where(lane_hot, 1.0, 0.0).astype(BF16),
                (((1,), (1,)), ((), ())),
                preferred_element_type=F32,
            )
            total = here if total is None else total + here
    height = 3 * groups
    summed = total[0:height] + total[height : 2 * height] + total[2 * height : 3 * height]
    for c in range(3):
        for g in range(groups):
            row = c * groups + g
            forces[c : c + 1, g * LANES : (g + 1) * LANES] = summed[row : row + 1, :]


def call(kernel, name, outs, *args, scalars=(), limit=None):
    specs = [SMEM if at in scalars else VMEM for at in range(len(args))]
    many = isinstance(outs, tuple)
    return pl.pallas_call(
        kernel,
        out_shape=outs,
        in_specs=specs,
        out_specs=tuple(VMEM for _ in outs) if many else VMEM,
        compiler_params=pltpu.CompilerParams(vmem_limit_bytes=limit or 40 * 2**20),
        name=name,
    )(*args)


def shape(*dims, dtype=F32):
    return jax.ShapeDtypeStruct(dims, dtype)


def on_device(positions, velocity, applied, suscept, contact_owner, contact_partner, contact_count):
    count = positions.shape[1]
    columns, slot_len = contact_owner.shape[2:]
    groups, slots = count // LANES, slot_len // LANES
    suscept = suscept.reshape(1, count)
    send_rows = 6 * groups + 2 * slots + 1
    send_rows += -send_rows % SUBS
    sent, row_send = call(
        pack_kernel,
        "pack",
        (shape(columns, send_rows, LANES), shape(8, count)),
        positions,
        velocity,
        applied,
        suscept,
        contact_owner.reshape(columns, slot_len),
        contact_partner.reshape(columns, slot_len),
        contact_count.reshape(columns),
        scalars=(6,),
    )
    received = lax.all_to_all(sent, "col", split_axis=0, concat_axis=0, tiled=True)
    sources = lax.all_gather(row_send, "row", axis=1, tiled=True)
    length = sources.shape[1]
    block = math.gcd(length, 512)
    keep = 4 * length * count <= KEEP_BYTES
    kept_shape = (shape(length, count, dtype=BF16),) * 2 if keep else ()
    moments, *kept = call(
        functools.partial(first_kernel, block),
        "first_field",
        (shape(3, count),) + kept_shape,
        row_send,
        sources,
        applied,
        suscept,
    )
    for iteration in range(1, ITERS):
        source_mom = lax.all_gather(moments, "row", axis=1, tiled=True)
        moments, mom_sent = call(
            functools.partial(second_kernel, block),
            "next_field",
            (shape(3, count), shape(columns, 3 * groups, LANES)),
            row_send,
            sources,
            moments,
            source_mom,
            applied,
            suscept,
            *kept,
        )
    mom_received = lax.all_to_all(mom_sent, "col", split_axis=0, concat_axis=0, tiled=True)
    blocks = len(contact_blocks(columns, slots))
    geometry = call(
        functools.partial(geometry_kernel, slots),
        "contact_geometry",
        shape(blocks, 7, SUBS, LANES),
        sent,
        received,
        mom_sent,
    )
    forces = call(
        functools.partial(force_kernel, slots),
        "contact_force",
        shape(3, count),
        geometry,
        sent,
        received,
        mom_received,
    )
    return (moments, forces)


def solution(mesh):
    placed = (
        P(None, ("col", "row")),
        P(None, ("col", "row")),
        P(None, ("col", "row")),
        P(("col", "row")),
        P("col", "row", None, None),
        P("col", "row", None, None),
        P("col", "row", None),
    )
    return jax.shard_map(
        on_device,
        mesh=mesh,
        in_specs=placed,
        out_specs=(P(None, ("col", "row")), P(None, ("col", "row"))),
        check_vma=False,
    )
```

time: 226 us -> 61.9 us (0.27)
  other arithmetic: 140 us -> 0 us
  local copies, waits for them, and re-layouts: 42 us -> 6.32 us
  Pallas kernels: 0 us -> 25.7 us
  loops' own time: 5.98 us -> 0 us
  starting transfers between devices: 19.2 us -> 13.3 us
  blocking collectives: 15.9 us -> 10.6 us
  waiting for transfers between devices: 0.01 us -> 4.41 us
    reduce_sum x386 -> x0, other arithmetic: 75.4 us -> none  [the longest x128 31.6 us: dipole_block(): jnp.sum(radial_coef[None] * offset, axis=2)]
    scatter-add x2 -> x0, other arithmetic: 45 us -> none  [accumulate(): jnp.zeros((3, particle_count), jnp.float32).at[:, flat_ids].add(flat_values)]
    pallas_call x0 -> x5, Pallas kernels: none -> 25.7 us  [call(): pl.pallas_call(kernel, out_shape=outs, in_specs=specs, out_specs=tuple((V...]
    gather x4 -> x0, local copies, waits for them, and re-layouts: 22.8 us -> none  [the longest x2 11.4 us: on_device(): looked_up = jnp.take(state_rows, asked_ids, axis=1)]
    select_n x132 -> x0, other arithmetic: 14.4 us -> none  [the longest x128 13.6 us: dipole_block(): direct_coef = jnp.where(keep_mask, inverse_cube, 0.0)]
    squeeze x32 -> x0, local copies, waits for them, and re-layouts: 11.1 us -> none  [local_field(): result_blocks = lax.map(per_target, target_blocks)]
    all_to_all x3 -> x2, starting transfers between devices: 19.2 us -> 13.3 us  [the longest x1 7.25 us: on_device(): lax.all_to_all(sent, 'col', split_axis=0, concat_axis=0, tiled=True)]
    another operation x18 -> x0, loops' own time: 5.98 us -> none  [the longest x16 5.48 us: per_target(): lax.scan(add_block, jnp.zeros((3, target_block), jnp.float32), source_blo...]
  transfers between devices with their start and end apart: 3 -> 2, of which waited for: 0 -> 1; matrix products, arithmetic and copies ran while one was open for 64% -> 0% of each run, Pallas kernels for 0% -> 34%
where the time goes in v1:
time: 61.9 us; the launch traced here: 61 us
  Pallas kernels  25.7 us (42%)
  starting transfers between devices  13.3 us (21%)
  blocking collectives  10.6 us (17%)
  local copies, waits for them, and re-layouts  6.32 us (10%)
  waiting for transfers between devices  4.41 us (7%)
  between operations  0.66 us (1%)
    pallas_call x5, Pallas kernels, call(): pl.pallas_call(kernel, out_shape=outs, in_specs=specs, out_specs=tuple((V...  25.7 us
    all_to_all x1, starting transfers between devices, on_device(): lax.all_to_all(sent, 'col', split_axis=0, concat_axis=0, tiled=True)  7.25 us
    unnamed x18, local copies, waits for them, and re-layouts  6.32 us
    all_to_all x1, starting transfers between devices, on_device(): lax.all_to_all(mom_sent, 'col', split_axis=0, concat_axis=0, tiled=True)  6.01 us
    all_gather x1, blocking collectives, on_device(): sources = lax.all_gather(row_send, 'row', axis=1, tiled=True)  5.41 us
    all_gather x1, blocking collectives, on_device(): source_mom = lax.all_gather(moments, 'row', axis=1, tiled=True)  5.23 us
    all_to_all x1, waiting for transfers between devices, on_device(): lax.all_to_all(mom_sent, 'col', split_axis=0, concat_axis=0, tiled=True)  4.41 us
  transfers between devices with their start and end apart: 2, of which 1 were waited for; matrix products, arithmetic and copies ran while one was open for 0% of the time, Pallas kernels for 34%

profile of v1, /device:TPU:0, one launch (start us, length us, event | category | flops | bytes accessed | tf_op | source)
XLA Modules:
  0.0 61.0 jit_solution(2432952153844732712)
XLA Ops:
  0.6 0.0 copy-start
  0.6 0.7 %copy-done = f32[3,1024]{1,0:T(4,128)S(1)} copy-done((f32[3,1024]{1,0:T(4,128)S(1)}, f32[3,1024]{1,0:T(4,128)}, u32[]{:S(2)}) %copy-start) | copy-done | bytes 12312
  1.4 0.0 copy-start.2
  1.4 0.7 %copy-done.2 = f32[1024]{0:T(1024)S(1)} copy-done((f32[1024]{0:T(1024)S(1)}, f32[1024]{0:T(1024)}, u32[]{:S(2)}) %copy-start.2) | copy-done | bytes 4120
  2.0 0.0 copy-start.4
  2.0 0.7 %copy-done.4 = f32[3,1024]{1,0:T(4,128)S(1)} copy-done((f32[3,1024]{1,0:T(4,128)S(1)}, f32[3,1024]{1,0:T(4,128)}, u32[]{:S(2)}) %copy-start.4) | copy-done | bytes 12312
  2.8 0.0 copy-start.5
  2.8 0.7 %copy-done.5 = f32[3,1024]{1,0:T(4,128)S(1)} copy-done((f32[3,1024]{1,0:T(4,128)S(1)}, f32[3,1024]{1,0:T(4,128)}, u32[]{:S(2)}) %copy-start.5) | copy-done | bytes 12312
  3.5 0.0 copy-start.6
  3.5 0.7 %copy-done.6 = s32[1,1,8,512]{3,2,1,0:T(8,128)S(1)} copy-done((s32[1,1,8,512]{3,2,1,0:T(8,128)S(1)}, s32[1,1,8,512]{3,2,1,0:T(8,128)}, u32[]{:S(2)}) %copy-start.6) | copy-done | bytes 16408
  4.2 0.0 copy-start.7
  4.2 0.7 %copy-done.7 = s32[1,1,8,512]{3,2,1,0:T(8,128)S(1)} copy-done((s32[1,1,8,512]{3,2,1,0:T(8,128)S(1)}, s32[1,1,8,512]{3,2,1,0:T(8,128)}, u32[]{:S(2)}) %copy-start.7) | copy-done | bytes 16408
  4.9 0.0 copy-start.8
  4.9 0.7 %copy-done.8 = s32[1,1,8]{2,1,0:T(1,128)S(1)} copy-done((s32[1,1,8]{2,1,0:T(1,128)S(1)}, s32[1,1,8]{2,1,0:T(1,128)}, u32[]{:S(2)}) %copy-start.8) | copy-done | bytes 56
  5.6 1.3 %pack.1 = (f32[8,64,128]{2,1,0:T(8,128)}, f32[8,1024]{1,0:T(8,128)S(1)}) custom-call(f32[3,1024]{1,0:T(4,128)S(1)} %copy-done.4, f32[3,1024]{1,0:T(4,128)S(1)} %copy-done.5, f32[3,1024]{1,0:T(4,128)S(1)} %copy-done, f32[1,1024]{1,0:T(1,128)S(1)} %bitcast.4, s32[8,512]{1,0:T(8,128)S(1)} %bitcast.7, s32[8,512]{1,0:T(8,128)S(1)} %bitcast.8, s32[8]{0:T(128)S(1)} %bitcast.9), custom_call_target="tpu_custom_call" | custom-call | tf_op jit(solution)/shard_map/pack/pallas_call | solution.py:279
  6.9 7.3 %all-to-all-start = ((f32[8,64,128]{2,1,0:T(8,128)}), f32[8,64,128]{2,1,0:T(8,128)S(1)}, u32[]{:S(2)}, u32[]{:S(2)}) async-start(f32[8,64,128]{2,1,0:T(8,128)} %get-tuple-element.14.sent), calls=%async_computation | async-start | bytes 524288 | tf_op jit(solution)/shard_map/all_to_all | solution.py:313
  14.1 5.4 %all_gather.6.sources = f32[8,4096]{1,0:T(8,128)S(1)} all-gather(f32[8,1024]{1,0:T(8,128)S(1)} %get-tuple-element.9.own), channel_id=1, replica_groups=mesh['row'=4,'col'=8] {'row'}, dimensions={1}, use_global_device_ids=true | all-gather | bytes 163840 | tf_op jit(solution)/shard_map/all_gather | solution.py:314
  19.5 0.0 copy-start.1
  19.5 0.7 %copy-done.1 = f32[3,1024]{1,0:T(4,128)S(1)} copy-done((f32[3,1024]{1,0:T(4,128)S(1)}, f32[3,1024]{1,0:T(4,128)}, u32[]{:S(2)}) %copy-start.1) | copy-done | bytes 12312
  20.2 0.0 copy-start.3
  20.3 0.7 %copy-done.3 = f32[1024]{0:T(1024)S(1)} copy-done((f32[1024]{0:T(1024)S(1)}, f32[1024]{0:T(1024)}, u32[]{:S(2)}) %copy-start.3) | copy-done | bytes 4120
  20.9 11.4 %first_field.1 = (f32[3,1024]{1,0:T(4,128)S(1)}, bf16[4096,1024]{1,0:T(8,128)(2,1)S(1)}, bf16[4096,1024]{1,0:T(8,128)(2,1)}) custom-call(f32[8,1024]{1,0:T(8,128)S(1)} %get-tuple-element.9.own, f32[8,4096]{1,0:T(8,128)S(1)} %all_gather.6.sources, f32[3,1024]{1,0:T(4,128)S(1)} %copy-done.1, f32[1,1024]{1,0:T(1,128)S(1)} %bitcast.5), custom_call_target="tpu_custom_call" | custom-call | tf_op jit(solution)/shard_map/first_field/pallas_call | solution.py:279
  32.4 5.2 %all_gather.7.source_mom = f32[3,4096]{1,0:T(4,128)S(1)} all-gather(f32[3,1024]{1,0:T(4,128)S(1)} %get-tuple-element.10.own_mom), channel_id=1, replica_groups=mesh['row'=4,'col'=8] {'row'}, dimensions={1}, use_global_device_ids=true | all-gather | bytes 61440 | tf_op jit(solution)/shard_map/all_gather | solution.py:329
  37.6 6.9 %next_field.1 = (f32[3,1024]{1,0:T(4,128)}, f32[8,24,128]{2,1,0:T(8,128)}) custom-call(f32[8,1024]{1,0:T(8,128)S(1)} %get-tuple-element.9.own, f32[8,4096]{1,0:T(8,128)S(1)} %all_gather.6.sources, f32[3,1024]{1,0:T(4,128)S(1)} %get-tuple-element.10.own_mom, f32[3,4096]{1,0:T(4,128)S(1)} %all_gather.7.source_mom, f32[3,1024]{1,0:T(4,128)S(1)} %copy-done.1, ...), custom_call_target="tpu_custom_call" | custom-call | tf_op jit(solution)/shard_map/next_field/pallas_call | solution.py:279
  44.5 0.0 all-to-all-done.received
  44.5 6.0 %all-to-all-start.1 = ((f32[8,24,128]{2,1,0:T(8,128)}), f32[8,24,128]{2,1,0:T(8,128)S(1)}, u32[]{:S(2)}, u32[]{:S(2)}) async-start(f32[8,24,128]{2,1,0:T(8,128)} %get-tuple-element.15.mom_sent), calls=%async_computation.1 | async-start | bytes 196608 | tf_op jit(solution)/shard_map/all_to_all | solution.py:342
  50.5 2.7 %contact_geometry.1.geometry = f32[8,7,8,128]{3,2,1,0:T(8,128)S(1)} custom-call(f32[8,64,128]{2,1,0:T(8,128)} %get-tuple-element.14.sent, f32[8,64,128]{2,1,0:T(8,128)S(1)} %all-to-all-done.received, f32[8,24,128]{2,1,0:T(8,128)} %get-tuple-element.15.mom_sent), custom_call_target="tpu_custom_call" | custom-call | tf_op jit(solution)/shard_map/contact_geometry/pallas_call | solution.py:279
  53.2 4.4 %all-to-all-done.1.mom_received = f32[8,24,128]{2,1,0:T(8,128)S(1)} async-done(((f32[8,24,128]{2,1,0:T(8,128)}), f32[8,24,128]{2,1,0:T(8,128)S(1)}, u32[]{:S(2)}, u32[]{:S(2)}) %all-to-all-start.1) | async-done | bytes 98336 | tf_op jit(solution)/shard_map/all_to_all | solution.py:342
  57.6 3.3 %contact_force.1 = f32[3,1024]{1,0:T(4,128)} custom-call(f32[8,7,8,128]{3,2,1,0:T(8,128)S(1)} %contact_geometry.1.geometry, f32[8,64,128]{2,1,0:T(8,128)} %get-tuple-element.14.sent, f32[8,64,128]{2,1,0:T(8,128)S(1)} %all-to-all-done.received, f32[8,24,128]{2,1,0:T(8,128)S(1)} %all-to-all-done.1.mom_received), custom_call_target="tpu_custom_call" | custom-call | tf_op jit(solution)/shard_map/contact_force/pallas_call | solution.py:279
Async XLA Ops:
  0.6 0.7 %copy-start = (f32[3,1024]{1,0:T(4,128)S(1)}, f32[3,1024]{1,0:T(4,128)}, u32[]{:S(2)}) copy-start(f32[3,1024]{1,0:T(4,128)} %applied.5) | copy-start | bytes 36868
  1.4 0.7 %copy-start.2 = (f32[1024]{0:T(1024)S(1)}, f32[1024]{0:T(1024)}, u32[]{:S(2)}) copy-start(f32[1024]{0:T(1024)} %param.10) | copy-start | bytes 12292
  2.0 0.7 %copy-start.4 = (f32[3,1024]{1,0:T(4,128)S(1)}, f32[3,1024]{1,0:T(4,128)}, u32[]{:S(2)}) copy-start(f32[3,1024]{1,0:T(4,128)} %pos.1) | copy-start | bytes 36868
  2.8 0.7 %copy-start.5 = (f32[3,1024]{1,0:T(4,128)S(1)}, f32[3,1024]{1,0:T(4,128)}, u32[]{:S(2)}) copy-start(f32[3,1024]{1,0:T(4,128)} %vel.1) | copy-start | bytes 36868
  3.5 0.7 %copy-start.6 = (s32[1,1,8,512]{3,2,1,0:T(8,128)S(1)}, s32[1,1,8,512]{3,2,1,0:T(8,128)}, u32[]{:S(2)}) copy-start(s32[1,1,8,512]{3,2,1,0:T(8,128)} %param.11) | copy-start | bytes 49156
  4.2 0.7 %copy-start.7 = (s32[1,1,8,512]{3,2,1,0:T(8,128)S(1)}, s32[1,1,8,512]{3,2,1,0:T(8,128)}, u32[]{:S(2)}) copy-start(s32[1,1,8,512]{3,2,1,0:T(8,128)} %param.12) | copy-start | bytes 49156
  4.9 0.7 %copy-start.8 = (s32[1,1,8]{2,1,0:T(1,128)S(1)}, s32[1,1,8]{2,1,0:T(1,128)}, u32[]{:S(2)}) copy-start(s32[1,1,8]{2,1,0:T(1,128)} %param.13) | copy-start | bytes 100
  6.9 37.6 %all-to-all-start = ((f32[8,64,128]{2,1,0:T(8,128)}), f32[8,64,128]{2,1,0:T(8,128)S(1)}, u32[]{:S(2)}, u32[]{:S(2)}) async-start(f32[8,64,128]{2,1,0:T(8,128)} %get-tuple-element.14.sent), calls=%async_computation | async-start | bytes 524288 | tf_op jit(solution)/shard_map/all_to_all | solution.py:313
  19.5 0.7 %copy-start.1 = (f32[3,1024]{1,0:T(4,128)S(1)}, f32[3,1024]{1,0:T(4,128)}, u32[]{:S(2)}) copy-start(f32[3,1024]{1,0:T(4,128)} %applied.5) | copy-start | bytes 36868
  20.2 0.7 %copy-start.3 = (f32[1024]{0:T(1024)S(1)}, f32[1024]{0:T(1024)}, u32[]{:S(2)}) copy-start(f32[1024]{0:T(1024)} %param.10) | copy-start | bytes 12292
  44.5 13.1 %all-to-all-start.1 = ((f32[8,24,128]{2,1,0:T(8,128)}), f32[8,24,128]{2,1,0:T(8,128)S(1)}, u32[]{:S(2)}, u32[]{:S(2)}) async-start(f32[8,24,128]{2,1,0:T(8,128)} %get-tuple-element.15.mom_sent), calls=%async_computation.1 | async-start | bytes 196608 | tf_op jit(solution)/shard_map/all_to_all | solution.py:342

commit v2 on v1

v2 whole, which is shorter than its diff:
```python
import functools
import math

import jax
import jax.numpy as jnp
from jax import lax
from jax.experimental import pallas as pl
from jax.experimental.pallas import tpu as pltpu
from jax.sharding import PartitionSpec as P

ITERS = 2
LANES = 128
SUBS = 8
FEATURES = 16
PAIR_ROWS = 24
KEEP_BYTES = 20 * 2**20
BLOCK = 512
F32 = jnp.float32
BF16 = jnp.bfloat16
VMEM = pl.BlockSpec(memory_space=pltpu.VMEM)
HBM = pl.BlockSpec(memory_space=pltpu.HBM)


def split3(value):
    high = value.astype(BF16).astype(F32)
    rest = value - high
    middle = rest.astype(BF16).astype(F32)
    return high, middle, rest - middle


def norm_sq(pos):
    return pos[0] * pos[0] + pos[1] * pos[1] + pos[2] * pos[2]


def to_rows(vectors, held, out, first, columns):
    groups = held.shape[1]
    for f, vector in enumerate(vectors):
        held[f] = vector
    for g in range(groups):
        lanes = slice(columns + g * LANES, columns + (g + 1) * LANES)
        out[first : first + len(vectors), lanes] = held[0 : len(vectors), g, :].astype(BF16)


def moment_rows(pos, mom, held, out, columns):
    outer = [mom[a] * pos[b] for a in range(3) for b in range(3)]
    along = outer[0] + outer[4] + outer[8]
    square = norm_sq(pos)
    mixed = [3.0 * along * pos[a] - square * mom[a] for a in range(3)]
    pieces = [split3(v) for v in list(mom) + outer + mixed + [along]]
    for k in range(3):
        to_rows([p[k] for p in pieces], held, out, k * FEATURES, columns)


def target_rows(pos, held, out):
    high, middle, low = zip(*(split3(p) for p in pos))
    norms = split3(norm_sq(pos) + 1.0)
    ones = (jnp.ones_like(pos[0]),) * 3
    to_rows(high + high + middle + middle + high + low + norms + ones, held, out, 0, 0)


def source_rows(pos, held, out, columns):
    high, middle, low = zip(*(split3(p) for p in pos))
    norms = split3(norm_sq(pos))
    ones = (jnp.ones_like(pos[0]),) * 3
    doubled = tuple(-2.0 * p for p in high + middle + high + middle + low + high)
    to_rows(doubled + ones + norms, held, out, 3 * FEATURES, columns)


def field_from_sums(sums, held, pos, mom):
    groups = held.shape[1]
    for g in range(groups):
        lanes = slice(g * LANES, (g + 1) * LANES)
        held[0:FEATURES, g, :] = (
            sums[0:FEATURES, lanes]
            + sums[FEATURES : 2 * FEATURES, lanes]
            + sums[2 * FEATURES : 3 * FEATURES, lanes]
        )
    m = [held[a] for a in range(3)]
    outer = [[held[3 + 3 * a + b] for b in range(3)] for a in range(3)]
    trace = outer[0][0] + outer[1][1] + outer[2][2]
    scale_sq = norm_sq(pos) + 1.0
    along = m[0] * pos[0] + m[1] * pos[1] + m[2] * pos[2] - trace
    parts = []
    for a in range(3):
        by_column = outer[0][a] * pos[0] + outer[1][a] * pos[1] + outer[2][a] * pos[2]
        by_row = outer[a][0] * pos[0] + outer[a][1] * pos[1] + outer[a][2] * pos[2]
        parts.append(
            3.0 * (along * pos[a] - by_column)
            + 2.0 * by_row
            + held[12 + a]
            - scale_sq * m[a]
            + mom[a]
        )
    return parts


def pair_coefficient(radius_sq):
    inverse = lax.rsqrt(radius_sq)
    square = inverse * inverse
    fifth = square * square * inverse
    high = fifth.astype(BF16)
    return high, (fifth - high.astype(F32)).astype(BF16)


def vectors_of(ref, first, groups):
    return [ref[first + c * groups : first + (c + 1) * groups, :] for c in range(3)]


def about(pos, center):
    return [p - c for p, c in zip(pos, center)]


def field_kernel(has_mom, has_kept, has_before, is_last, columns, *refs):
    refs = list(refs)
    own, source = refs.pop(0), refs.pop(0)
    own_mom, source_mom = (refs.pop(0), refs.pop(0)) if has_mom else (None, None)
    kept = (refs.pop(0), refs.pop(0)) if has_kept else None
    before = refs.pop(0) if has_before else None
    outs, (held, target, feats, sums) = refs[:-4], refs[-4:]
    made = outs[1:] if len(outs) == 3 else None
    blocks = source.shape[0]
    groups = held.shape[1]
    count = groups * LANES
    own_pos = vectors_of(own, 0, groups)
    center = [jnp.sum(p, keepdims=True) * (1.0 / count) for p in own_pos]
    pos = about(own_pos, center)
    if not has_kept:
        target_rows(pos, held, target)
    sums[...] = before[...] if has_before else jnp.zeros_like(sums)
    for k in range(blocks):
        there = source.at[k]
        their_pos = about(vectors_of(there, 0, groups), center)
        if has_mom:
            their_mom = vectors_of(source_mom.at[k], 0, groups)
        else:
            chi = there[6 * groups : 7 * groups, :]
            their_mom = [chi * v for v in vectors_of(there, 3 * groups, groups)]
        moment_rows(their_pos, their_mom, held, feats, k * count)
        if not has_kept:
            source_rows(their_pos, held, feats, k * count)
    block = math.gcd(count, BLOCK)
    for start in range(0, blocks * count, block):
        part = slice(start, start + block)
        if has_kept:
            high, low = kept[0][part, :], kept[1][part, :]
        else:
            radius_sq = lax.dot_general(
                feats[3 * FEATURES :, part],
                target[...],
                (((0,), (0,)), ((), ())),
                preferred_element_type=F32,
            )
            high, low = pair_coefficient(radius_sq)
            if made:
                made[0][part, :] = high
                made[1][part, :] = low
        moments = feats[0 : 3 * FEATURES, part]
        sums[...] += jnp.dot(moments, high, preferred_element_type=F32) + jnp.dot(
            moments, low, preferred_element_type=F32
        )
    if not is_last:
        outs[0][...] = sums[...]
        return
    applied = vectors_of(own, 3 * groups, groups)
    chi = own[6 * groups : 7 * groups, :]
    own_now = vectors_of(own_mom, 0, groups) if has_mom else [chi * v for v in applied]
    field = field_from_sums(sums, held, pos, own_now)
    result = [chi * (applied[a] + field[a]) for a in range(3)]
    if not columns:
        for a in range(3):
            outs[0][a * groups : (a + 1) * groups, :] = result[a]
        return
    for a in range(3):
        for e in range(columns):
            outs[1][e, a * groups : (a + 1) * groups, :] = result[a]
        for g in range(groups):
            outs[0][a : a + 1, g * LANES : (g + 1) * LANES] = result[a][g : g + 1, :]


def pack_kernel(*refs):
    inputs, (send, payload), (pos, vel, field, chi, owner, partner, counts, done) = (
        refs[0:7],
        refs[7:9],
        refs[9:],
    )
    held = (pos, vel, field, chi, owner, partner, counts)
    copies = [
        pltpu.make_async_copy(src, dst, done.at[k]) for k, (src, dst) in enumerate(zip(inputs, held))
    ]
    for copy in copies:
        copy.start()
    for copy in copies:
        copy.wait()
    groups = pos.shape[1] // LANES
    slots = owner.shape[1] // LANES
    columns = owner.shape[0]
    for g in range(groups):
        lanes = slice(g * LANES, (g + 1) * LANES)
        for c in range(3):
            row = slice(c * groups + g, c * groups + g + 1)
            payload[row, :] = pos[c : c + 1, lanes]
            row = slice((3 + c) * groups + g, (3 + c) * groups + g + 1)
            payload[row, :] = field[c : c + 1, lanes]
            send[0, row, :] = vel[c : c + 1, lanes]
        payload[6 * groups + g : 6 * groups + g + 1, :] = chi[:, lanes]
    send[0, 0 : 3 * groups, :] = payload[0 : 3 * groups, :]
    for e in range(1, columns):
        send[e, 0 : 6 * groups, :] = send[0, 0 : 6 * groups, :]
    for q in range(slots):
        lanes = slice(q * LANES, (q + 1) * LANES)
        send[:, 6 * groups + q, :] = owner[:, lanes].astype(F32)
        send[:, 6 * groups + slots + q, :] = partner[:, lanes].astype(F32)
    tail = 6 * groups + 2 * slots
    for e in range(columns):
        send[e, tail:, :] = jnp.full((send.shape[1] - tail, LANES), counts[0, e].astype(F32))


def split_index(index):
    return index & (LANES - 1), index >> (LANES.bit_length() - 1)


def look_up(tables, lane, bits):
    found = [jnp.take_along_axis(t, lane, axis=1, mode="promise_in_bounds") for t in tables]
    for bit in bits:
        found = [
            jnp.where(bit, found[k + 1], found[k]) if k + 1 < len(found) else found[k]
            for k in range(0, len(found), 2)
        ]
    return found[0]


def bits_of(group, groups):
    return [(group >> k) & 1 == 1 for k in range((groups - 1).bit_length())]


def own_tables(ref, first, groups):
    return [
        jnp.broadcast_to(ref[first + g : first + g + 1, :], (SUBS, LANES)) for g in range(groups)
    ]


def their_tables(ref, rows, first, groups):
    return [ref[rows, first + g, :] for g in range(groups)]


def slot_index(sent, received, kind, rows, q, groups, slots):
    ref = received if kind else sent
    owner = ref[rows, 6 * groups + q, :].astype(jnp.int32)
    partner = ref[rows, 6 * groups + slots + q, :].astype(jnp.int32)
    return (partner, owner) if kind else (owner, partner)


def contact_blocks(columns, slots):
    return [
        (kind, slice(first, first + SUBS), q)
        for kind in range(2)
        for first in range(0, columns, SUBS)
        for q in range(slots)
    ]


def geometry_kernel(slots, groups, sent, received, out):
    columns = sent.shape[0]
    count_row = 6 * groups + 2 * slots
    for at, (kind, rows, q) in enumerate(contact_blocks(columns, slots)):
        mine, other = slot_index(sent, received, kind, rows, q, groups, slots)
        count = (received if kind else sent)[rows, count_row, :]
        slot = (lax.broadcasted_iota(jnp.int32, (SUBS, LANES), 1) + q * LANES).astype(F32)
        live = slot < count
        lane, group = split_index(mine)
        bits = bits_of(group, groups)
        their_lane, their_group = split_index(other)
        their_bits = bits_of(their_group, groups)
        gap = []
        for c in range(6):
            gap.append(
                look_up(own_tables(sent.at[0], c * groups, groups), lane, bits)
                - look_up(
                    their_tables(received, rows, c * groups, groups), their_lane, their_bits
                )
            )
        radius_sq = gap[0] * gap[0] + gap[1] * gap[1] + gap[2] * gap[2] + 1.0
        inverse = lax.rsqrt(radius_sq)
        normal = [jnp.where(live, gap[c] * inverse, 0.0) for c in range(3)]
        speed = gap[3] * normal[0] + gap[4] * normal[1] + gap[5] * normal[2]
        for c in range(3):
            out[at, c] = normal[c]
        out[at, 3] = -0.03 * (radius_sq * inverse - 1.0) - 0.5 * speed


def force_kernel(slots, geometry, sent, received, mom_sent, mom_received, forces, places, pieces):
    columns = sent.shape[0]
    groups = mom_received.shape[1] // 3
    for at, (kind, rows, q) in enumerate(contact_blocks(columns, slots)):
        mine, other = slot_index(sent, received, kind, rows, q, groups, slots)
        lane, group = split_index(mine)
        bits = bits_of(group, groups)
        their_lane, their_group = split_index(other)
        their_bits = bits_of(their_group, groups)
        normal = [geometry[at, c] for c in range(3)]
        own = [look_up(own_tables(mom_sent.at[0], c * groups, groups), lane, bits) for c in range(3)]
        their = [
            look_up(their_tables(mom_received, rows, c * groups, groups), their_lane, their_bits)
            for c in range(3)
        ]
        along_own = own[0] * normal[0] + own[1] * normal[1] + own[2] * normal[2]
        along_their = their[0] * normal[0] + their[1] * normal[1] + their[2] * normal[2]
        product = own[0] * their[0] + own[1] * their[1] + own[2] * their[2]
        radial = 3.0 * (product - 5.0 * along_own * along_their) + geometry[at, 3]
        lanes = slice(q * LANES, (q + 1) * LANES)
        places[kind, 0, rows, lanes] = group
        places[kind, 1, rows, lanes] = lane
        for c in range(3):
            force = 3.0 * (along_own * their[c] + along_their * own[c]) + radial * normal[c]
            for k, piece in enumerate(split3(force)):
                pieces[kind, k * 3 + c, rows, lanes] = piece
    width = slots * LANES
    row_of = lax.broadcasted_iota(jnp.int32, (groups, width), 0)
    lane_of = lax.broadcasted_iota(jnp.int32, (LANES, width), 0)
    total = None
    for kind in range(2):
        for e in range(columns):
            here = places[kind, 0, e : e + 1, :] == row_of
            values = jnp.concatenate(
                [jnp.where(here, pieces[kind, k, e : e + 1, :], 0.0) for k in range(9)], axis=0
            ).astype(BF16)
            hot = jnp.where(places[kind, 1, e : e + 1, :] == lane_of, 1.0, 0.0).astype(BF16)
            summed = lax.dot_general(
                values, hot, (((1,), (1,)), ((), ())), preferred_element_type=F32
            )
            total = summed if total is None else total + summed
    height = 3 * groups
    total = total[0:height] + total[height : 2 * height] + total[2 * height : 3 * height]
    for c in range(3):
        for g in range(groups):
            row = c * groups + g
            forces[c : c + 1, g * LANES : (g + 1) * LANES] = total[row : row + 1, :]


def call(kernel, name, outs, *args, specs=None, scratch=(), limit=24):
    many = isinstance(outs, tuple)
    return pl.pallas_call(
        kernel,
        out_shape=outs,
        in_specs=specs or [VMEM] * len(args),
        out_specs=tuple(VMEM for _ in outs) if many else VMEM,
        scratch_shapes=scratch,
        compiler_params=pltpu.CompilerParams(vmem_limit_bytes=limit * 2**20),
        name=name,
    )(*args)


def shape(*dims, dtype=F32):
    return jax.ShapeDtypeStruct(dims, dtype)


def exchange(block, axis, size):
    if size & (size - 1):
        every = lambda k: lax.ppermute(block, axis, [(i, (i + k) % size) for i in range(size)])
        return [every(k)[None] for k in range(1, size)]
    held, rounds = block[None], []
    for k in range(size.bit_length() - 1):
        arrived = lax.ppermute(held, axis, [(i, i ^ (1 << k)) for i in range(size)])
        rounds.append(arrived)
        if k + 2 < size.bit_length():
            held = jnp.concatenate([held, arrived], axis=0)
    return rounds


def add_fields(payload, payloads, mom, moms, kept, columns, keep):
    count = payload.shape[0] // SUBS * LANES
    groups = count // LANES
    sums, made = None, []
    for k, source in enumerate(payloads):
        is_last = k == len(payloads) - 1
        length = source.shape[0] * count
        args = [payload, source]
        if mom is not None:
            args += [mom, moms[k]]
        if kept:
            args += kept[k]
        if sums is not None:
            args.append(sums)
        if not is_last:
            outs = (shape(3 * FEATURES, count),)
        elif columns:
            outs = (shape(3, count), shape(columns, 3 * groups, LANES))
        else:
            outs = (shape(3 * groups, LANES),)
        if keep:
            outs += (shape(length, count, dtype=BF16),) * 2
        results = call(
            functools.partial(
                field_kernel, mom is not None, bool(kept), sums is not None, is_last, columns
            ),
            "field_sums",
            outs,
            *args,
            scratch=[
                pltpu.VMEM((PAIR_ROWS, groups, LANES), F32),
                pltpu.VMEM((PAIR_ROWS, count), BF16),
                pltpu.VMEM((3 * FEATURES + PAIR_ROWS, length), BF16),
                pltpu.VMEM((3 * FEATURES, count), F32),
            ],
        )
        sums = results[0]
        if keep:
            made.append(results[1:])
    return results, made


def on_device(row_size, positions, velocity, applied, suscept, owner, partner, contact_count):
    count = positions.shape[1]
    columns, slot_len = owner.shape[2:]
    groups, slots = count // LANES, slot_len // LANES
    send_rows = 6 * groups + 2 * slots + 1
    send_rows += -send_rows % SUBS
    inputs = (
        positions,
        velocity,
        applied,
        suscept.reshape(1, count),
        owner.reshape(columns, slot_len),
        partner.reshape(columns, slot_len),
        contact_count.reshape(1, columns),
    )
    sent, payload = call(
        pack_kernel,
        "pack",
        (shape(columns, send_rows, LANES), shape(8 * groups, LANES)),
        *(pltpu.with_memory_space_constraint(v, pltpu.HBM) for v in inputs),
        specs=[HBM] * 7,
        scratch=[pltpu.VMEM(v.shape, v.dtype) for v in inputs[:-1]]
        + [pltpu.SMEM((1, columns), jnp.int32), pltpu.SemaphoreType.DMA((7,))],
    )
    payloads = [payload[None]] + exchange(payload, "row", row_size)
    received = lax.all_to_all(sent, "col", split_axis=0, concat_axis=0, tiled=True)
    keep = 4 * row_size * count * count <= KEEP_BYTES
    (mom, *unused), kept = add_fields(payload, payloads, None, None, None, 0, keep)
    geometry = call(
        functools.partial(geometry_kernel, slots, groups),
        "contact_geometry",
        shape(len(contact_blocks(columns, slots)), 4, SUBS, LANES),
        sent,
        received,
    )
    for iteration in range(1, ITERS):
        is_last = iteration == ITERS - 1
        moms = [mom[None]] + exchange(mom, "row", row_size)
        results, unused = add_fields(
            payload, payloads, mom, moms, kept, columns if is_last else 0, False
        )
        mom = results[0]
    moments, mom_sent = results
    mom_received = lax.all_to_all(mom_sent, "col", split_axis=0, concat_axis=0, tiled=True)
    forces = call(
        functools.partial(force_kernel, slots),
        "contact_force",
        shape(3, count),
        geometry,
        sent,
        received,
        mom_sent,
        mom_received,
        scratch=[
            pltpu.VMEM((2, 2, columns, slot_len), jnp.int32),
            pltpu.VMEM((2, 9, columns, slot_len), F32),
        ],
    )
    return (moments, forces)


def solution(mesh):
    placed = (
        P(None, ("col", "row")),
        P(None, ("col", "row")),
        P(None, ("col", "row")),
        P(("col", "row")),
        P("col", "row", None, None),
        P("col", "row", None, None),
        P("col", "row", None),
    )
    return jax.shard_map(
        functools.partial(on_device, mesh.shape["row"]),
        mesh=mesh,
        in_specs=placed,
        out_specs=(P(None, ("col", "row")), P(None, ("col", "row"))),
        check_vma=False,
    )
```

time: 61.9 us -> 46.4 us (0.75)
  blocking collectives: 10.6 us -> 0 us
  local copies, waits for them, and re-layouts: 6.32 us -> 0 us
  Pallas kernels: 25.7 us -> 21.7 us
  waiting for transfers between devices: 4.41 us -> 8.22 us
  starting transfers between devices: 13.3 us -> 15.3 us
    all_gather x2 -> x0, blocking collectives: 10.6 us -> none  [the longest x1 5.41 us: on_device(): sources = lax.all_gather(row_send, 'row', axis=1, tiled=True)]
    unnamed x18 -> x0, local copies, waits for them, and re-layouts: 6.32 us -> none
    pallas_call x5 -> x9, Pallas kernels: 25.7 us -> 21.7 us  [call(): pl.pallas_call(kernel, out_shape=outs, in_specs=specs or [VMEM] * len(arg...]
    ppermute x0 -> x4, waiting for transfers between devices: none -> 3.49 us  [exchange(): arrived = lax.ppermute(held, axis, [(i, i ^ 1 << k) for i in range(size)])]
    ppermute x0 -> x4, starting transfers between devices: none -> 2.09 us  [exchange(): arrived = lax.ppermute(held, axis, [(i, i ^ 1 << k) for i in range(size)])]
  transfers between devices with their start and end apart: 2 -> 6, of which waited for: 1 -> 4; matrix products, arithmetic and copies ran while one was open for 0% -> 0% of each run, Pallas kernels for 34% -> 36%
where the time goes in v2:
time: 46.4 us; the launch traced here: 46 us
  Pallas kernels  21.7 us (47%)
  starting transfers between devices  15.3 us (33%)
  waiting for transfers between devices  8.22 us (18%)
  between operations  0.7 us (2%)
    pallas_call x9, Pallas kernels, call(): pl.pallas_call(kernel, out_shape=outs, in_specs=specs or [VMEM] * len(arg...  21.7 us
    all_to_all x1, starting transfers between devices, on_device(): lax.all_to_all(sent, 'col', split_axis=0, concat_axis=0, tiled=True)  7.26 us
    all_to_all x1, starting transfers between devices, on_device(): lax.all_to_all(mom_sent, 'col', split_axis=0, concat_axis=0, tiled=True)  5.98 us
    all_to_all x1, waiting for transfers between devices, on_device(): lax.all_to_all(mom_sent, 'col', split_axis=0, concat_axis=0, tiled=True)  4.73 us
    ppermute x4, waiting for transfers between devices, exchange(): arrived = lax.ppermute(held, axis, [(i, i ^ 1 << k) for i in range(size)])  3.49 us
    ppermute x4, starting transfers between devices, exchange(): arrived = lax.ppermute(held, axis, [(i, i ^ 1 << k) for i in range(size)])  2.09 us
  transfers between devices with their start and end apart: 6, of which 4 were waited for; matrix products, arithmetic and copies ran while one was open for 0% of the time, Pallas kernels for 36%

profile of v2, /device:TPU:0, one launch (start us, length us, event | category | flops | bytes accessed | tf_op | source)
XLA Modules:
  0.0 46.0 jit_solution(2125068034020299908)
XLA Ops:
  0.6 1.6 %pack.1 = (f32[8,64,128]{2,1,0:T(8,128)}, f32[64,128]{1,0:T(8,128)S(1)}) custom-call(f32[3,1024]{1,0:T(4,128)} %refs_0_.1, f32[3,1024]{1,0:T(4,128)} %refs_1_.1, f32[3,1024]{1,0:T(4,128)} %refs_2_.1, f32[1,1024]{1,0:T(1,128)} %bitcast.15, s32[8,512]{1,0:T(8,128)} %bitcast.13, s32[8,512]{1,0:T(8,128)} %bitcast.14, s32[1,8]{1,0:T(1,128)} %bitcast.16), custom_call_target="tpu_custom_call" | custom-call | tf_op jit(solution)/shard_map/pack/pallas_call | solution.py:342
  2.3 7.3 %all-to-all-start = ((f32[8,64,128]{2,1,0:T(8,128)}), f32[8,64,128]{2,1,0:T(8,128)S(1)}, u32[]{:S(2)}, u32[]{:S(2)}) async-start(f32[8,64,128]{2,1,0:T(8,128)} %get-tuple-element.26.sent), calls=%async_computation | async-start | bytes 524288 | tf_op jit(solution)/shard_map/all_to_all | solution.py:437
  9.5 0.0 collective-permute-start
  9.6 1.2 %collective-permute-done.refs_1_ = f32[1,64,128]{2,1,0:T(8,128)S(1)} collective-permute-done((f32[1,64,128]{2,1,0:T(8,128)S(1)}, f32[1,64,128]{2,1,0:T(8,128)S(1)}, u32[]{:S(2)}, u32[]{:S(2)}) %collective-permute-start) | collective-permute-done | bytes 32800 | tf_op jit(solution)/shard_map/ppermute | solution.py:363
  10.8 1.5 %collective-permute-start.1 = (f32[2,64,128]{2,1,0:T(8,128)S(1)}, f32[2,64,128]{2,1,0:T(8,128)S(1)}, u32[]{:S(2)}, u32[]{:S(2)}) collective-permute-start(f32[2,64,128]{2,1,0:T(8,128)S(1)} %pad_maximum_fusion), channel_id=1, source_target_pairs={{0,16},{8,24},{16,0},{24,8},{1,17},{9,25},{17,1},{25,9},{2,18},{10... | collective-permute-start | bytes 196616 | tf_op jit(solution)/shard_map/ppermute | solution.py:363
  12.3 2.5 %field_sums.6 = (f32[48,1024]{1,0:T(8,128)S(1)}, bf16[1024,1024]{1,0:T(8,128)(2,1)S(1)}, bf16[1024,1024]{1,0:T(8,128)(2,1)S(1)}) custom-call(f32[64,128]{1,0:T(8,128)S(1)} %get-tuple-element.15.refs_0_, f32[1,64,128]{2,1,0:T(8,128)S(1)} %bitcast.8), custom_call_target="tpu_custom_call" | custom-call | tf_op jit(solution)/shard_map/field_sums/pallas_call | solution.py:342
  14.8 2.5 %field_sums.7 = (f32[48,1024]{1,0:T(8,128)S(1)}, bf16[1024,1024]{1,0:T(8,128)(2,1)S(1)}, bf16[1024,1024]{1,0:T(8,128)(2,1)S(1)}) custom-call(f32[64,128]{1,0:T(8,128)S(1)} %get-tuple-element.15.refs_0_, f32[1,64,128]{2,1,0:T(8,128)S(1)} %collective-permute-done.refs_1_, f32[48,1024]{1,0:T(8,128)S(1)} %get-tuple-element.16.refs_2_), custom_call_target="tpu_custom_call" | custom-call | tf_op jit(solution)/shard_map/field_sums/pallas_call | solution.py:342
  17.3 0.0 collective-permute-done.1.refs_1_
  17.3 4.6 %field_sums.8 = (f32[24,128]{1,0:T(8,128)S(1)}, bf16[2048,1024]{1,0:T(8,128)(2,1)S(1)}, bf16[2048,1024]{1,0:T(8,128)(2,1)S(1)}) custom-call(f32[64,128]{1,0:T(8,128)S(1)} %get-tuple-element.15.refs_0_, f32[2,64,128]{2,1,0:T(8,128)S(1)} %collective-permute-done.1.refs_1_, f32[48,1024]{1,0:T(8,128)S(1)} %get-tuple-element.17.refs_2_), custom_call_target="tpu_custom_call" | custom-call | tf_op jit(solution)/shard_map/field_sums/pallas_call | solution.py:342
  21.8 0.1 collective-permute-start.2
  21.9 1.2 %collective-permute-done.2.refs_3_ = f32[1,24,128]{2,1,0:T(8,128)S(1)} collective-permute-done((f32[1,24,128]{2,1,0:T(8,128)S(1)}, f32[1,24,128]{2,1,0:T(8,128)S(1)}, u32[]{:S(2)}, u32[]{:S(2)}) %collective-permute-start.2) | collective-permute-done | bytes 12320 | tf_op jit(solution)/shard_map/ppermute | solution.py:363
  23.1 0.5 %collective-permute-start.3 = (f32[2,24,128]{2,1,0:T(8,128)S(1)}, f32[2,24,128]{2,1,0:T(8,128)S(1)}, u32[]{:S(2)}, u32[]{:S(2)}) collective-permute-start(f32[2,24,128]{2,1,0:T(8,128)S(1)} %pad_maximum_fusion.1), channel_id=1, source_target_pairs={{0,16},{8,24},{16,0},{24,8},{1,17},{9,25},{17,1},{25,9},{2,18},{10... | collective-permute-start | bytes 73736 | tf_op jit(solution)/shard_map/ppermute | solution.py:363
  23.6 1.1 %field_sums.9.refs_6_ = f32[48,1024]{1,0:T(8,128)S(1)} custom-call(f32[64,128]{1,0:T(8,128)S(1)} %get-tuple-element.15.refs_0_, f32[1,64,128]{2,1,0:T(8,128)S(1)} %bitcast.9, f32[24,128]{1,0:T(8,128)S(1)} %get-tuple-element.18.refs_2_, f32[1,24,128]{2,1,0:T(8,128)S(1)} %bitcast.12, bf16[1024,1024]{1,0:T(8,128)(2,1)S(1)} %get-tuple-element.23.refs_4_, ...), custom_call_target="tpu_custom_call" | custom-call | tf_op jit(solution)/shard_map/field_sums/pallas_call | solution.py:342
  24.7 1.1 %field_sums.10.refs_6_ = f32[48,1024]{1,0:T(8,128)S(1)} custom-call(f32[64,128]{1,0:T(8,128)S(1)} %get-tuple-element.15.refs_0_, f32[1,64,128]{2,1,0:T(8,128)S(1)} %collective-permute-done.refs_1_, f32[24,128]{1,0:T(8,128)S(1)} %get-tuple-element.18.refs_2_, f32[1,24,128]{2,1,0:T(8,128)S(1)} %collective-permute-done.2.refs_3_, ...), custom_call_target="tpu_custom_call" | custom-call | tf_op jit(solution)/shard_map/field_sums/pallas_call | solution.py:342
  25.8 1.1 %collective-permute-done.3.refs_3_ = f32[2,24,128]{2,1,0:T(8,128)S(1)} collective-permute-done((f32[2,24,128]{2,1,0:T(8,128)S(1)}, f32[2,24,128]{2,1,0:T(8,128)S(1)}, u32[]{:S(2)}, u32[]{:S(2)}) %collective-permute-start.3) | collective-permute-done | bytes 24608 | tf_op jit(solution)/shard_map/ppermute | solution.py:363
  26.9 2.6 %field_sums.11 = (f32[3,1024]{1,0:T(4,128)}, f32[8,24,128]{2,1,0:T(8,128)}) custom-call(f32[64,128]{1,0:T(8,128)S(1)} %get-tuple-element.15.refs_0_, f32[2,64,128]{2,1,0:T(8,128)S(1)} %collective-permute-done.1.refs_1_, f32[24,128]{1,0:T(8,128)S(1)} %get-tuple-element.18.refs_2_, f32[2,24,128]{2,1,0:T(8,128)S(1)} %collective-permute-done.3.refs_3_, ...), custom_call_target="tpu_custom_call" | custom-call | tf_op jit(solution)/shard_map/field_sums/pallas_call | solution.py:342
  29.5 0.0 all-to-all-done.received
  29.5 6.0 %all-to-all-start.1 = ((f32[8,24,128]{2,1,0:T(8,128)}), f32[8,24,128]{2,1,0:T(8,128)S(1)}, u32[]{:S(2)}, u32[]{:S(2)}) async-start(f32[8,24,128]{2,1,0:T(8,128)} %get-tuple-element.27.mom_sent), calls=%async_computation.1 | async-start | bytes 196608 | tf_op jit(solution)/shard_map/all_to_all | solution.py:455
  35.5 2.4 %contact_geometry.1.geometry = f32[8,4,8,128]{3,2,1,0:T(8,128)S(1)} custom-call(f32[8,64,128]{2,1,0:T(8,128)} %get-tuple-element.26.sent, f32[8,64,128]{2,1,0:T(8,128)S(1)} %all-to-all-done.received), custom_call_target="tpu_custom_call" | custom-call | tf_op jit(solution)/shard_map/contact_geometry/pallas_call | solution.py:342
  37.9 4.7 %all-to-all-done.1.mom_received = f32[8,24,128]{2,1,0:T(8,128)S(1)} async-done(((f32[8,24,128]{2,1,0:T(8,128)}), f32[8,24,128]{2,1,0:T(8,128)S(1)}, u32[]{:S(2)}, u32[]{:S(2)}) %all-to-all-start.1) | async-done | bytes 98336 | tf_op jit(solution)/shard_map/all_to_all | solution.py:455
  42.6 3.4 %contact_force.1 = f32[3,1024]{1,0:T(4,128)} custom-call(f32[8,4,8,128]{3,2,1,0:T(8,128)S(1)} %contact_geometry.1.geometry, f32[8,64,128]{2,1,0:T(8,128)} %get-tuple-element.26.sent, f32[8,64,128]{2,1,0:T(8,128)S(1)} %all-to-all-done.received, f32[8,24,128]{2,1,0:T(8,128)} %get-tuple-element.27.mom_sent, f32[8,24,128]{2,1,0:T(8,128)S(1)} %all-to-all-done.1.mom_received), custom_call_target="tpu_custom_call" | custom-call | tf_op jit(solution)/shard_map/contact_force/pallas_call | solution.py:342
  (2 shorter events, 0.0 us)
Async XLA Ops:
  2.3 27.2 %all-to-all-start = ((f32[8,64,128]{2,1,0:T(8,128)}), f32[8,64,128]{2,1,0:T(8,128)S(1)}, u32[]{:S(2)}, u32[]{:S(2)}) async-start(f32[8,64,128]{2,1,0:T(8,128)} %get-tuple-element.26.sent), calls=%async_computation | async-start | bytes 524288 | tf_op jit(solution)/shard_map/all_to_all | solution.py:437
  9.5 1.2 %collective-permute-start = (f32[1,64,128]{2,1,0:T(8,128)S(1)}, f32[1,64,128]{2,1,0:T(8,128)S(1)}, u32[]{:S(2)}, u32[]{:S(2)}) collective-permute-start(f32[1,64,128]{2,1,0:T(8,128)S(1)} %bitcast.6), channel_id=1, source_target_pairs={{0,8},{8,0},{16,24},{24,16},{1,9},{9,1},{17,25},{25,17},{2,10},{10... | collective-permute-start | bytes 98312 | tf_op jit(solution)/shard_map/ppermute | solution.py:363
  10.8 6.5 %collective-permute-start.1 = (f32[2,64,128]{2,1,0:T(8,128)S(1)}, f32[2,64,128]{2,1,0:T(8,128)S(1)}, u32[]{:S(2)}, u32[]{:S(2)}) collective-permute-start(f32[2,64,128]{2,1,0:T(8,128)S(1)} %pad_maximum_fusion), channel_id=1, source_target_pairs={{0,16},{8,24},{16,0},{24,8},{1,17},{9,25},{17,1},{25,9},{2,18},{10... | collective-permute-start | bytes 196616 | tf_op jit(solution)/shard_map/ppermute | solution.py:363
  21.8 1.2 %collective-permute-start.2 = (f32[1,24,128]{2,1,0:T(8,128)S(1)}, f32[1,24,128]{2,1,0:T(8,128)S(1)}, u32[]{:S(2)}, u32[]{:S(2)}) collective-permute-start(f32[1,24,128]{2,1,0:T(8,128)S(1)} %bitcast.10), channel_id=1, source_target_pairs={{0,8},{8,0},{16,24},{24,16},{1,9},{9,1},{17,25},{25,17},{2,10},{10... | collective-permute-start | bytes 36872 | tf_op jit(solution)/shard_map/ppermute | solution.py:363
  23.1 3.8 %collective-permute-start.3 = (f32[2,24,128]{2,1,0:T(8,128)S(1)}, f32[2,24,128]{2,1,0:T(8,128)S(1)}, u32[]{:S(2)}, u32[]{:S(2)}) collective-permute-start(f32[2,24,128]{2,1,0:T(8,128)S(1)} %pad_maximum_fusion.1), channel_id=1, source_target_pairs={{0,16},{8,24},{16,0},{24,8},{1,17},{9,25},{17,1},{25,9},{2,18},{10... | collective-permute-start | bytes 73736 | tf_op jit(solution)/shard_map/ppermute | solution.py:363
  29.5 13.1 %all-to-all-start.1 = ((f32[8,24,128]{2,1,0:T(8,128)}), f32[8,24,128]{2,1,0:T(8,128)S(1)}, u32[]{:S(2)}, u32[]{:S(2)}) async-start(f32[8,24,128]{2,1,0:T(8,128)} %get-tuple-element.27.mom_sent), calls=%async_computation.1 | async-start | bytes 196608 | tf_op jit(solution)/shard_map/all_to_all | solution.py:455

commit v3 on v2

--- a/solution.py
+++ b/solution.py
@@ -15,6 +15,7 @@
 PAIR_ROWS = 24
 KEEP_BYTES = 20 * 2**20
 BLOCK = 512
+WIDTH = 256
 F32 = jnp.float32
 BF16 = jnp.bfloat16
 VMEM = pl.BlockSpec(memory_space=pltpu.VMEM)
@@ -110,15 +111,20 @@
     return [p - c for p, c in zip(pos, center)]
 
 
-def field_kernel(has_mom, has_kept, has_before, is_last, columns, *refs):
+def field_kernel(sources, with_mom, kept_at, has_before, is_last, columns, *refs):
     refs = list(refs)
-    own, source = refs.pop(0), refs.pop(0)
-    own_mom, source_mom = (refs.pop(0), refs.pop(0)) if has_mom else (None, None)
+    own = refs.pop(0)
+    blocks = [ref.at[k] for ref in refs[:sources] for k in range(ref.shape[0])]
+    refs = refs[sources:]
+    if with_mom:
+        own_mom = refs.pop(0)
+        mom_blocks = [ref.at[k] for ref in refs[:sources] for k in range(ref.shape[0])]
+        refs = refs[sources:]
+    has_kept = kept_at is not None
     kept = (refs.pop(0), refs.pop(0)) if has_kept else None
     before = refs.pop(0) if has_before else None
     outs, (held, target, feats, sums) = refs[:-4], refs[-4:]
     made = outs[1:] if len(outs) == 3 else None
-    blocks = source.shape[0]
     groups = held.shape[1]
     count = groups * LANES
     own_pos = vectors_of(own, 0, groups)
@@ -127,63 +133,71 @@
     if not has_kept:
         target_rows(pos, held, target)
     sums[...] = before[...] if has_before else jnp.zeros_like(sums)
-    for k in range(blocks):
-        there = source.at[k]
+    for k, there in enumerate(blocks):
         their_pos = about(vectors_of(there, 0, groups), center)
-        if has_mom:
-            their_mom = vectors_of(source_mom.at[k], 0, groups)
+        if with_mom:
+            their_mom = vectors_of(mom_blocks[k], 0, groups)
         else:
             chi = there[6 * groups : 7 * groups, :]
             their_mom = [chi * v for v in vectors_of(there, 3 * groups, groups)]
         moment_rows(their_pos, their_mom, held, feats, k * count)
         if not has_kept:
             source_rows(their_pos, held, feats, k * count)
-    block = math.gcd(count, BLOCK)
-    for start in range(0, blocks * count, block):
-        part = slice(start, start + block)
-        if has_kept:
-            high, low = kept[0][part, :], kept[1][part, :]
-        else:
-            radius_sq = lax.dot_general(
-                feats[3 * FEATURES :, part],
-                target[...],
-                (((0,), (0,)), ((), ())),
-                preferred_element_type=F32,
-            )
+    height, width = math.gcd(count, BLOCK), math.gcd(count, WIDTH)
+    tiles = [
+        (slice(a, a + height), slice(b, b + width))
+        for a in range(0, len(blocks) * count, height)
+        for b in range(0, count, width)
+    ]
+
+    def radius_of(tile):
+        return lax.dot_general(
+            feats[3 * FEATURES :, tile[0]],
+            target[:, tile[1]],
+            (((0,), (0,)), ((), ())),
+            preferred_element_type=F32,
+        )
+
+    def add(tile, high, low):
+        moments = feats[0 : 3 * FEATURES, tile[0]]
+        sums[:, tile[1]] += jnp.dot(moments, high, preferred_element_type=F32) + jnp.dot(
+            moments, low, preferred_element_type=F32
+        )
+
+    if has_kept:
+        for a, b in tiles:
+            rows = slice(kept_at + a.start, kept_at + a.stop)
+            add((a, b), kept[0][rows, b], kept[1][rows, b])
+    else:
+        radius_sq, ready = radius_of(tiles[0]), None
+        for at, tile in enumerate(tiles):
+            following = radius_of(tiles[at + 1]) if at + 1 < len(tiles) else None
             high, low = pair_coefficient(radius_sq)
             if made:
-                made[0][part, :] = high
-                made[1][part, :] = low
-        moments = feats[0 : 3 * FEATURES, part]
-        sums[...] += jnp.dot(moments, high, preferred_element_type=F32) + jnp.dot(
-            moments, low, preferred_element_type=F32
-        )
+                made[0][tile] = high
+                made[1][tile] = low
+            if ready is not None:
+                add(*ready)
+            ready, radius_sq = (tile, high, low), following
+        add(*ready)
     if not is_last:
         outs[0][...] = sums[...]
         return
     applied = vectors_of(own, 3 * groups, groups)
     chi = own[6 * groups : 7 * groups, :]
-    own_now = vectors_of(own_mom, 0, groups) if has_mom else [chi * v for v in applied]
+    own_now = vectors_of(own_mom, 0, groups) if with_mom else [chi * v for v in applied]
     field = field_from_sums(sums, held, pos, own_now)
-    result = [chi * (applied[a] + field[a]) for a in range(3)]
-    if not columns:
-        for a in range(3):
-            outs[0][a * groups : (a + 1) * groups, :] = result[a]
-        return
     for a in range(3):
-        for e in range(columns):
-            outs[1][e, a * groups : (a + 1) * groups, :] = result[a]
-        for g in range(groups):
-            outs[0][a : a + 1, g * LANES : (g + 1) * LANES] = result[a][g : g + 1, :]
-
-
-def pack_kernel(*refs):
-    inputs, (send, payload), (pos, vel, field, chi, owner, partner, counts, done) = (
-        refs[0:7],
-        refs[7:9],
-        refs[9:],
-    )
-    held = (pos, vel, field, chi, owner, partner, counts)
+        result = chi * (applied[a] + field[a])
+        rows = slice(a * groups, (a + 1) * groups)
+        if columns:
+            for e in range(columns):
+                outs[0][e, rows, :] = result
+        else:
+            outs[0][rows, :] = result
+
+
+def copy_in(inputs, held, done):
     copies = [
         pltpu.make_async_copy(src, dst, done.at[k]) for k, (src, dst) in enumerate(zip(inputs, held))
     ]
@@ -191,19 +205,33 @@
         copy.start()
     for copy in copies:
         copy.wait()
+
+
+def row_pack_kernel(*refs):
+    inputs, payload, (pos, field, chi, done) = refs[0:3], refs[3], refs[4:]
+    copy_in(inputs, (pos, field, chi), done)
     groups = pos.shape[1] // LANES
-    slots = owner.shape[1] // LANES
-    columns = owner.shape[0]
     for g in range(groups):
         lanes = slice(g * LANES, (g + 1) * LANES)
         for c in range(3):
-            row = slice(c * groups + g, c * groups + g + 1)
-            payload[row, :] = pos[c : c + 1, lanes]
-            row = slice((3 + c) * groups + g, (3 + c) * groups + g + 1)
-            payload[row, :] = field[c : c + 1, lanes]
-            send[0, row, :] = vel[c : c + 1, lanes]
+            payload[c * groups + g : c * groups + g + 1, :] = pos[c : c + 1, lanes]
+            row = (3 + c) * groups + g
+            payload[row : row + 1, :] = field[c : c + 1, lanes]
         payload[6 * groups + g : 6 * groups + g + 1, :] = chi[:, lanes]
+    payload[7 * groups :, :] = jnp.zeros_like(payload[7 * groups :, :])
+
+
+def column_pack_kernel(*refs):
+    inputs, payload, send, (vel, owner, partner, counts, done) = refs[0:4], refs[4], refs[5], refs[6:]
+    copy_in(inputs, (vel, owner, partner, counts), done)
+    groups = vel.shape[1] // LANES
+    slots = owner.shape[1] // LANES
+    columns = owner.shape[0]
     send[0, 0 : 3 * groups, :] = payload[0 : 3 * groups, :]
+    for g in range(groups):
+        for c in range(3):
+            row = (3 + c) * groups + g
+            send[0, row : row + 1, :] = vel[c : c + 1, g * LANES : (g + 1) * LANES]
     for e in range(1, columns):
         send[e, 0 : 6 * groups, :] = send[0, 0 : 6 * groups, :]
     for q in range(slots):
@@ -259,9 +287,14 @@
     ]
 
 
-def geometry_kernel(slots, groups, sent, received, out):
+def geometry_kernel(slots, sent, received, mom_sent, moments, out, places, hot):
     columns = sent.shape[0]
+    groups = mom_sent.shape[1] // 3
     count_row = 6 * groups + 2 * slots
+    for c in range(3):
+        for g in range(groups):
+            lanes = slice(g * LANES, (g + 1) * LANES)
+            moments[c : c + 1, lanes] = mom_sent[0, c * groups + g : c * groups + g + 1, :]
     for at, (kind, rows, q) in enumerate(contact_blocks(columns, slots)):
         mine, other = slot_index(sent, received, kind, rows, q, groups, slots)
         count = (received if kind else sent)[rows, count_row, :]
@@ -283,40 +316,45 @@
         inverse = lax.rsqrt(radius_sq)
         normal = [jnp.where(live, gap[c] * inverse, 0.0) for c in range(3)]
         speed = gap[3] * normal[0] + gap[4] * normal[1] + gap[5] * normal[2]
+        own = [look_up(own_tables(mom_sent.at[0], c * groups, groups), lane, bits) for c in range(3)]
         for c in range(3):
             out[at, c] = normal[c]
-        out[at, 3] = -0.03 * (radius_sq * inverse - 1.0) - 0.5 * speed
-
-
-def force_kernel(slots, geometry, sent, received, mom_sent, mom_received, forces, places, pieces):
+            out[at, 3 + c] = own[c]
+        out[at, 6] = -0.03 * (radius_sq * inverse - 1.0) - 0.5 * speed
+        out[at, 7] = own[0] * normal[0] + own[1] * normal[1] + own[2] * normal[2]
+        lanes = slice(q * LANES, (q + 1) * LANES)
+        places[kind, 0, rows, lanes] = group
+        places[kind, 1, rows, lanes] = lane
+    lane_of = lax.broadcasted_iota(jnp.int32, (LANES, slots * LANES), 0)
+    for kind in range(2):
+        for e in range(columns):
+            here = places[kind, 1, e : e + 1, :] == lane_of
+            hot[kind * columns + e] = jnp.where(here, 1.0, 0.0).astype(BF16)
+
+
+def force_kernel(slots, geometry, places, hot, sent, received, mom_received, forces, pieces):
     columns = sent.shape[0]
     groups = mom_received.shape[1] // 3
     for at, (kind, rows, q) in enumerate(contact_blocks(columns, slots)):
-        mine, other = slot_index(sent, received, kind, rows, q, groups, slots)
-        lane, group = split_index(mine)
-        bits = bits_of(group, groups)
+        unused, other = slot_index(sent, received, kind, rows, q, groups, slots)
         their_lane, their_group = split_index(other)
         their_bits = bits_of(their_group, groups)
         normal = [geometry[at, c] for c in range(3)]
-        own = [look_up(own_tables(mom_sent.at[0], c * groups, groups), lane, bits) for c in range(3)]
+        own = [geometry[at, 3 + c] for c in range(3)]
+        along_own = geometry[at, 7]
         their = [
             look_up(their_tables(mom_received, rows, c * groups, groups), their_lane, their_bits)
             for c in range(3)
         ]
-        along_own = own[0] * normal[0] + own[1] * normal[1] + own[2] * normal[2]
         along_their = their[0] * normal[0] + their[1] * normal[1] + their[2] * normal[2]
         product = own[0] * their[0] + own[1] * their[1] + own[2] * their[2]
-        radial = 3.0 * (product - 5.0 * along_own * along_their) + geometry[at, 3]
+        radial = 3.0 * (product - 5.0 * along_own * along_their) + geometry[at, 6]
         lanes = slice(q * LANES, (q + 1) * LANES)
-        places[kind, 0, rows, lanes] = group
-        places[kind, 1, rows, lanes] = lane
         for c in range(3):
             force = 3.0 * (along_own * their[c] + along_their * own[c]) + radial * normal[c]
             for k, piece in enumerate(split3(force)):
                 pieces[kind, k * 3 + c, rows, lanes] = piece
-    width = slots * LANES
-    row_of = lax.broadcasted_iota(jnp.int32, (groups, width), 0)
-    lane_of = lax.broadcasted_iota(jnp.int32, (LANES, width), 0)
+    row_of = lax.broadcasted_iota(jnp.int32, (groups, slots * LANES), 0)
     total = None
     for kind in range(2):
         for e in range(columns):
@@ -324,9 +362,11 @@
             values = jnp.concatenate(
                 [jnp.where(here, pieces[kind, k, e : e + 1, :], 0.0) for k in range(9)], axis=0
             ).astype(BF16)
-            hot = jnp.where(places[kind, 1, e : e + 1, :] == lane_of, 1.0, 0.0).astype(BF16)
             summed = lax.dot_general(
-                values, hot, (((1,), (1,)), ((), ())), preferred_element_type=F32
+                values,
+                hot[kind * columns + e],
+                (((1,), (1,)), ((), ())),
+                preferred_element_type=F32,
             )
             total = summed if total is None else total + summed
     height = 3 * groups
@@ -371,27 +411,33 @@
     count = payload.shape[0] // SUBS * LANES
     groups = count // LANES
     sums, made = None, []
-    for k, source in enumerate(payloads):
+    for k, sources in enumerate(payloads):
         is_last = k == len(payloads) - 1
-        length = source.shape[0] * count
-        args = [payload, source]
+        length = sum(a.shape[0] for a in sources) * count
+        args = [payload, *sources]
         if mom is not None:
-            args += [mom, moms[k]]
+            args += [mom, *moms[k]]
         if kept:
-            args += kept[k]
+            args += kept[k][1]
         if sums is not None:
             args.append(sums)
         if not is_last:
             outs = (shape(3 * FEATURES, count),)
         elif columns:
-            outs = (shape(3, count), shape(columns, 3 * groups, LANES))
+            outs = (shape(columns, 3 * groups, LANES),)
         else:
             outs = (shape(3 * groups, LANES),)
         if keep:
             outs += (shape(length, count, dtype=BF16),) * 2
-        results = call(
+        sums, *now = call(
             functools.partial(
-                field_kernel, mom is not None, bool(kept), sums is not None, is_last, columns
+                field_kernel,
+                len(sources),
+                mom is not None,
+                kept[k][0] if kept else None,
+                sums is not None,
+                is_last,
+                columns,
             ),
             "field_sums",
             outs,
@@ -403,10 +449,8 @@
                 pltpu.VMEM((3 * FEATURES, count), F32),
             ],
         )
-        sums = results[0]
-        if keep:
-            made.append(results[1:])
-    return results, made
+        made.append(now)
+    return sums, made
 
 
 def on_device(row_size, positions, velocity, applied, suscept, owner, partner, contact_count):
@@ -415,57 +459,73 @@
     groups, slots = count // LANES, slot_len // LANES
     send_rows = 6 * groups + 2 * slots + 1
     send_rows += -send_rows % SUBS
-    inputs = (
-        positions,
+    def in_hbm(*arrays):
+        return [pltpu.with_memory_space_constraint(v, pltpu.HBM) for v in arrays]
+
+    inputs = in_hbm(positions, applied, suscept.reshape(1, count))
+    payload = call(
+        row_pack_kernel,
+        "row_pack",
+        shape(8 * groups, LANES),
+        *inputs,
+        specs=[HBM] * 3,
+        scratch=[pltpu.VMEM(v.shape, v.dtype) for v in inputs] + [pltpu.SemaphoreType.DMA((3,))],
+    )
+    inputs = in_hbm(
         velocity,
-        applied,
-        suscept.reshape(1, count),
         owner.reshape(columns, slot_len),
         partner.reshape(columns, slot_len),
         contact_count.reshape(1, columns),
     )
-    sent, payload = call(
-        pack_kernel,
-        "pack",
-        (shape(columns, send_rows, LANES), shape(8 * groups, LANES)),
-        *(pltpu.with_memory_space_constraint(v, pltpu.HBM) for v in inputs),
-        specs=[HBM] * 7,
+    sent = call(
+        column_pack_kernel,
+        "column_pack",
+        shape(columns, send_rows, LANES),
+        *inputs,
+        payload,
+        specs=[HBM] * 4 + [VMEM],
         scratch=[pltpu.VMEM(v.shape, v.dtype) for v in inputs[:-1]]
-        + [pltpu.SMEM((1, columns), jnp.int32), pltpu.SemaphoreType.DMA((7,))],
-    )
-    payloads = [payload[None]] + exchange(payload, "row", row_size)
+        + [pltpu.SMEM((1, columns), jnp.int32), pltpu.SemaphoreType.DMA((4,))],
+    )
+    rounds = exchange(payload, "row", row_size)
+    first, sent = lax.optimization_barrier((rounds[0], sent))
+    payloads = [[payload[None], first]] + [[r] for r in rounds[1:]]
     received = lax.all_to_all(sent, "col", split_axis=0, concat_axis=0, tiled=True)
     keep = 4 * row_size * count * count <= KEEP_BYTES
-    (mom, *unused), kept = add_fields(payload, payloads, None, None, None, 0, keep)
-    geometry = call(
-        functools.partial(geometry_kernel, slots, groups),
+    mom, made = add_fields(payload, payloads, None, None, None, 0, keep)
+    payloads = [[payload[None]], [first]] + payloads[1:]
+    kept = [(0, made[0]), (count, made[0])] + [(0, m) for m in made[1:]] if keep else None
+    for iteration in range(1, ITERS):
+        is_last = iteration == ITERS - 1
+        moms = [[mom[None]]] + [[r] for r in exchange(mom, "row", row_size)]
+        mom, unused = add_fields(
+            payload, payloads, mom, moms, kept, columns if is_last else 0, False
+        )
+    mom_received = lax.all_to_all(mom, "col", split_axis=0, concat_axis=0, tiled=True)
+    moments, geometry, places, hot = call(
+        functools.partial(geometry_kernel, slots),
         "contact_geometry",
-        shape(len(contact_blocks(columns, slots)), 4, SUBS, LANES),
+        (
+            shape(3, count),
+            shape(len(contact_blocks(columns, slots)), 8, SUBS, LANES),
+            shape(2, 2, columns, slot_len, dtype=jnp.int32),
+            shape(2 * columns, LANES, slot_len, dtype=BF16),
+        ),
         sent,
         received,
-    )
-    for iteration in range(1, ITERS):
-        is_last = iteration == ITERS - 1
-        moms = [mom[None]] + exchange(mom, "row", row_size)
-        results, unused = add_fields(
-            payload, payloads, mom, moms, kept, columns if is_last else 0, False
-        )
-        mom = results[0]
-    moments, mom_sent = results
-    mom_received = lax.all_to_all(mom_sent, "col", split_axis=0, concat_axis=0, tiled=True)
+        mom,
+    )
     forces = call(
         functools.partial(force_kernel, slots),
         "contact_force",
         shape(3, count),
         geometry,
+        places,
+        hot,
         sent,
         received,
-        mom_sent,
         mom_received,
-        scratch=[
-            pltpu.VMEM((2, 2, columns, slot_len), jnp.int32),
-            pltpu.VMEM((2, 9, columns, slot_len), F32),
-        ],
+        scratch=[pltpu.VMEM((2, 9, columns, slot_len), F32)],
     )
     return (moments, forces)
 

time: 46.4 us -> 44 us (0.948)
  waiting for transfers between devices: 8.22 us -> 5.48 us
    all_to_all x1, waiting for transfers between devices: 4.73 us -> 3.13 us  [on_device(): lax.all_to_all(mom, 'col', split_axis=0, concat_axis=0, tiled=True)]
    ppermute x4, waiting for transfers between devices: 3.49 us -> 2.36 us  [exchange(): arrived = lax.ppermute(held, axis, [(i, i ^ 1 << k) for i in range(size)])]
    ppermute x4, starting transfers between devices: 2.09 us -> 2.68 us  [exchange(): arrived = lax.ppermute(held, axis, [(i, i ^ 1 << k) for i in range(size)])]
  transfers between devices with their start and end apart: 6 -> 6, of which waited for: 4 -> 3; matrix products, arithmetic and copies ran while one was open for 0% -> 0% of each run, Pallas kernels for 36% -> 42%
where the time goes in v3:
time: 44 us; the launch traced here: 43.5 us
  Pallas kernels  21.8 us (50%)
  starting transfers between devices  15.5 us (35%)
  waiting for transfers between devices  5.48 us (12%)
  between operations  0.7 us (2%)
    pallas_call x9, Pallas kernels, call(): pl.pallas_call(kernel, out_shape=outs, in_specs=specs or [VMEM] * len(arg...  21.8 us
    all_to_all x1, starting transfers between devices, on_device(): lax.all_to_all(sent, 'col', split_axis=0, concat_axis=0, tiled=True)  6.83 us
    all_to_all x1, starting transfers between devices, on_device(): lax.all_to_all(mom, 'col', split_axis=0, concat_axis=0, tiled=True)  6.01 us
    all_to_all x1, waiting for transfers between devices, on_device(): lax.all_to_all(mom, 'col', split_axis=0, concat_axis=0, tiled=True)  3.13 us
    ppermute x4, starting transfers between devices, exchange(): arrived = lax.ppermute(held, axis, [(i, i ^ 1 << k) for i in range(size)])  2.68 us
    ppermute x4, waiting for transfers between devices, exchange(): arrived = lax.ppermute(held, axis, [(i, i ^ 1 << k) for i in range(size)])  2.36 us
  transfers between devices with their start and end apart: 6, of which 3 were waited for; matrix products, arithmetic and copies ran while one was open for 0% of the time, Pallas kernels for 42%

profile of v3, /device:TPU:0, one launch (start us, length us, event | category | flops | bytes accessed | tf_op | source)
XLA Modules:
  0.0 43.5 jit_solution(14572937591000329574)
XLA Ops:
  0.6 0.8 %row_pack.1.refs_4_.refs_0_ = f32[64,128]{1,0:T(8,128)S(1)} custom-call(f32[3,1024]{1,0:T(4,128)} %refs_0_.2, f32[3,1024]{1,0:T(4,128)} %refs_1_.1, f32[1,1024]{1,0:T(1,128)} %bitcast.15), custom_call_target="tpu_custom_call" | custom-call | tf_op jit(solution)/shard_map/row_pack/pallas_call | solution.py:382
  1.4 0.5 %collective-permute-start = (f32[1,64,128]{2,1,0:T(8,128)S(1)}, f32[1,64,128]{2,1,0:T(8,128)S(1)}, u32[]{:S(2)}, u32[]{:S(2)}) collective-permute-start(f32[1,64,128]{2,1,0:T(8,128)S(1)} %bitcast.6), channel_id=1, source_target_pairs={{0,8},{8,0},{16,24},{24,16},{1,9},{9,1},{17,25},{25,17},{2,10},{10... | collective-permute-start | bytes 98312 | tf_op jit(solution)/shard_map/ppermute | solution.py:403
  1.9 1.6 %column_pack.1.sent = f32[8,64,128]{2,1,0:T(8,128)} custom-call(f32[3,1024]{1,0:T(4,128)} %refs_0_.3, s32[8,512]{1,0:T(8,128)} %bitcast.13, s32[8,512]{1,0:T(8,128)} %bitcast.14, s32[1,8]{1,0:T(1,128)} %bitcast.16, f32[64,128]{1,0:T(8,128)S(1)} %row_pack.1.refs_4_.refs_0_), custom_call_target="tpu_custom_call" | custom-call | tf_op jit(solution)/shard_map/column_pack/pallas_call | solution.py:382
  3.5 0.0 collective-permute-done.refs_2_.refs_1_
  3.5 6.8 %all-to-all-start = ((f32[8,64,128]{2,1,0:T(8,128)}), f32[8,64,128]{2,1,0:T(8,128)S(1)}, u32[]{:S(2)}, u32[]{:S(2)}) async-start(f32[8,64,128]{2,1,0:T(8,128)} %column_pack.1.sent), calls=%async_computation | async-start | bytes 524288 | tf_op jit(solution)/shard_map/all_to_all | solution.py:493
  10.4 1.6 %collective-permute-start.1 = (f32[2,64,128]{2,1,0:T(8,128)S(1)}, f32[2,64,128]{2,1,0:T(8,128)S(1)}, u32[]{:S(2)}, u32[]{:S(2)}) collective-permute-start(f32[2,64,128]{2,1,0:T(8,128)S(1)} %pad_maximum_fusion), channel_id=1, source_target_pairs={{0,16},{8,24},{16,0},{24,8},{1,17},{9,25},{17,1},{25,9},{2,18},{10... | collective-permute-start | bytes 196616 | tf_op jit(solution)/shard_map/ppermute | solution.py:403
  12.0 4.0 %field_sums.5 = (f32[48,1024]{1,0:T(8,128)S(1)}, bf16[2048,1024]{1,0:T(8,128)(2,1)S(1)}, bf16[2048,1024]{1,0:T(8,128)(2,1)S(1)}) custom-call(f32[64,128]{1,0:T(8,128)S(1)} %row_pack.1.refs_4_.refs_0_, f32[1,64,128]{2,1,0:T(8,128)S(1)} %bitcast.8, f32[1,64,128]{2,1,0:T(8,128)S(1)} %collective-permute-done.refs_2_.refs_1_), custom_call_target="tpu_custom_call" | custom-call | tf_op jit(solution)/shard_map/field_sums/pallas_call | solution.py:382
  15.9 0.0 collective-permute-done.1.refs_1_
  15.9 3.9 %field_sums.6 = (f32[24,128]{1,0:T(8,128)S(1)}, bf16[2048,1024]{1,0:T(8,128)(2,1)S(1)}, bf16[2048,1024]{1,0:T(8,128)(2,1)S(1)}) custom-call(f32[64,128]{1,0:T(8,128)S(1)} %row_pack.1.refs_4_.refs_0_, f32[2,64,128]{2,1,0:T(8,128)S(1)} %collective-permute-done.1.refs_1_, f32[48,1024]{1,0:T(8,128)S(1)} %get-tuple-element.16.refs_2_), custom_call_target="tpu_custom_call" | custom-call | tf_op jit(solution)/shard_map/field_sums/pallas_call | solution.py:382
  19.8 0.1 collective-permute-start.2
  19.9 1.2 %collective-permute-done.2.refs_3_ = f32[1,24,128]{2,1,0:T(8,128)S(1)} collective-permute-done((f32[1,24,128]{2,1,0:T(8,128)S(1)}, f32[1,24,128]{2,1,0:T(8,128)S(1)}, u32[]{:S(2)}, u32[]{:S(2)}) %collective-permute-start.2) | collective-permute-done | bytes 12320 | tf_op jit(solution)/shard_map/ppermute | solution.py:403
  21.1 0.5 %collective-permute-start.3 = (f32[2,24,128]{2,1,0:T(8,128)S(1)}, f32[2,24,128]{2,1,0:T(8,128)S(1)}, u32[]{:S(2)}, u32[]{:S(2)}) collective-permute-start(f32[2,24,128]{2,1,0:T(8,128)S(1)} %pad_maximum_fusion.1), channel_id=1, source_target_pairs={{0,16},{8,24},{16,0},{24,8},{1,17},{9,25},{17,1},{25,9},{2,18},{10... | collective-permute-start | bytes 73736 | tf_op jit(solution)/shard_map/ppermute | solution.py:403
  21.6 1.1 %field_sums.7.refs_6_ = f32[48,1024]{1,0:T(8,128)S(1)} custom-call(f32[64,128]{1,0:T(8,128)S(1)} %row_pack.1.refs_4_.refs_0_, f32[1,64,128]{2,1,0:T(8,128)S(1)} %bitcast.9, f32[24,128]{1,0:T(8,128)S(1)} %get-tuple-element.17.refs_2_, f32[1,24,128]{2,1,0:T(8,128)S(1)} %bitcast.12, bf16[2048,1024]{1,0:T(8,128)(2,1)S(1)} %get-tuple-element.20.refs_4_, ...), custom_call_target="tpu_custom_call" | custom-call | tf_op jit(solution)/shard_map/field_sums/pallas_call | solution.py:382
  22.7 1.1 %field_sums.8.refs_6_ = f32[48,1024]{1,0:T(8,128)S(1)} custom-call(f32[64,128]{1,0:T(8,128)S(1)} %row_pack.1.refs_4_.refs_0_, f32[1,64,128]{2,1,0:T(8,128)S(1)} %collective-permute-done.refs_2_.refs_1_, f32[24,128]{1,0:T(8,128)S(1)} %get-tuple-element.17.refs_2_, f32[1,24,128]{2,1,0:T(8,128)S(1)} %collective-permute-done.2.refs_3_, ...), custom_call_target="tpu_custom_call" | custom-call | tf_op jit(solution)/shard_map/field_sums/pallas_call | solution.py:382
  23.7 1.2 %collective-permute-done.3.refs_3_ = f32[2,24,128]{2,1,0:T(8,128)S(1)} collective-permute-done((f32[2,24,128]{2,1,0:T(8,128)S(1)}, f32[2,24,128]{2,1,0:T(8,128)S(1)}, u32[]{:S(2)}, u32[]{:S(2)}) %collective-permute-start.3) | collective-permute-done | bytes 24608 | tf_op jit(solution)/shard_map/ppermute | solution.py:403
  24.9 2.5 %field_sums.9.mom_sent = f32[8,24,128]{2,1,0:T(8,128)} custom-call(f32[64,128]{1,0:T(8,128)S(1)} %row_pack.1.refs_4_.refs_0_, f32[2,64,128]{2,1,0:T(8,128)S(1)} %collective-permute-done.1.refs_1_, f32[24,128]{1,0:T(8,128)S(1)} %get-tuple-element.17.refs_2_, f32[2,24,128]{2,1,0:T(8,128)S(1)} %collective-permute-done.3.refs_3_, ...), custom_call_target="tpu_custom_call" | custom-call | tf_op jit(solution)/shard_map/field_sums/pallas_call | solution.py:382
  27.4 0.0 all-to-all-done.received
  27.4 6.0 %all-to-all-start.1 = ((f32[8,24,128]{2,1,0:T(8,128)}), f32[8,24,128]{2,1,0:T(8,128)S(1)}, u32[]{:S(2)}, u32[]{:S(2)}) async-start(f32[8,24,128]{2,1,0:T(8,128)} %field_sums.9.mom_sent), calls=%async_computation.1 | async-start | bytes 196608 | tf_op jit(solution)/shard_map/all_to_all | solution.py:504
  33.5 4.0 %contact_geometry.1 = (f32[3,1024]{1,0:T(4,128)}, f32[8,8,8,128]{3,2,1,0:T(8,128)S(1)}, s32[2,2,8,512]{3,2,1,0:T(8,128)S(1)}, bf16[16,128,512]{2,1,0:T(8,128)(2,1)S(1)}) custom-call(f32[8,64,128]{2,1,0:T(8,128)} %column_pack.1.sent, f32[8,64,128]{2,1,0:T(8,128)S(1)} %all-to-all-done.received, f32[8,24,128]{2,1,0:T(8,128)} %field_sums.9.mom_sent), custom_call_target="tpu_custom_call" | custom-call | tf_op jit(solution)/shard_map/contact_geometry/pallas_call | solution.py:382
  37.5 3.1 %all-to-all-done.1.mom_received = f32[8,24,128]{2,1,0:T(8,128)S(1)} async-done(((f32[8,24,128]{2,1,0:T(8,128)}), f32[8,24,128]{2,1,0:T(8,128)S(1)}, u32[]{:S(2)}, u32[]{:S(2)}) %all-to-all-start.1) | async-done | bytes 98336 | tf_op jit(solution)/shard_map/all_to_all | solution.py:504
  40.6 2.9 %contact_force.1 = f32[3,1024]{1,0:T(4,128)} custom-call(f32[8,8,8,128]{3,2,1,0:T(8,128)S(1)} %get-tuple-element.23.geometry, s32[2,2,8,512]{3,2,1,0:T(8,128)S(1)} %get-tuple-element.24.places, bf16[16,128,512]{2,1,0:T(8,128)(2,1)S(1)} %get-tuple-element.25.hot, f32[8,64,128]{2,1,0:T(8,128)} %column_pack.1.sent, f32[8,64,128]{2,1,0:T(8,128)S(1)} %all-to-all-done.received, ...), custom_call_target="tpu_custom_call" | custom-call | tf_op jit(solution)/shard_map/contact_force/pallas_call | solution.py:382
  (2 shorter events, 0.0 us)
Async XLA Ops:
  1.4 2.1 %collective-permute-start = (f32[1,64,128]{2,1,0:T(8,128)S(1)}, f32[1,64,128]{2,1,0:T(8,128)S(1)}, u32[]{:S(2)}, u32[]{:S(2)}) collective-permute-start(f32[1,64,128]{2,1,0:T(8,128)S(1)} %bitcast.6), channel_id=1, source_target_pairs={{0,8},{8,0},{16,24},{24,16},{1,9},{9,1},{17,25},{25,17},{2,10},{10... | collective-permute-start | bytes 98312 | tf_op jit(solution)/shard_map/ppermute | solution.py:403
  3.5 23.9 %all-to-all-start = ((f32[8,64,128]{2,1,0:T(8,128)}), f32[8,64,128]{2,1,0:T(8,128)S(1)}, u32[]{:S(2)}, u32[]{:S(2)}) async-start(f32[8,64,128]{2,1,0:T(8,128)} %column_pack.1.sent), calls=%async_computation | async-start | bytes 524288 | tf_op jit(solution)/shard_map/all_to_all | solution.py:493
  10.4 5.6 %collective-permute-start.1 = (f32[2,64,128]{2,1,0:T(8,128)S(1)}, f32[2,64,128]{2,1,0:T(8,128)S(1)}, u32[]{:S(2)}, u32[]{:S(2)}) collective-permute-start(f32[2,64,128]{2,1,0:T(8,128)S(1)} %pad_maximum_fusion), channel_id=1, source_target_pairs={{0,16},{8,24},{16,0},{24,8},{1,17},{9,25},{17,1},{25,9},{2,18},{10... | collective-permute-start | bytes 196616 | tf_op jit(solution)/shard_map/ppermute | solution.py:403
  19.8 1.2 %collective-permute-start.2 = (f32[1,24,128]{2,1,0:T(8,128)S(1)}, f32[1,24,128]{2,1,0:T(8,128)S(1)}, u32[]{:S(2)}, u32[]{:S(2)}) collective-permute-start(f32[1,24,128]{2,1,0:T(8,128)S(1)} %bitcast.10), channel_id=1, source_target_pairs={{0,8},{8,0},{16,24},{24,16},{1,9},{9,1},{17,25},{25,17},{2,10},{10... | collective-permute-start | bytes 36872 | tf_op jit(solution)/shard_map/ppermute | solution.py:403
  21.1 3.8 %collective-permute-start.3 = (f32[2,24,128]{2,1,0:T(8,128)S(1)}, f32[2,24,128]{2,1,0:T(8,128)S(1)}, u32[]{:S(2)}, u32[]{:S(2)}) collective-permute-start(f32[2,24,128]{2,1,0:T(8,128)S(1)} %pad_maximum_fusion.1), channel_id=1, source_target_pairs={{0,16},{8,24},{16,0},{24,8},{1,17},{9,25},{17,1},{25,9},{2,18},{10... | collective-permute-start | bytes 73736 | tf_op jit(solution)/shard_map/ppermute | solution.py:403
  27.4 13.1 %all-to-all-start.1 = ((f32[8,24,128]{2,1,0:T(8,128)}), f32[8,24,128]{2,1,0:T(8,128)S(1)}, u32[]{:S(2)}, u32[]{:S(2)}) async-start(f32[8,24,128]{2,1,0:T(8,128)} %field_sums.9.mom_sent), calls=%async_computation.1 | async-start | bytes 196608 | tf_op jit(solution)/shard_map/all_to_all | solution.py:504

commit v4 on v3

--- a/solution.py
+++ b/solution.py
@@ -12,7 +12,7 @@
 LANES = 128
 SUBS = 8
 FEATURES = 16
-PAIR_ROWS = 24
+PAIR_ROWS = 48
 KEEP_BYTES = 20 * 2**20
 BLOCK = 512
 WIDTH = 256
@@ -33,13 +33,19 @@
     return pos[0] * pos[0] + pos[1] * pos[1] + pos[2] * pos[2]
 
 
-def to_rows(vectors, held, out, first, columns):
-    groups = held.shape[1]
+def to_rows(vectors, held):
     for f, vector in enumerate(vectors):
         held[f] = vector
-    for g in range(groups):
+    return [held[0 : len(vectors), g, :] for g in range(held.shape[1])]
+
+
+def put_pieces(rows, out, first, columns, order):
+    for g, row in enumerate(rows):
+        pieces = split3(row)
         lanes = slice(columns + g * LANES, columns + (g + 1) * LANES)
-        out[first : first + len(vectors), lanes] = held[0 : len(vectors), g, :].astype(BF16)
+        out[first : first + len(order) * row.shape[0], lanes] = jnp.concatenate(
+            [pieces[k] for k in order], axis=0
+        ).astype(BF16)
 
 
 def moment_rows(pos, mom, held, out, columns):
@@ -47,24 +53,23 @@
     along = outer[0] + outer[4] + outer[8]
     square = norm_sq(pos)
     mixed = [3.0 * along * pos[a] - square * mom[a] for a in range(3)]
-    pieces = [split3(v) for v in list(mom) + outer + mixed + [along]]
-    for k in range(3):
-        to_rows([p[k] for p in pieces], held, out, k * FEATURES, columns)
+    put_pieces(to_rows(list(mom) + outer + mixed + [along], held), out, 0, columns, (0, 1, 2))
+
+
+TARGET_ORDER = (0, 1, 0, 1, 2, 0)
+SOURCE_ORDER = (0, 0, 1, 1, 0, 2)
 
 
 def target_rows(pos, held, out):
-    high, middle, low = zip(*(split3(p) for p in pos))
-    norms = split3(norm_sq(pos) + 1.0)
-    ones = (jnp.ones_like(pos[0]),) * 3
-    to_rows(high + high + middle + middle + high + low + norms + ones, held, out, 0, 0)
+    one, zero = jnp.ones_like(pos[0]), jnp.zeros_like(pos[0])
+    rows = list(pos) + [one, norm_sq(pos) + 1.0, zero, zero, zero]
+    put_pieces(to_rows(rows, held), out, 0, 0, TARGET_ORDER)
 
 
 def source_rows(pos, held, out, columns):
-    high, middle, low = zip(*(split3(p) for p in pos))
-    norms = split3(norm_sq(pos))
-    ones = (jnp.ones_like(pos[0]),) * 3
-    doubled = tuple(-2.0 * p for p in high + middle + high + middle + low + high)
-    to_rows(doubled + ones + norms, held, out, 3 * FEATURES, columns)
+    one, zero = jnp.ones_like(pos[0]), jnp.zeros_like(pos[0])
+    rows = [-2.0 * p for p in pos] + [norm_sq(pos), one, zero, zero, zero]
+    put_pieces(to_rows(rows, held), out, 3 * FEATURES, columns, SOURCE_ORDER)
 
 
 def field_from_sums(sums, held, pos, mom):
@@ -124,7 +129,7 @@
     kept = (refs.pop(0), refs.pop(0)) if has_kept else None
     before = refs.pop(0) if has_before else None
     outs, (held, target, feats, sums) = refs[:-4], refs[-4:]
-    made = outs[1:] if len(outs) == 3 else None
+    made = outs[1:3] if len(outs) == 3 else None
     groups = held.shape[1]
     count = groups * LANES
     own_pos = vectors_of(own, 0, groups)
@@ -190,11 +195,9 @@
     for a in range(3):
         result = chi * (applied[a] + field[a])
         rows = slice(a * groups, (a + 1) * groups)
-        if columns:
-            for e in range(columns):
-                outs[0][e, rows, :] = result
-        else:
-            outs[0][rows, :] = result
+        outs[0][rows, :] = result
+        for e in range(columns):
+            outs[1][e, rows, :] = result
 
 
 def copy_in(inputs, held, done):
@@ -222,25 +225,31 @@
 
 
 def column_pack_kernel(*refs):
-    inputs, payload, send, (vel, owner, partner, counts, done) = refs[0:4], refs[4], refs[5], refs[6:]
+    inputs, payload, (send, table, listed), (vel, owner, partner, counts, done) = (
+        refs[0:4],
+        refs[4],
+        refs[5:8],
+        refs[8:],
+    )
     copy_in(inputs, (vel, owner, partner, counts), done)
     groups = vel.shape[1] // LANES
     slots = owner.shape[1] // LANES
     columns = owner.shape[0]
-    send[0, 0 : 3 * groups, :] = payload[0 : 3 * groups, :]
+    table[0 : 3 * groups, :] = payload[0 : 3 * groups, :]
     for g in range(groups):
         for c in range(3):
             row = (3 + c) * groups + g
-            send[0, row : row + 1, :] = vel[c : c + 1, g * LANES : (g + 1) * LANES]
-    for e in range(1, columns):
-        send[e, 0 : 6 * groups, :] = send[0, 0 : 6 * groups, :]
+            table[row : row + 1, :] = vel[c : c + 1, g * LANES : (g + 1) * LANES]
+    for e in range(columns):
+        send[e, 0 : 6 * groups, :] = table[...]
+        live = jnp.full((send.shape[1] - 6 * groups - 2 * slots, LANES), counts[0, e])
+        send[e, 6 * groups + 2 * slots :, :] = live.astype(F32)
+        listed[2 * slots, e : e + 1, :] = live[0:1]
     for q in range(slots):
         lanes = slice(q * LANES, (q + 1) * LANES)
-        send[:, 6 * groups + q, :] = owner[:, lanes].astype(F32)
-        send[:, 6 * groups + slots + q, :] = partner[:, lanes].astype(F32)
-    tail = 6 * groups + 2 * slots
-    for e in range(columns):
-        send[e, tail:, :] = jnp.full((send.shape[1] - tail, LANES), counts[0, e].astype(F32))
+        for k, index in enumerate((owner[:, lanes], partner[:, lanes])):
+            send[:, 6 * groups + k * slots + q, :] = index.astype(F32)
+            listed[k * slots + q] = index
 
 
 def split_index(index):
@@ -271,11 +280,17 @@
     return [ref[rows, first + g, :] for g in range(groups)]
 
 
-def slot_index(sent, received, kind, rows, q, groups, slots):
-    ref = received if kind else sent
-    owner = ref[rows, 6 * groups + q, :].astype(jnp.int32)
-    partner = ref[rows, 6 * groups + slots + q, :].astype(jnp.int32)
-    return (partner, owner) if kind else (owner, partner)
+def slot_index(listed, received, kind, rows, q, groups, slots):
+    if kind:
+        first = 6 * groups + q
+        owner, partner, count = (
+            received[rows, row, :].astype(jnp.int32)
+            for row in (first, first + slots, 6 * groups + 2 * slots)
+        )
+    else:
+        owner, partner, count = (listed[row, rows, :] for row in (q, slots + q, 2 * slots))
+    live = lax.broadcasted_iota(jnp.int32, (SUBS, LANES), 1) + q * LANES < count
+    return (partner, owner, live) if kind else (owner, partner, live)
 
 
 def contact_blocks(columns, slots):
@@ -287,19 +302,15 @@
     ]
 
 
-def geometry_kernel(slots, sent, received, mom_sent, moments, out, places, hot):
-    columns = sent.shape[0]
-    groups = mom_sent.shape[1] // 3
-    count_row = 6 * groups + 2 * slots
+def geometry_kernel(slots, table, listed, received, mom, moments, out, places, hot):
+    columns = received.shape[0]
+    groups = mom.shape[0] // 3
     for c in range(3):
         for g in range(groups):
             lanes = slice(g * LANES, (g + 1) * LANES)
-            moments[c : c + 1, lanes] = mom_sent[0, c * groups + g : c * groups + g + 1, :]
+            moments[c : c + 1, lanes] = mom[c * groups + g : c * groups + g + 1, :]
     for at, (kind, rows, q) in enumerate(contact_blocks(columns, slots)):
-        mine, other = slot_index(sent, received, kind, rows, q, groups, slots)
-        count = (received if kind else sent)[rows, count_row, :]
-        slot = (lax.broadcasted_iota(jnp.int32, (SUBS, LANES), 1) + q * LANES).astype(F32)
-        live = slot < count
+        mine, other, live = slot_index(listed, received, kind, rows, q, groups, slots)
         lane, group = split_index(mine)
         bits = bits_of(group, groups)
         their_lane, their_group = split_index(other)
@@ -307,7 +318,7 @@
         gap = []
         for c in range(6):
             gap.append(
-                look_up(own_tables(sent.at[0], c * groups, groups), lane, bits)
+                look_up(own_tables(table, c * groups, groups), lane, bits)
                 - look_up(
                     their_tables(received, rows, c * groups, groups), their_lane, their_bits
                 )
@@ -316,7 +327,7 @@
         inverse = lax.rsqrt(radius_sq)
         normal = [jnp.where(live, gap[c] * inverse, 0.0) for c in range(3)]
         speed = gap[3] * normal[0] + gap[4] * normal[1] + gap[5] * normal[2]
-        own = [look_up(own_tables(mom_sent.at[0], c * groups, groups), lane, bits) for c in range(3)]
+        own = [look_up(own_tables(mom, c * groups, groups), lane, bits) for c in range(3)]
         for c in range(3):
             out[at, c] = normal[c]
             out[at, 3 + c] = own[c]
@@ -325,6 +336,7 @@
         lanes = slice(q * LANES, (q + 1) * LANES)
         places[kind, 0, rows, lanes] = group
         places[kind, 1, rows, lanes] = lane
+        places[kind, 2, rows, lanes] = other
     lane_of = lax.broadcasted_iota(jnp.int32, (LANES, slots * LANES), 0)
     for kind in range(2):
         for e in range(columns):
@@ -332,12 +344,12 @@
             hot[kind * columns + e] = jnp.where(here, 1.0, 0.0).astype(BF16)
 
 
-def force_kernel(slots, geometry, places, hot, sent, received, mom_received, forces, pieces):
-    columns = sent.shape[0]
+def force_kernel(slots, geometry, places, hot, mom_received, forces, pieces):
+    columns = mom_received.shape[0]
     groups = mom_received.shape[1] // 3
     for at, (kind, rows, q) in enumerate(contact_blocks(columns, slots)):
-        unused, other = slot_index(sent, received, kind, rows, q, groups, slots)
-        their_lane, their_group = split_index(other)
+        lanes = slice(q * LANES, (q + 1) * LANES)
+        their_lane, their_group = split_index(places[kind, 2, rows, lanes])
         their_bits = bits_of(their_group, groups)
         normal = [geometry[at, c] for c in range(3)]
         own = [geometry[at, 3 + c] for c in range(3)]
@@ -349,7 +361,6 @@
         along_their = their[0] * normal[0] + their[1] * normal[1] + their[2] * normal[2]
         product = own[0] * their[0] + own[1] * their[1] + own[2] * their[2]
         radial = 3.0 * (product - 5.0 * along_own * along_their) + geometry[at, 6]
-        lanes = slice(q * LANES, (q + 1) * LANES)
         for c in range(3):
             force = 3.0 * (along_own * their[c] + along_their * own[c]) + radial * normal[c]
             for k, piece in enumerate(split3(force)):
@@ -423,10 +434,9 @@
             args.append(sums)
         if not is_last:
             outs = (shape(3 * FEATURES, count),)
-        elif columns:
-            outs = (shape(columns, 3 * groups, LANES),)
         else:
             outs = (shape(3 * groups, LANES),)
+            outs += (shape(columns, 3 * groups, LANES),) if columns else ()
         if keep:
             outs += (shape(length, count, dtype=BF16),) * 2
         sums, *now = call(
@@ -443,7 +453,7 @@
             outs,
             *args,
             scratch=[
-                pltpu.VMEM((PAIR_ROWS, groups, LANES), F32),
+                pltpu.VMEM((FEATURES, groups, LANES), F32),
                 pltpu.VMEM((PAIR_ROWS, count), BF16),
                 pltpu.VMEM((3 * FEATURES + PAIR_ROWS, length), BF16),
                 pltpu.VMEM((3 * FEATURES, count), F32),
@@ -477,10 +487,14 @@
         partner.reshape(columns, slot_len),
         contact_count.reshape(1, columns),
     )
-    sent = call(
+    sent, table, listed = call(
         column_pack_kernel,
         "column_pack",
-        shape(columns, send_rows, LANES),
+        (
+            shape(columns, send_rows, LANES),
+            shape(6 * groups, LANES),
+            shape(2 * slots + 1, columns, LANES, dtype=jnp.int32),
+        ),
         *inputs,
         payload,
         specs=[HBM] * 4 + [VMEM],
@@ -493,25 +507,27 @@
     received = lax.all_to_all(sent, "col", split_axis=0, concat_axis=0, tiled=True)
     keep = 4 * row_size * count * count <= KEEP_BYTES
     mom, made = add_fields(payload, payloads, None, None, None, 0, keep)
-    payloads = [[payload[None]], [first]] + payloads[1:]
-    kept = [(0, made[0]), (count, made[0])] + [(0, m) for m in made[1:]] if keep else None
+    kept = [(0, m) for m in made] if keep else None
     for iteration in range(1, ITERS):
         is_last = iteration == ITERS - 1
-        moms = [[mom[None]]] + [[r] for r in exchange(mom, "row", row_size)]
-        mom, unused = add_fields(
+        arrived = exchange(mom, "row", row_size)
+        moms = [[mom[None], arrived[0]]] + [[r] for r in arrived[1:]]
+        mom, made = add_fields(
             payload, payloads, mom, moms, kept, columns if is_last else 0, False
         )
-    mom_received = lax.all_to_all(mom, "col", split_axis=0, concat_axis=0, tiled=True)
+    (mom_sent,) = made[-1]
+    mom_received = lax.all_to_all(mom_sent, "col", split_axis=0, concat_axis=0, tiled=True)
     moments, geometry, places, hot = call(
         functools.partial(geometry_kernel, slots),
         "contact_geometry",
         (
             shape(3, count),
             shape(len(contact_blocks(columns, slots)), 8, SUBS, LANES),
-            shape(2, 2, columns, slot_len, dtype=jnp.int32),
+            shape(2, 3, columns, slot_len, dtype=jnp.int32),
             shape(2 * columns, LANES, slot_len, dtype=BF16),
         ),
-        sent,
+        table,
+        listed,
         received,
         mom,
     )
@@ -522,8 +538,6 @@
         geometry,
         places,
         hot,
-        sent,
-        received,
         mom_received,
         scratch=[pltpu.VMEM((2, 9, columns, slot_len), F32)],
     )

time: 44 us -> 42.2 us (0.959)
  Pallas kernels: 21.8 us -> 18.7 us
  waiting for transfers between devices: 5.48 us -> 6.74 us
    pallas_call x9 -> x8, Pallas kernels: 21.8 us -> 18.7 us  [call(): pl.pallas_call(kernel, out_shape=outs, in_specs=specs or [VMEM] * len(arg...]
    all_to_all x1, waiting for transfers between devices: 3.13 us -> 4.19 us  [on_device(): lax.all_to_all(mom_sent, 'col', split_axis=0, concat_axis=0, tiled=True)]
  transfers between devices with their start and end apart: 6 -> 6, of which waited for: 3 -> 3; matrix products, arithmetic and copies ran while one was open for 0% -> 0% of each run, Pallas kernels for 42% -> 39%
where the time goes in v4:
time: 42.2 us; the launch traced here: 41.7 us
  Pallas kernels  18.7 us (44%)
  starting transfers between devices  15.6 us (37%)
  waiting for transfers between devices  6.74 us (16%)
  between operations  0.69 us (2%)
    pallas_call x8, Pallas kernels, call(): pl.pallas_call(kernel, out_shape=outs, in_specs=specs or [VMEM] * len(arg...  18.7 us
    all_to_all x1, starting transfers between devices, on_device(): lax.all_to_all(sent, 'col', split_axis=0, concat_axis=0, tiled=True)  6.83 us
    all_to_all x1, starting transfers between devices, on_device(): lax.all_to_all(mom_sent, 'col', split_axis=0, concat_axis=0, tiled=True)  6 us
    all_to_all x1, waiting for transfers between devices, on_device(): lax.all_to_all(mom_sent, 'col', split_axis=0, concat_axis=0, tiled=True)  4.19 us
    ppermute x4, starting transfers between devices, exchange(): arrived = lax.ppermute(held, axis, [(i, i ^ 1 << k) for i in range(size)])  2.75 us
    ppermute x4, waiting for transfers between devices, exchange(): arrived = lax.ppermute(held, axis, [(i, i ^ 1 << k) for i in range(size)])  2.55 us
  transfers between devices with their start and end apart: 6, of which 3 were waited for; matrix products, arithmetic and copies ran while one was open for 0% of the time, Pallas kernels for 39%

profile of v4, /device:TPU:0, one launch (start us, length us, event | category | flops | bytes accessed | tf_op | source)
XLA Modules:
  0.0 41.7 jit_solution(7625309734115457914)
XLA Ops:
  0.6 0.8 %row_pack.1.refs_4_.refs_0_ = f32[64,128]{1,0:T(8,128)S(1)} custom-call(f32[3,1024]{1,0:T(4,128)} %refs_0_.2, f32[3,1024]{1,0:T(4,128)} %refs_1_.1, f32[1,1024]{1,0:T(1,128)} %bitcast.15), custom_call_target="tpu_custom_call" | custom-call | tf_op jit(solution)/shard_map/row_pack/pallas_call | solution.py:393
  1.4 0.5 %collective-permute-start = (f32[1,64,128]{2,1,0:T(8,128)S(1)}, f32[1,64,128]{2,1,0:T(8,128)S(1)}, u32[]{:S(2)}, u32[]{:S(2)}) collective-permute-start(f32[1,64,128]{2,1,0:T(8,128)S(1)} %bitcast.6), channel_id=1, source_target_pairs={{0,8},{8,0},{16,24},{24,16},{1,9},{9,1},{17,25},{25,17},{2,10},{10... | collective-permute-start | bytes 98312 | tf_op jit(solution)/shard_map/ppermute | solution.py:414
  1.9 1.6 %column_pack.1 = (f32[8,64,128]{2,1,0:T(8,128)}, f32[48,128]{1,0:T(8,128)S(1)}, s32[9,8,128]{2,1,0:T(8,128)S(1)}) custom-call(f32[3,1024]{1,0:T(4,128)} %refs_0_.3, s32[8,512]{1,0:T(8,128)} %bitcast.13, s32[8,512]{1,0:T(8,128)} %bitcast.14, s32[1,8]{1,0:T(1,128)} %bitcast.16, f32[64,128]{1,0:T(8,128)S(1)} %row_pack.1.refs_4_.refs_0_), custom_call_target="tpu_custom_call" | custom-call | tf_op jit(solution)/shard_map/column_pack/pallas_call | solution.py:393
  3.5 0.0 collective-permute-done.refs_2_
  3.5 6.8 %all-to-all-start = ((f32[8,64,128]{2,1,0:T(8,128)}), f32[8,64,128]{2,1,0:T(8,128)S(1)}, u32[]{:S(2)}, u32[]{:S(2)}) async-start(f32[8,64,128]{2,1,0:T(8,128)} %get-tuple-element.22), calls=%async_computation | async-start | bytes 524288 | tf_op jit(solution)/shard_map/all_to_all | solution.py:507
  10.4 1.6 %collective-permute-start.1 = (f32[2,64,128]{2,1,0:T(8,128)S(1)}, f32[2,64,128]{2,1,0:T(8,128)S(1)}, u32[]{:S(2)}, u32[]{:S(2)}) collective-permute-start(f32[2,64,128]{2,1,0:T(8,128)S(1)} %pad_maximum_fusion), channel_id=1, source_target_pairs={{0,16},{8,24},{16,0},{24,8},{1,17},{9,25},{17,1},{25,9},{2,18},{10... | collective-permute-start | bytes 196616 | tf_op jit(solution)/shard_map/ppermute | solution.py:414
  12.0 3.7 %field_sums.4 = (f32[48,1024]{1,0:T(8,128)S(1)}, bf16[2048,1024]{1,0:T(8,128)(2,1)S(1)}, bf16[2048,1024]{1,0:T(8,128)(2,1)S(1)}) custom-call(f32[64,128]{1,0:T(8,128)S(1)} %row_pack.1.refs_4_.refs_0_, f32[1,64,128]{2,1,0:T(8,128)S(1)} %bitcast.8, f32[1,64,128]{2,1,0:T(8,128)S(1)} %collective-permute-done.refs_2_), custom_call_target="tpu_custom_call" | custom-call | tf_op jit(solution)/shard_map/field_sums/pallas_call | solution.py:393
  15.6 0.0 collective-permute-done.1.refs_1_
  15.6 3.7 %field_sums.5 = (f32[24,128]{1,0:T(8,128)S(1)}, bf16[2048,1024]{1,0:T(8,128)(2,1)S(1)}, bf16[2048,1024]{1,0:T(8,128)(2,1)S(1)}) custom-call(f32[64,128]{1,0:T(8,128)S(1)} %row_pack.1.refs_4_.refs_0_, f32[2,64,128]{2,1,0:T(8,128)S(1)} %collective-permute-done.1.refs_1_, f32[48,1024]{1,0:T(8,128)S(1)} %get-tuple-element.24.refs_2_), custom_call_target="tpu_custom_call" | custom-call | tf_op jit(solution)/shard_map/field_sums/pallas_call | solution.py:393
  19.3 0.1 collective-permute-start.2
  19.4 1.2 %collective-permute-done.2.refs_5_ = f32[1,24,128]{2,1,0:T(8,128)S(1)} collective-permute-done((f32[1,24,128]{2,1,0:T(8,128)S(1)}, f32[1,24,128]{2,1,0:T(8,128)S(1)}, u32[]{:S(2)}, u32[]{:S(2)}) %collective-permute-start.2) | collective-permute-done | bytes 12320 | tf_op jit(solution)/shard_map/ppermute | solution.py:414
  20.6 0.6 %collective-permute-start.3 = (f32[2,24,128]{2,1,0:T(8,128)S(1)}, f32[2,24,128]{2,1,0:T(8,128)S(1)}, u32[]{:S(2)}, u32[]{:S(2)}) collective-permute-start(f32[2,24,128]{2,1,0:T(8,128)S(1)} %pad_maximum_fusion.1), channel_id=1, source_target_pairs={{0,16},{8,24},{16,0},{24,8},{1,17},{9,25},{17,1},{25,9},{2,18},{10... | collective-permute-start | bytes 73736 | tf_op jit(solution)/shard_map/ppermute | solution.py:414
  21.2 1.9 %field_sums.6.refs_6_ = f32[48,1024]{1,0:T(8,128)S(1)} custom-call(f32[64,128]{1,0:T(8,128)S(1)} %row_pack.1.refs_4_.refs_0_, f32[1,64,128]{2,1,0:T(8,128)S(1)} %bitcast.9, f32[1,64,128]{2,1,0:T(8,128)S(1)} %collective-permute-done.refs_2_, f32[24,128]{1,0:T(8,128)S(1)} %get-tuple-element.25.refs_3_.refs_2_, f32[1,24,128]{2,1,0:T(8,128)S(1)} %bitcast.12, ...), custom_call_target="tpu_custom_call" | custom-call | tf_op jit(solution)/shard_map/field_sums/pallas_call | solution.py:393
  23.0 1.4 %collective-permute-done.3.refs_3_ = f32[2,24,128]{2,1,0:T(8,128)S(1)} collective-permute-done((f32[2,24,128]{2,1,0:T(8,128)S(1)}, f32[2,24,128]{2,1,0:T(8,128)S(1)}, u32[]{:S(2)}, u32[]{:S(2)}) %collective-permute-start.3) | collective-permute-done | bytes 24608 | tf_op jit(solution)/shard_map/ppermute | solution.py:414
  24.4 2.4 %field_sums.7 = (f32[24,128]{1,0:T(8,128)S(1)}, f32[8,24,128]{2,1,0:T(8,128)}) custom-call(f32[64,128]{1,0:T(8,128)S(1)} %row_pack.1.refs_4_.refs_0_, f32[2,64,128]{2,1,0:T(8,128)S(1)} %collective-permute-done.1.refs_1_, f32[24,128]{1,0:T(8,128)S(1)} %get-tuple-element.25.refs_3_.refs_2_, f32[2,24,128]{2,1,0:T(8,128)S(1)} %collective-permute-done.3.refs_3_, ...), custom_call_target="tpu_custom_call" | custom-call | tf_op jit(solution)/shard_map/field_sums/pallas_call | solution.py:393
  26.8 0.0 all-to-all-done.received
  26.8 6.0 %all-to-all-start.1 = ((f32[8,24,128]{2,1,0:T(8,128)}), f32[8,24,128]{2,1,0:T(8,128)S(1)}, u32[]{:S(2)}, u32[]{:S(2)}) async-start(f32[8,24,128]{2,1,0:T(8,128)} %get-tuple-element.35), calls=%async_computation.1 | async-start | bytes 196608 | tf_op jit(solution)/shard_map/all_to_all | solution.py:519
  32.8 2.9 %contact_geometry.1 = (f32[3,1024]{1,0:T(4,128)}, f32[8,8,8,128]{3,2,1,0:T(8,128)S(1)}, s32[2,3,8,512]{3,2,1,0:T(8,128)S(1)}, bf16[16,128,512]{2,1,0:T(8,128)(2,1)S(1)}) custom-call(f32[48,128]{1,0:T(8,128)S(1)} %get-tuple-element.19.table, s32[9,8,128]{2,1,0:T(8,128)S(1)} %get-tuple-element.20.listed, f32[8,64,128]{2,1,0:T(8,128)S(1)} %all-to-all-done.received, ...), custom_call_target="tpu_custom_call" | custom-call | tf_op jit(solution)/shard_map/contact_geometry/pallas_call | solution.py:393
  35.7 4.2 %all-to-all-done.1.mom_received = f32[8,24,128]{2,1,0:T(8,128)S(1)} async-done(((f32[8,24,128]{2,1,0:T(8,128)}), f32[8,24,128]{2,1,0:T(8,128)S(1)}, u32[]{:S(2)}, u32[]{:S(2)}) %all-to-all-start.1) | async-done | bytes 98336 | tf_op jit(solution)/shard_map/all_to_all | solution.py:519
  39.9 1.8 %contact_force.1 = f32[3,1024]{1,0:T(4,128)} custom-call(f32[8,8,8,128]{3,2,1,0:T(8,128)S(1)} %get-tuple-element.32.geometry, s32[2,3,8,512]{3,2,1,0:T(8,128)S(1)} %get-tuple-element.33.places, bf16[16,128,512]{2,1,0:T(8,128)(2,1)S(1)} %get-tuple-element.34.hot, f32[8,24,128]{2,1,0:T(8,128)S(1)} %all-to-all-done.1.mom_received), custom_call_target="tpu_custom_call" | custom-call | tf_op jit(solution)/shard_map/contact_force/pallas_call | solution.py:393
  (2 shorter events, 0.0 us)
Async XLA Ops:
  1.4 2.1 %collective-permute-start = (f32[1,64,128]{2,1,0:T(8,128)S(1)}, f32[1,64,128]{2,1,0:T(8,128)S(1)}, u32[]{:S(2)}, u32[]{:S(2)}) collective-permute-start(f32[1,64,128]{2,1,0:T(8,128)S(1)} %bitcast.6), channel_id=1, source_target_pairs={{0,8},{8,0},{16,24},{24,16},{1,9},{9,1},{17,25},{25,17},{2,10},{10... | collective-permute-start | bytes 98312 | tf_op jit(solution)/shard_map/ppermute | solution.py:414
  3.5 23.3 %all-to-all-start = ((f32[8,64,128]{2,1,0:T(8,128)}), f32[8,64,128]{2,1,0:T(8,128)S(1)}, u32[]{:S(2)}, u32[]{:S(2)}) async-start(f32[8,64,128]{2,1,0:T(8,128)} %get-tuple-element.22), calls=%async_computation | async-start | bytes 524288 | tf_op jit(solution)/shard_map/all_to_all | solution.py:507
  10.4 5.3 %collective-permute-start.1 = (f32[2,64,128]{2,1,0:T(8,128)S(1)}, f32[2,64,128]{2,1,0:T(8,128)S(1)}, u32[]{:S(2)}, u32[]{:S(2)}) collective-permute-start(f32[2,64,128]{2,1,0:T(8,128)S(1)} %pad_maximum_fusion), channel_id=1, source_target_pairs={{0,16},{8,24},{16,0},{24,8},{1,17},{9,25},{17,1},{25,9},{2,18},{10... | collective-permute-start | bytes 196616 | tf_op jit(solution)/shard_map/ppermute | solution.py:414
  19.3 1.2 %collective-permute-start.2 = (f32[1,24,128]{2,1,0:T(8,128)S(1)}, f32[1,24,128]{2,1,0:T(8,128)S(1)}, u32[]{:S(2)}, u32[]{:S(2)}) collective-permute-start(f32[1,24,128]{2,1,0:T(8,128)S(1)} %bitcast.10), channel_id=1, source_target_pairs={{0,8},{8,0},{16,24},{24,16},{1,9},{9,1},{17,25},{25,17},{2,10},{10... | collective-permute-start | bytes 36872 | tf_op jit(solution)/shard_map/ppermute | solution.py:414
  20.6 3.8 %collective-permute-start.3 = (f32[2,24,128]{2,1,0:T(8,128)S(1)}, f32[2,24,128]{2,1,0:T(8,128)S(1)}, u32[]{:S(2)}, u32[]{:S(2)}) collective-permute-start(f32[2,24,128]{2,1,0:T(8,128)S(1)} %pad_maximum_fusion.1), channel_id=1, source_target_pairs={{0,16},{8,24},{16,0},{24,8},{1,17},{9,25},{17,1},{25,9},{2,18},{10... | collective-permute-start | bytes 73736 | tf_op jit(solution)/shard_map/ppermute | solution.py:414
  26.8 13.1 %all-to-all-start.1 = ((f32[8,24,128]{2,1,0:T(8,128)}), f32[8,24,128]{2,1,0:T(8,128)S(1)}, u32[]{:S(2)}, u32[]{:S(2)}) async-start(f32[8,24,128]{2,1,0:T(8,128)} %get-tuple-element.35), calls=%async_computation.1 | async-start | bytes 196608 | tf_op jit(solution)/shard_map/all_to_all | solution.py:519

commit v5 on v4

--- a/solution.py
+++ b/solution.py
@@ -210,6 +210,21 @@
         copy.wait()
 
 
+def column_order(columns):
+    return [(k + columns // 2) % columns for k in range(columns)]
+
+
+def to_columns(blocks):
+    return lax.all_to_all(
+        blocks,
+        "col",
+        split_axis=0,
+        concat_axis=0,
+        axis_index_groups=[column_order(blocks.shape[0])],
+        tiled=True,
+    )
+
+
 def row_pack_kernel(*refs):
     inputs, payload, (pos, field, chi, done) = refs[0:3], refs[3], refs[4:]
     copy_in(inputs, (pos, field, chi), done)
@@ -242,12 +257,16 @@
             table[row : row + 1, :] = vel[c : c + 1, g * LANES : (g + 1) * LANES]
     for e in range(columns):
         send[e, 0 : 6 * groups, :] = table[...]
-        live = jnp.full((send.shape[1] - 6 * groups - 2 * slots, LANES), counts[0, e])
+        live = jnp.full(
+            (send.shape[1] - 6 * groups - 2 * slots, LANES), counts[0, column_order(columns)[e]]
+        )
         send[e, 6 * groups + 2 * slots :, :] = live.astype(F32)
         listed[2 * slots, e : e + 1, :] = live[0:1]
     for q in range(slots):
         lanes = slice(q * LANES, (q + 1) * LANES)
-        for k, index in enumerate((owner[:, lanes], partner[:, lanes])):
+        for k, ref in enumerate((owner, partner)):
+            half = columns // 2
+            index = jnp.concatenate([ref[half:, lanes], ref[:half, lanes]], axis=0)
             send[:, 6 * groups + k * slots + q, :] = index.astype(F32)
             listed[k * slots + q] = index
 
@@ -504,7 +523,7 @@
     rounds = exchange(payload, "row", row_size)
     first, sent = lax.optimization_barrier((rounds[0], sent))
     payloads = [[payload[None], first]] + [[r] for r in rounds[1:]]
-    received = lax.all_to_all(sent, "col", split_axis=0, concat_axis=0, tiled=True)
+    received = to_columns(sent)
     keep = 4 * row_size * count * count <= KEEP_BYTES
     mom, made = add_fields(payload, payloads, None, None, None, 0, keep)
     kept = [(0, m) for m in made] if keep else None
@@ -516,7 +535,7 @@
             payload, payloads, mom, moms, kept, columns if is_last else 0, False
         )
     (mom_sent,) = made[-1]
-    mom_received = lax.all_to_all(mom_sent, "col", split_axis=0, concat_axis=0, tiled=True)
+    mom_received = to_columns(mom_sent)
     moments, geometry, places, hot = call(
         functools.partial(geometry_kernel, slots),
         "contact_geometry",

time: 42.2 us -> 39.5 us (0.936)
  waiting for transfers between devices: 6.74 us -> 4.37 us
    all_to_all x2, waiting for transfers between devices: 4.19 us -> 1.83 us  [to_columns(): lax.all_to_all(blocks, 'col', split_axis=0, concat_axis=0, axis_index_gro...]
  transfers between devices with their start and end apart: 6 -> 6, of which waited for: 3 -> 3; matrix products, arithmetic and copies ran while one was open for 0% -> 0% of each run, Pallas kernels for 39% -> 41%
where the time goes in v5:
time: 39.5 us; the launch traced here: 39 us
  Pallas kernels  18.7 us (47%)
  starting transfers between devices  15.3 us (39%)
  waiting for transfers between devices  4.37 us (11%)
  between operations  0.69 us (2%)
    pallas_call x8, Pallas kernels, call(): pl.pallas_call(kernel, out_shape=outs, in_specs=specs or [VMEM] * len(arg...  18.7 us
    all_to_all x2, starting transfers between devices, to_columns(): lax.all_to_all(blocks, 'col', split_axis=0, concat_axis=0, axis_index_gro...  12.5 us
    ppermute x4, starting transfers between devices, exchange(): arrived = lax.ppermute(held, axis, [(i, i ^ 1 << k) for i in range(size)])  2.77 us
    ppermute x4, waiting for transfers between devices, exchange(): arrived = lax.ppermute(held, axis, [(i, i ^ 1 << k) for i in range(size)])  2.54 us
    all_to_all x2, waiting for transfers between devices, to_columns(): lax.all_to_all(blocks, 'col', split_axis=0, concat_axis=0, axis_index_gro...  1.83 us
  transfers between devices with their start and end apart: 6, of which 3 were waited for; matrix products, arithmetic and copies ran while one was open for 0% of the time, Pallas kernels for 41%

profile of v5, /device:TPU:0, one launch (start us, length us, event | category | flops | bytes accessed | tf_op | source)
XLA Modules:
  0.0 39.0 jit_solution(5788824584701870830)
XLA Ops:
  0.6 0.8 %row_pack.1.refs_4_.refs_0_ = f32[64,128]{1,0:T(8,128)S(1)} custom-call(f32[3,1024]{1,0:T(4,128)} %refs_0_.2, f32[3,1024]{1,0:T(4,128)} %refs_1_.1, f32[1,1024]{1,0:T(1,128)} %bitcast.15), custom_call_target="tpu_custom_call" | custom-call | tf_op jit(solution)/shard_map/row_pack/pallas_call | solution.py:412
  1.4 0.5 %collective-permute-start = (f32[1,64,128]{2,1,0:T(8,128)S(1)}, f32[1,64,128]{2,1,0:T(8,128)S(1)}, u32[]{:S(2)}, u32[]{:S(2)}) collective-permute-start(f32[1,64,128]{2,1,0:T(8,128)S(1)} %bitcast.6), channel_id=1, source_target_pairs={{0,8},{8,0},{16,24},{24,16},{1,9},{9,1},{17,25},{25,17},{2,10},{10... | collective-permute-start | bytes 98312 | tf_op jit(solution)/shard_map/ppermute | solution.py:433
  1.9 1.6 %column_pack.1 = (f32[8,64,128]{2,1,0:T(8,128)}, f32[48,128]{1,0:T(8,128)S(1)}, s32[9,8,128]{2,1,0:T(8,128)S(1)}) custom-call(f32[3,1024]{1,0:T(4,128)} %refs_0_.3, s32[8,512]{1,0:T(8,128)} %bitcast.13, s32[8,512]{1,0:T(8,128)} %bitcast.14, s32[1,8]{1,0:T(1,128)} %bitcast.16, f32[64,128]{1,0:T(8,128)S(1)} %row_pack.1.refs_4_.refs_0_), custom_call_target="tpu_custom_call" | custom-call | tf_op jit(solution)/shard_map/column_pack/pallas_call | solution.py:412
  3.5 0.0 collective-permute-done.refs_2_
  3.5 7.4 %all-to-all-start = ((f32[8,64,128]{2,1,0:T(8,128)}), f32[8,64,128]{2,1,0:T(8,128)S(1)}, u32[]{:S(2)}, u32[]{:S(2)}) async-start(f32[8,64,128]{2,1,0:T(8,128)} %get-tuple-element.22), calls=%async_computation | async-start | bytes 524288 | tf_op jit(solution)/shard_map/all_to_all | solution.py:218
  10.9 1.6 %collective-permute-start.1 = (f32[2,64,128]{2,1,0:T(8,128)S(1)}, f32[2,64,128]{2,1,0:T(8,128)S(1)}, u32[]{:S(2)}, u32[]{:S(2)}) collective-permute-start(f32[2,64,128]{2,1,0:T(8,128)S(1)} %pad_maximum_fusion), channel_id=1, source_target_pairs={{0,16},{8,24},{16,0},{24,8},{1,17},{9,25},{17,1},{25,9},{2,18},{10... | collective-permute-start | bytes 196616 | tf_op jit(solution)/shard_map/ppermute | solution.py:433
  12.5 3.7 %field_sums.4 = (f32[48,1024]{1,0:T(8,128)S(1)}, bf16[2048,1024]{1,0:T(8,128)(2,1)S(1)}, bf16[2048,1024]{1,0:T(8,128)(2,1)S(1)}) custom-call(f32[64,128]{1,0:T(8,128)S(1)} %row_pack.1.refs_4_.refs_0_, f32[1,64,128]{2,1,0:T(8,128)S(1)} %bitcast.8, f32[1,64,128]{2,1,0:T(8,128)S(1)} %collective-permute-done.refs_2_), custom_call_target="tpu_custom_call" | custom-call | tf_op jit(solution)/shard_map/field_sums/pallas_call | solution.py:412
  16.2 0.0 collective-permute-done.1.refs_1_
  16.2 3.7 %field_sums.5 = (f32[24,128]{1,0:T(8,128)S(1)}, bf16[2048,1024]{1,0:T(8,128)(2,1)S(1)}, bf16[2048,1024]{1,0:T(8,128)(2,1)S(1)}) custom-call(f32[64,128]{1,0:T(8,128)S(1)} %row_pack.1.refs_4_.refs_0_, f32[2,64,128]{2,1,0:T(8,128)S(1)} %collective-permute-done.1.refs_1_, f32[48,1024]{1,0:T(8,128)S(1)} %get-tuple-element.24.refs_2_), custom_call_target="tpu_custom_call" | custom-call | tf_op jit(solution)/shard_map/field_sums/pallas_call | solution.py:412
  19.9 0.1 collective-permute-start.2
  20.0 1.2 %collective-permute-done.2.refs_5_ = f32[1,24,128]{2,1,0:T(8,128)S(1)} collective-permute-done((f32[1,24,128]{2,1,0:T(8,128)S(1)}, f32[1,24,128]{2,1,0:T(8,128)S(1)}, u32[]{:S(2)}, u32[]{:S(2)}) %collective-permute-start.2) | collective-permute-done | bytes 12320 | tf_op jit(solution)/shard_map/ppermute | solution.py:433
  21.1 0.6 %collective-permute-start.3 = (f32[2,24,128]{2,1,0:T(8,128)S(1)}, f32[2,24,128]{2,1,0:T(8,128)S(1)}, u32[]{:S(2)}, u32[]{:S(2)}) collective-permute-start(f32[2,24,128]{2,1,0:T(8,128)S(1)} %pad_maximum_fusion.1), channel_id=1, source_target_pairs={{0,16},{8,24},{16,0},{24,8},{1,17},{9,25},{17,1},{25,9},{2,18},{10... | collective-permute-start | bytes 73736 | tf_op jit(solution)/shard_map/ppermute | solution.py:433
  21.7 1.9 %field_sums.6.refs_6_ = f32[48,1024]{1,0:T(8,128)S(1)} custom-call(f32[64,128]{1,0:T(8,128)S(1)} %row_pack.1.refs_4_.refs_0_, f32[1,64,128]{2,1,0:T(8,128)S(1)} %bitcast.9, f32[1,64,128]{2,1,0:T(8,128)S(1)} %collective-permute-done.refs_2_, f32[24,128]{1,0:T(8,128)S(1)} %get-tuple-element.25.refs_3_.refs_2_, f32[1,24,128]{2,1,0:T(8,128)S(1)} %bitcast.12, ...), custom_call_target="tpu_custom_call" | custom-call | tf_op jit(solution)/shard_map/field_sums/pallas_call | solution.py:412
  23.6 1.4 %collective-permute-done.3.refs_3_ = f32[2,24,128]{2,1,0:T(8,128)S(1)} collective-permute-done((f32[2,24,128]{2,1,0:T(8,128)S(1)}, f32[2,24,128]{2,1,0:T(8,128)S(1)}, u32[]{:S(2)}, u32[]{:S(2)}) %collective-permute-start.3) | collective-permute-done | bytes 24608 | tf_op jit(solution)/shard_map/ppermute | solution.py:433
  25.0 2.4 %field_sums.7 = (f32[24,128]{1,0:T(8,128)S(1)}, f32[8,24,128]{2,1,0:T(8,128)}) custom-call(f32[64,128]{1,0:T(8,128)S(1)} %row_pack.1.refs_4_.refs_0_, f32[2,64,128]{2,1,0:T(8,128)S(1)} %collective-permute-done.1.refs_1_, f32[24,128]{1,0:T(8,128)S(1)} %get-tuple-element.25.refs_3_.refs_2_, f32[2,24,128]{2,1,0:T(8,128)S(1)} %collective-permute-done.3.refs_3_, ...), custom_call_target="tpu_custom_call" | custom-call | tf_op jit(solution)/shard_map/field_sums/pallas_call | solution.py:412
  27.4 0.0 all-to-all-done.received
  27.4 5.1 %all-to-all-start.1 = ((f32[8,24,128]{2,1,0:T(8,128)}), f32[8,24,128]{2,1,0:T(8,128)S(1)}, u32[]{:S(2)}, u32[]{:S(2)}) async-start(f32[8,24,128]{2,1,0:T(8,128)} %get-tuple-element.35), calls=%async_computation.1 | async-start | bytes 196608 | tf_op jit(solution)/shard_map/all_to_all | solution.py:218
  32.5 2.9 %contact_geometry.1 = (f32[3,1024]{1,0:T(4,128)}, f32[8,8,8,128]{3,2,1,0:T(8,128)S(1)}, s32[2,3,8,512]{3,2,1,0:T(8,128)S(1)}, bf16[16,128,512]{2,1,0:T(8,128)(2,1)S(1)}) custom-call(f32[48,128]{1,0:T(8,128)S(1)} %get-tuple-element.19.table, s32[9,8,128]{2,1,0:T(8,128)S(1)} %get-tuple-element.20.listed, f32[8,64,128]{2,1,0:T(8,128)S(1)} %all-to-all-done.received, ...), custom_call_target="tpu_custom_call" | custom-call | tf_op jit(solution)/shard_map/contact_geometry/pallas_call | solution.py:412
  35.4 1.8 %all-to-all-done.1.mom_received = f32[8,24,128]{2,1,0:T(8,128)S(1)} async-done(((f32[8,24,128]{2,1,0:T(8,128)}), f32[8,24,128]{2,1,0:T(8,128)S(1)}, u32[]{:S(2)}, u32[]{:S(2)}) %all-to-all-start.1) | async-done | bytes 98336 | tf_op jit(solution)/shard_map/all_to_all | solution.py:218
  37.2 1.8 %contact_force.1 = f32[3,1024]{1,0:T(4,128)} custom-call(f32[8,8,8,128]{3,2,1,0:T(8,128)S(1)} %get-tuple-element.32.geometry, s32[2,3,8,512]{3,2,1,0:T(8,128)S(1)} %get-tuple-element.33.places, bf16[16,128,512]{2,1,0:T(8,128)(2,1)S(1)} %get-tuple-element.34.hot, f32[8,24,128]{2,1,0:T(8,128)S(1)} %all-to-all-done.1.mom_received), custom_call_target="tpu_custom_call" | custom-call | tf_op jit(solution)/shard_map/contact_force/pallas_call | solution.py:412
  (2 shorter events, 0.0 us)
Async XLA Ops:
  1.4 2.1 %collective-permute-start = (f32[1,64,128]{2,1,0:T(8,128)S(1)}, f32[1,64,128]{2,1,0:T(8,128)S(1)}, u32[]{:S(2)}, u32[]{:S(2)}) collective-permute-start(f32[1,64,128]{2,1,0:T(8,128)S(1)} %bitcast.6), channel_id=1, source_target_pairs={{0,8},{8,0},{16,24},{24,16},{1,9},{9,1},{17,25},{25,17},{2,10},{10... | collective-permute-start | bytes 98312 | tf_op jit(solution)/shard_map/ppermute | solution.py:433
  3.5 23.8 %all-to-all-start = ((f32[8,64,128]{2,1,0:T(8,128)}), f32[8,64,128]{2,1,0:T(8,128)S(1)}, u32[]{:S(2)}, u32[]{:S(2)}) async-start(f32[8,64,128]{2,1,0:T(8,128)} %get-tuple-element.22), calls=%async_computation | async-start | bytes 524288 | tf_op jit(solution)/shard_map/all_to_all | solution.py:218
  10.9 5.3 %collective-permute-start.1 = (f32[2,64,128]{2,1,0:T(8,128)S(1)}, f32[2,64,128]{2,1,0:T(8,128)S(1)}, u32[]{:S(2)}, u32[]{:S(2)}) collective-permute-start(f32[2,64,128]{2,1,0:T(8,128)S(1)} %pad_maximum_fusion), channel_id=1, source_target_pairs={{0,16},{8,24},{16,0},{24,8},{1,17},{9,25},{17,1},{25,9},{2,18},{10... | collective-permute-start | bytes 196616 | tf_op jit(solution)/shard_map/ppermute | solution.py:433
  19.9 1.2 %collective-permute-start.2 = (f32[1,24,128]{2,1,0:T(8,128)S(1)}, f32[1,24,128]{2,1,0:T(8,128)S(1)}, u32[]{:S(2)}, u32[]{:S(2)}) collective-permute-start(f32[1,24,128]{2,1,0:T(8,128)S(1)} %bitcast.10), channel_id=1, source_target_pairs={{0,8},{8,0},{16,24},{24,16},{1,9},{9,1},{17,25},{25,17},{2,10},{10... | collective-permute-start | bytes 36872 | tf_op jit(solution)/shard_map/ppermute | solution.py:433
  21.1 3.8 %collective-permute-start.3 = (f32[2,24,128]{2,1,0:T(8,128)S(1)}, f32[2,24,128]{2,1,0:T(8,128)S(1)}, u32[]{:S(2)}, u32[]{:S(2)}) collective-permute-start(f32[2,24,128]{2,1,0:T(8,128)S(1)} %pad_maximum_fusion.1), channel_id=1, source_target_pairs={{0,16},{8,24},{16,0},{24,8},{1,17},{9,25},{17,1},{25,9},{2,18},{10... | collective-permute-start | bytes 73736 | tf_op jit(solution)/shard_map/ppermute | solution.py:433
  27.4 9.9 %all-to-all-start.1 = ((f32[8,24,128]{2,1,0:T(8,128)}), f32[8,24,128]{2,1,0:T(8,128)S(1)}, u32[]{:S(2)}, u32[]{:S(2)}) async-start(f32[8,24,128]{2,1,0:T(8,128)} %get-tuple-element.35), calls=%async_computation.1 | async-start | bytes 196608 | tf_op jit(solution)/shard_map/all_to_all | solution.py:218

commit v6 on v5

--- a/solution.py
+++ b/solution.py
@@ -116,16 +116,18 @@
     return [p - c for p, c in zip(pos, center)]
 
 
-def field_kernel(sources, with_mom, kept_at, has_before, is_last, columns, *refs):
+def field_kernel(sources, picks, with_mom, has_kept, has_before, is_last, columns, *refs):
     refs = list(refs)
     own = refs.pop(0)
     blocks = [ref.at[k] for ref in refs[:sources] for k in range(ref.shape[0])]
+    blocks = [blocks[k] for k in picks]
     refs = refs[sources:]
     if with_mom:
         own_mom = refs.pop(0)
-        mom_blocks = [ref.at[k] for ref in refs[:sources] for k in range(ref.shape[0])]
-        refs = refs[sources:]
-    has_kept = kept_at is not None
+        mom_blocks = []
+        while len(mom_blocks) < len(picks):
+            mom_blocks += [refs[0].at[k] for k in range(refs[0].shape[0])]
+            refs.pop(0)
     kept = (refs.pop(0), refs.pop(0)) if has_kept else None
     before = refs.pop(0) if has_before else None
     outs, (held, target, feats, sums) = refs[:-4], refs[-4:]
@@ -171,7 +173,8 @@
 
     if has_kept:
         for a, b in tiles:
-            rows = slice(kept_at + a.start, kept_at + a.stop)
+            k, at = divmod(a.start, count)
+            rows = slice(picks[k] * count + at, picks[k] * count + at + height)
             add((a, b), kept[0][rows, b], kept[1][rows, b])
     else:
         radius_sq, ready = radius_of(tiles[0]), None
@@ -360,10 +363,12 @@
     for kind in range(2):
         for e in range(columns):
             here = places[kind, 1, e : e + 1, :] == lane_of
-            hot[kind * columns + e] = jnp.where(here, 1.0, 0.0).astype(BF16)
-
-
-def force_kernel(slots, geometry, places, hot, mom_received, forces, pieces):
+            width = slots * LANES
+            first = (kind * columns + e) * width
+            hot[:, first : first + width] = jnp.where(here, 1.0, 0.0).astype(BF16)
+
+
+def force_kernel(slots, geometry, places, hot, mom_received, forces, pieces, values):
     columns = mom_received.shape[0]
     groups = mom_received.shape[1] // 3
     for at, (kind, rows, q) in enumerate(contact_blocks(columns, slots)):
@@ -384,21 +389,18 @@
             force = 3.0 * (along_own * their[c] + along_their * own[c]) + radial * normal[c]
             for k, piece in enumerate(split3(force)):
                 pieces[kind, k * 3 + c, rows, lanes] = piece
-    row_of = lax.broadcasted_iota(jnp.int32, (groups, slots * LANES), 0)
-    total = None
+    width = slots * LANES
+    row_of = lax.broadcasted_iota(jnp.int32, (groups, width), 0)
     for kind in range(2):
         for e in range(columns):
             here = places[kind, 0, e : e + 1, :] == row_of
-            values = jnp.concatenate(
+            first = (kind * columns + e) * width
+            values[:, first : first + width] = jnp.concatenate(
                 [jnp.where(here, pieces[kind, k, e : e + 1, :], 0.0) for k in range(9)], axis=0
             ).astype(BF16)
-            summed = lax.dot_general(
-                values,
-                hot[kind * columns + e],
-                (((1,), (1,)), ((), ())),
-                preferred_element_type=F32,
-            )
-            total = summed if total is None else total + summed
+    total = lax.dot_general(
+        values[...], hot[...], (((1,), (1,)), ((), ())), preferred_element_type=F32
+    )
     height = 3 * groups
     total = total[0:height] + total[height : 2 * height] + total[2 * height : 3 * height]
     for c in range(3):
@@ -424,31 +426,36 @@
     return jax.ShapeDtypeStruct(dims, dtype)
 
 
-def exchange(block, axis, size):
-    if size & (size - 1):
-        every = lambda k: lax.ppermute(block, axis, [(i, (i + k) % size) for i in range(size)])
-        return [every(k)[None] for k in range(1, size)]
+def flip(blocks, axis, size, bit):
+    return lax.ppermute(blocks, axis, [(i, i ^ (1 << bit)) for i in range(size)])
+
+
+def others(block, axis, size):
+    return [lax.ppermute(block, axis, [(i, (i + k) % size) for i in range(size)])[None] for k in range(1, size)]
+
+
+def exchange(block, axis, size, first=0):
     held, rounds = block[None], []
-    for k in range(size.bit_length() - 1):
-        arrived = lax.ppermute(held, axis, [(i, i ^ (1 << k)) for i in range(size)])
-        rounds.append(arrived)
-        if k + 2 < size.bit_length():
-            held = jnp.concatenate([held, arrived], axis=0)
+    for bit in range(first, size.bit_length() - 1):
+        rounds.append(flip(held, axis, size, bit))
+        if bit + 2 < size.bit_length():
+            held = jnp.concatenate([held, rounds[-1]], axis=0)
     return rounds
 
 
-def add_fields(payload, payloads, mom, moms, kept, columns, keep):
+def add_fields(payload, parts, mom, columns, keep):
     count = payload.shape[0] // SUBS * LANES
     groups = count // LANES
     sums, made = None, []
-    for k, sources in enumerate(payloads):
-        is_last = k == len(payloads) - 1
-        length = sum(a.shape[0] for a in sources) * count
+    for at, (sources, picks, moms, kept) in enumerate(parts):
+        is_last = at == len(parts) - 1
+        length = len(picks) * count
         args = [payload, *sources]
+        if callable(moms):
+            moms, sums = moms(sums)
         if mom is not None:
-            args += [mom, *moms[k]]
-        if kept:
-            args += kept[k][1]
+            args += [mom, *moms]
+        args += kept
         if sums is not None:
             args.append(sums)
         if not is_last:
@@ -462,8 +469,9 @@
             functools.partial(
                 field_kernel,
                 len(sources),
+                picks,
                 mom is not None,
-                kept[k][0] if kept else None,
+                bool(kept),
                 sums is not None,
                 is_last,
                 columns,
@@ -520,20 +528,39 @@
         scratch=[pltpu.VMEM(v.shape, v.dtype) for v in inputs[:-1]]
         + [pltpu.SMEM((1, columns), jnp.int32), pltpu.SemaphoreType.DMA((4,))],
     )
-    rounds = exchange(payload, "row", row_size)
-    first, sent = lax.optimization_barrier((rounds[0], sent))
-    payloads = [[payload[None], first]] + [[r] for r in rounds[1:]]
+    paired = row_size > 1 and row_size & (row_size - 1) == 0
+    rounds = (exchange if paired else others)(payload, "row", row_size)
+    if rounds:
+        first, sent = lax.optimization_barrier((rounds[0], sent))
+        rounds = [first] + rounds[1:]
     received = to_columns(sent)
     keep = 4 * row_size * count * count <= KEEP_BYTES
-    mom, made = add_fields(payload, payloads, None, None, None, 0, keep)
-    kept = [(0, m) for m in made] if keep else None
+    sources = [[payload[None]] + rounds[:1]] + [[r] for r in rounds[1:]]
+    sizes = [sum(a.shape[0] for a in arrays) for arrays in sources]
+    parts = [(a, tuple(range(n)), [], []) for a, n in zip(sources, sizes)]
+    mom, kept = add_fields(payload, parts, None, 0, keep)
     for iteration in range(1, ITERS):
         is_last = iteration == ITERS - 1
-        arrived = exchange(mom, "row", row_size)
-        moms = [[mom[None], arrived[0]]] + [[r] for r in arrived[1:]]
-        mom, made = add_fields(
-            payload, payloads, mom, moms, kept, columns if is_last else 0, False
-        )
+        if paired:
+            far = exchange(mom, "row", row_size, 1)
+            moms = [[mom[None], flip(mom[None], "row", row_size, 0)]]
+            parts = [(sources[0], (0, 1), moms[0], kept[0])]
+            for k, direct in enumerate(far):
+                evens, odds = tuple(range(0, sizes[k + 1], 2)), tuple(range(1, sizes[k + 1], 2))
+                passed = []
+
+                def handed_on(sums, direct=direct, passed=passed):
+                    direct, sums = lax.optimization_barrier((direct, sums))
+                    passed.append(flip(direct, "row", row_size, 0))
+                    return [direct], sums
+
+                parts.append((sources[k + 1], evens, handed_on, kept[k + 1]))
+                parts.append((sources[k + 1], odds, lambda sums, p=passed: (p, sums), kept[k + 1]))
+        else:
+            moms = [[mom[None]] + others(mom, "row", row_size)[:1]]
+            moms += [[r] for r in others(mom, "row", row_size)[1:]]
+            parts = [(a, tuple(range(n)), m, k) for a, n, m, k in zip(sources, sizes, moms, kept)]
+        mom, made = add_fields(payload, parts, mom, columns if is_last else 0, False)
     (mom_sent,) = made[-1]
     mom_received = to_columns(mom_sent)
     moments, geometry, places, hot = call(
@@ -543,7 +570,7 @@
             shape(3, count),
             shape(len(contact_blocks(columns, slots)), 8, SUBS, LANES),
             shape(2, 3, columns, slot_len, dtype=jnp.int32),
-            shape(2 * columns, LANES, slot_len, dtype=BF16),
+            shape(LANES, 2 * columns * slot_len, dtype=BF16),
         ),
         table,
         listed,
@@ -558,7 +585,10 @@
         places,
         hot,
         mom_received,
-        scratch=[pltpu.VMEM((2, 9, columns, slot_len), F32)],
+        scratch=[
+            pltpu.VMEM((2, 9, columns, slot_len), F32),
+            pltpu.VMEM((9 * groups, 2 * columns * slot_len), BF16),
+        ],
     )
     return (moments, forces)
 

time: 39.5 us -> 38.6 us (0.977)
  waiting for transfers between devices: 4.37 us -> 3.17 us
    ppermute x4 -> x5, waiting for transfers between devices: 2.54 us -> 1.35 us  [flip(): return lax.ppermute(blocks, axis, [(i, i ^ 1 << bit) for i in range(size)])]
    pallas_call x8 -> x9, Pallas kernels: 18.7 us -> 19 us  [call(): pl.pallas_call(kernel, out_shape=outs, in_specs=specs or [VMEM] * len(arg...]
    ppermute x4 -> x5, starting transfers between devices: 2.77 us -> 2.83 us  [flip(): return lax.ppermute(blocks, axis, [(i, i ^ 1 << bit) for i in range(size)])]
  transfers between devices with their start and end apart: 6 -> 7, of which waited for: 3 -> 4; matrix products, arithmetic and copies ran while one was open for 0% -> 0% of each run, Pallas kernels for 41% -> 43%
where the time goes in v6:
time: 38.6 us; the launch traced here: 38.2 us
  Pallas kernels  19 us (49%)
  starting transfers between devices  15.3 us (40%)
  waiting for transfers between devices  3.17 us (8%)
  between operations  0.7 us (2%)
    pallas_call x9, Pallas kernels, call(): pl.pallas_call(kernel, out_shape=outs, in_specs=specs or [VMEM] * len(arg...  19 us
    all_to_all x2, starting transfers between devices, to_columns(): lax.all_to_all(blocks, 'col', split_axis=0, concat_axis=0, axis_index_gro...  12.5 us
    ppermute x5, starting transfers between devices, flip(): return lax.ppermute(blocks, axis, [(i, i ^ 1 << bit) for i in range(size)])  2.83 us
    all_to_all x2, waiting for transfers between devices, to_columns(): lax.all_to_all(blocks, 'col', split_axis=0, concat_axis=0, axis_index_gro...  1.83 us
    ppermute x5, waiting for transfers between devices, flip(): return lax.ppermute(blocks, axis, [(i, i ^ 1 << bit) for i in range(size)])  1.35 us
  transfers between devices with their start and end apart: 7, of which 4 were waited for; matrix products, arithmetic and copies ran while one was open for 0% of the time, Pallas kernels for 43%

profile of v6, /device:TPU:0, one launch (start us, length us, event | category | flops | bytes accessed | tf_op | source)
XLA Modules:
  0.0 38.2 jit_solution(13900335021058458327)
XLA Ops:
  0.6 0.8 %row_pack.1.refs_4_.refs_0_ = f32[64,128]{1,0:T(8,128)S(1)} custom-call(f32[3,1024]{1,0:T(4,128)} %refs_0_.2, f32[3,1024]{1,0:T(4,128)} %refs_1_.1, f32[1,1024]{1,0:T(1,128)} %bitcast.15), custom_call_target="tpu_custom_call" | custom-call | tf_op jit(solution)/shard_map/row_pack/pallas_call | solution.py:414
  1.4 0.5 %collective-permute-start = (f32[1,64,128]{2,1,0:T(8,128)S(1)}, f32[1,64,128]{2,1,0:T(8,128)S(1)}, u32[]{:S(2)}, u32[]{:S(2)}) collective-permute-start(f32[1,64,128]{2,1,0:T(8,128)S(1)} %bitcast.6), channel_id=1, source_target_pairs={{0,8},{8,0},{16,24},{24,16},{1,9},{9,1},{17,25},{25,17},{2,10},{10... | collective-permute-start | bytes 98312 | tf_op jit(solution)/shard_map/ppermute | solution.py:430
  1.9 1.6 %column_pack.1 = (f32[8,64,128]{2,1,0:T(8,128)}, f32[48,128]{1,0:T(8,128)S(1)}, s32[9,8,128]{2,1,0:T(8,128)S(1)}) custom-call(f32[3,1024]{1,0:T(4,128)} %refs_0_.3, s32[8,512]{1,0:T(8,128)} %bitcast.13, s32[8,512]{1,0:T(8,128)} %bitcast.14, s32[1,8]{1,0:T(1,128)} %bitcast.16, f32[64,128]{1,0:T(8,128)S(1)} %row_pack.1.refs_4_.refs_0_), custom_call_target="tpu_custom_call" | custom-call | tf_op jit(solution)/shard_map/column_pack/pallas_call | solution.py:414
  3.5 0.0 collective-permute-done.refs_2_
  3.5 7.4 %all-to-all-start = ((f32[8,64,128]{2,1,0:T(8,128)}), f32[8,64,128]{2,1,0:T(8,128)S(1)}, u32[]{:S(2)}, u32[]{:S(2)}) async-start(f32[8,64,128]{2,1,0:T(8,128)} %get-tuple-element.24), calls=%async_computation | async-start | bytes 524288 | tf_op jit(solution)/shard_map/all_to_all | solution.py:221
  10.9 1.6 %collective-permute-start.1 = (f32[2,64,128]{2,1,0:T(8,128)S(1)}, f32[2,64,128]{2,1,0:T(8,128)S(1)}, u32[]{:S(2)}, u32[]{:S(2)}) collective-permute-start(f32[2,64,128]{2,1,0:T(8,128)S(1)} %pad_maximum_fusion), channel_id=1, source_target_pairs={{0,16},{8,24},{16,0},{24,8},{1,17},{9,25},{17,1},{25,9},{2,18},{10... | collective-permute-start | bytes 196616 | tf_op jit(solution)/shard_map/ppermute | solution.py:430
  12.5 3.7 %field_sums.5 = (f32[48,1024]{1,0:T(8,128)S(1)}, bf16[2048,1024]{1,0:T(8,128)(2,1)S(1)}, bf16[2048,1024]{1,0:T(8,128)(2,1)S(1)}) custom-call(f32[64,128]{1,0:T(8,128)S(1)} %row_pack.1.refs_4_.refs_0_, f32[1,64,128]{2,1,0:T(8,128)S(1)} %bitcast.8, f32[1,64,128]{2,1,0:T(8,128)S(1)} %collective-permute-done.refs_2_), custom_call_target="tpu_custom_call" | custom-call | tf_op jit(solution)/shard_map/field_sums/pallas_call | solution.py:414
  16.2 0.0 collective-permute-done.1.refs_1_
  16.2 3.7 %field_sums.6 = (f32[24,128]{1,0:T(8,128)S(1)}, bf16[2048,1024]{1,0:T(8,128)(2,1)S(1)}, bf16[2048,1024]{1,0:T(8,128)(2,1)S(1)}) custom-call(f32[64,128]{1,0:T(8,128)S(1)} %row_pack.1.refs_4_.refs_0_, f32[2,64,128]{2,1,0:T(8,128)S(1)} %collective-permute-done.1.refs_1_, f32[48,1024]{1,0:T(8,128)S(1)} %get-tuple-element.26.refs_2_), custom_call_target="tpu_custom_call" | custom-call | tf_op jit(solution)/shard_map/field_sums/pallas_call | solution.py:414
  19.9 0.1 collective-permute-start.3
  20.0 0.7 %collective-permute-start.2 = (f32[1,24,128]{2,1,0:T(8,128)S(1)}, f32[1,24,128]{2,1,0:T(8,128)S(1)}, u32[]{:S(2)}, u32[]{:S(2)}) collective-permute-start(f32[1,24,128]{2,1,0:T(8,128)S(1)} %bitcast.11), channel_id=1, source_target_pairs={{0,16},{8,24},{16,0},{24,8},{1,17},{9,25},{17,1},{25,9},{2,18},{10... | collective-permute-start | bytes 36872 | tf_op jit(solution)/shard_map/ppermute | solution.py:430
  20.6 0.5 %collective-permute-done.3.refs_5_ = f32[1,24,128]{2,1,0:T(8,128)S(1)} collective-permute-done((f32[1,24,128]{2,1,0:T(8,128)S(1)}, f32[1,24,128]{2,1,0:T(8,128)S(1)}, u32[]{:S(2)}, u32[]{:S(2)}) %collective-permute-start.3) | collective-permute-done | bytes 12320 | tf_op jit(solution)/shard_map/ppermute | solution.py:430
  21.1 1.9 %field_sums.7.refs_6_ = f32[48,1024]{1,0:T(8,128)S(1)} custom-call(f32[64,128]{1,0:T(8,128)S(1)} %row_pack.1.refs_4_.refs_0_, f32[1,64,128]{2,1,0:T(8,128)S(1)} %bitcast.9, f32[1,64,128]{2,1,0:T(8,128)S(1)} %collective-permute-done.refs_2_, f32[24,128]{1,0:T(8,128)S(1)} %get-tuple-element.27.refs_3_.refs_2_, f32[1,24,128]{2,1,0:T(8,128)S(1)} %bitcast.12, ...), custom_call_target="tpu_custom_call" | custom-call | tf_op jit(solution)/shard_map/field_sums/pallas_call | solution.py:414
  23.0 0.7 %collective-permute-done.2.refs_3_ = f32[1,24,128]{2,1,0:T(8,128)S(1)} collective-permute-done((f32[1,24,128]{2,1,0:T(8,128)S(1)}, f32[1,24,128]{2,1,0:T(8,128)S(1)}, u32[]{:S(2)}, u32[]{:S(2)}) %collective-permute-start.2) | collective-permute-done | bytes 12320 | tf_op jit(solution)/shard_map/ppermute | solution.py:430
  23.7 0.0 collective-permute-start.4
  23.7 1.1 %field_sums.8.refs_6_ = f32[48,1024]{1,0:T(8,128)S(1)} custom-call(f32[64,128]{1,0:T(8,128)S(1)} %row_pack.1.refs_4_.refs_0_, f32[2,64,128]{2,1,0:T(8,128)S(1)} %collective-permute-done.1.refs_1_, f32[24,128]{1,0:T(8,128)S(1)} %get-tuple-element.27.refs_3_.refs_2_, f32[1,24,128]{2,1,0:T(8,128)S(1)} %collective-permute-done.2.refs_3_, ...), custom_call_target="tpu_custom_call" | custom-call | tf_op jit(solution)/shard_map/field_sums/pallas_call | solution.py:414
  24.8 0.1 collective-permute-done.4.refs_3_
  24.9 1.7 %field_sums.9 = (f32[24,128]{1,0:T(8,128)S(1)}, f32[8,24,128]{2,1,0:T(8,128)}) custom-call(f32[64,128]{1,0:T(8,128)S(1)} %row_pack.1.refs_4_.refs_0_, f32[2,64,128]{2,1,0:T(8,128)S(1)} %collective-permute-done.1.refs_1_, f32[24,128]{1,0:T(8,128)S(1)} %get-tuple-element.27.refs_3_.refs_2_, f32[1,24,128]{2,1,0:T(8,128)S(1)} %collective-permute-done.4.refs_3_, ...), custom_call_target="tpu_custom_call" | custom-call | tf_op jit(solution)/shard_map/field_sums/pallas_call | solution.py:414
  26.6 0.0 all-to-all-done.received
  26.6 5.1 %all-to-all-start.1 = ((f32[8,24,128]{2,1,0:T(8,128)}), f32[8,24,128]{2,1,0:T(8,128)S(1)}, u32[]{:S(2)}, u32[]{:S(2)}) async-start(f32[8,24,128]{2,1,0:T(8,128)} %get-tuple-element.39), calls=%async_computation.1 | async-start | bytes 196608 | tf_op jit(solution)/shard_map/all_to_all | solution.py:221
  31.7 2.9 %contact_geometry.1 = (f32[3,1024]{1,0:T(4,128)}, f32[8,8,8,128]{3,2,1,0:T(8,128)S(1)}, s32[2,3,8,512]{3,2,1,0:T(8,128)S(1)}, bf16[128,8192]{1,0:T(8,128)(2,1)S(1)}) custom-call(f32[48,128]{1,0:T(8,128)S(1)} %get-tuple-element.21.table, s32[9,8,128]{2,1,0:T(8,128)S(1)} %get-tuple-element.22.listed, f32[8,64,128]{2,1,0:T(8,128)S(1)} %all-to-all-done.received, ...), custom_call_target="tpu_custom_call" | custom-call | tf_op jit(solution)/shard_map/contact_geometry/pallas_call | solution.py:414
  34.6 1.8 %all-to-all-done.1.mom_received = f32[8,24,128]{2,1,0:T(8,128)S(1)} async-done(((f32[8,24,128]{2,1,0:T(8,128)}), f32[8,24,128]{2,1,0:T(8,128)S(1)}, u32[]{:S(2)}, u32[]{:S(2)}) %all-to-all-start.1) | async-done | bytes 98336 | tf_op jit(solution)/shard_map/all_to_all | solution.py:221
  36.4 1.7 %contact_force.1 = f32[3,1024]{1,0:T(4,128)} custom-call(f32[8,8,8,128]{3,2,1,0:T(8,128)S(1)} %get-tuple-element.36.geometry, s32[2,3,8,512]{3,2,1,0:T(8,128)S(1)} %get-tuple-element.37.places, bf16[128,8192]{1,0:T(8,128)(2,1)S(1)} %get-tuple-element.38.hot, f32[8,24,128]{2,1,0:T(8,128)S(1)} %all-to-all-done.1.mom_received), custom_call_target="tpu_custom_call" | custom-call | tf_op jit(solution)/shard_map/contact_force/pallas_call | solution.py:414
  (1 shorter events, 0.0 us)
Async XLA Ops:
  1.4 2.1 %collective-permute-start = (f32[1,64,128]{2,1,0:T(8,128)S(1)}, f32[1,64,128]{2,1,0:T(8,128)S(1)}, u32[]{:S(2)}, u32[]{:S(2)}) collective-permute-start(f32[1,64,128]{2,1,0:T(8,128)S(1)} %bitcast.6), channel_id=1, source_target_pairs={{0,8},{8,0},{16,24},{24,16},{1,9},{9,1},{17,25},{25,17},{2,10},{10... | collective-permute-start | bytes 98312 | tf_op jit(solution)/shard_map/ppermute | solution.py:430
  3.5 23.0 %all-to-all-start = ((f32[8,64,128]{2,1,0:T(8,128)}), f32[8,64,128]{2,1,0:T(8,128)S(1)}, u32[]{:S(2)}, u32[]{:S(2)}) async-start(f32[8,64,128]{2,1,0:T(8,128)} %get-tuple-element.24), calls=%async_computation | async-start | bytes 524288 | tf_op jit(solution)/shard_map/all_to_all | solution.py:221
  10.9 5.3 %collective-permute-start.1 = (f32[2,64,128]{2,1,0:T(8,128)S(1)}, f32[2,64,128]{2,1,0:T(8,128)S(1)}, u32[]{:S(2)}, u32[]{:S(2)}) collective-permute-start(f32[2,64,128]{2,1,0:T(8,128)S(1)} %pad_maximum_fusion), channel_id=1, source_target_pairs={{0,16},{8,24},{16,0},{24,8},{1,17},{9,25},{17,1},{25,9},{2,18},{10... | collective-permute-start | bytes 196616 | tf_op jit(solution)/shard_map/ppermute | solution.py:430
  19.9 1.2 %collective-permute-start.3 = (f32[1,24,128]{2,1,0:T(8,128)S(1)}, f32[1,24,128]{2,1,0:T(8,128)S(1)}, u32[]{:S(2)}, u32[]{:S(2)}) collective-permute-start(f32[1,24,128]{2,1,0:T(8,128)S(1)} %bitcast.10), channel_id=1, source_target_pairs={{0,8},{8,0},{16,24},{24,16},{1,9},{9,1},{17,25},{25,17},{2,10},{10... | collective-permute-start | bytes 36872 | tf_op jit(solution)/shard_map/ppermute | solution.py:430
  20.0 3.8 %collective-permute-start.2 = (f32[1,24,128]{2,1,0:T(8,128)S(1)}, f32[1,24,128]{2,1,0:T(8,128)S(1)}, u32[]{:S(2)}, u32[]{:S(2)}) collective-permute-start(f32[1,24,128]{2,1,0:T(8,128)S(1)} %bitcast.11), channel_id=1, source_target_pairs={{0,16},{8,24},{16,0},{24,8},{1,17},{9,25},{17,1},{25,9},{2,18},{10... | collective-permute-start | bytes 36872 | tf_op jit(solution)/shard_map/ppermute | solution.py:430
  23.7 1.2 %collective-permute-start.4 = (f32[1,24,128]{2,1,0:T(8,128)S(1)}, f32[1,24,128]{2,1,0:T(8,128)S(1)}, u32[]{:S(2)}, u32[]{:S(2)}) collective-permute-start(f32[1,24,128]{2,1,0:T(8,128)S(1)} %collective-permute-done.2.refs_3_), channel_id=1, source_target_pairs={{0,8},{8,0},{16,24},{24,16},{1,9},{9,1},{17,25},{25,17},{2,10},{10... | collective-permute-start | bytes 36872 | tf_op jit(solution)/shard_map/ppermute | solution.py:430
  26.6 9.9 %all-to-all-start.1 = ((f32[8,24,128]{2,1,0:T(8,128)}), f32[8,24,128]{2,1,0:T(8,128)S(1)}, u32[]{:S(2)}, u32[]{:S(2)}) async-start(f32[8,24,128]{2,1,0:T(8,128)} %get-tuple-element.39), calls=%async_computation.1 | async-start | bytes 196608 | tf_op jit(solution)/shard_map/all_to_all | solution.py:221

commit v7 on v6

--- a/solution.py
+++ b/solution.py
@@ -229,8 +229,8 @@
 
 
 def row_pack_kernel(*refs):
-    inputs, payload, (pos, field, chi, done) = refs[0:3], refs[3], refs[4:]
-    copy_in(inputs, (pos, field, chi), done)
+    inputs, payload, held, (pos, field, chi, done) = refs[0:7], refs[7], refs[8:12], refs[12:]
+    copy_in(inputs, (pos, field, chi, *held), done)
     groups = pos.shape[1] // LANES
     for g in range(groups):
         lanes = slice(g * LANES, (g + 1) * LANES)
@@ -242,14 +242,7 @@
     payload[7 * groups :, :] = jnp.zeros_like(payload[7 * groups :, :])
 
 
-def column_pack_kernel(*refs):
-    inputs, payload, (send, table, listed), (vel, owner, partner, counts, done) = (
-        refs[0:4],
-        refs[4],
-        refs[5:8],
-        refs[8:],
-    )
-    copy_in(inputs, (vel, owner, partner, counts), done)
+def column_pack_kernel(vel, owner, partner, counts, payload, send, table, listed):
     groups = vel.shape[1] // LANES
     slots = owner.shape[1] // LANES
     columns = owner.shape[0]
@@ -258,11 +251,11 @@
         for c in range(3):
             row = (3 + c) * groups + g
             table[row : row + 1, :] = vel[c : c + 1, g * LANES : (g + 1) * LANES]
+    order = column_order(columns)
+    tail = (send.shape[1] - 6 * groups - 2 * slots, LANES)
     for e in range(columns):
         send[e, 0 : 6 * groups, :] = table[...]
-        live = jnp.full(
-            (send.shape[1] - 6 * groups - 2 * slots, LANES), counts[0, column_order(columns)[e]]
-        )
+        live = jnp.broadcast_to(counts[:, order[e] : order[e] + 1], tail)
         send[e, 6 * groups + 2 * slots :, :] = live.astype(F32)
         listed[2 * slots, e : e + 1, :] = live[0:1]
     for q in range(slots):
@@ -327,6 +320,7 @@
 def geometry_kernel(slots, table, listed, received, mom, moments, out, places, hot):
     columns = received.shape[0]
     groups = mom.shape[0] // 3
+    lane_of = lax.broadcasted_iota(jnp.int32, (LANES, LANES), 1).astype(F32)
     for c in range(3):
         for g in range(groups):
             lanes = slice(g * LANES, (g + 1) * LANES)
@@ -357,15 +351,12 @@
         out[at, 7] = own[0] * normal[0] + own[1] * normal[1] + own[2] * normal[2]
         lanes = slice(q * LANES, (q + 1) * LANES)
         places[kind, 0, rows, lanes] = group
-        places[kind, 1, rows, lanes] = lane
-        places[kind, 2, rows, lanes] = other
-    lane_of = lax.broadcasted_iota(jnp.int32, (LANES, slots * LANES), 0)
-    for kind in range(2):
-        for e in range(columns):
-            here = places[kind, 1, e : e + 1, :] == lane_of
-            width = slots * LANES
-            first = (kind * columns + e) * width
-            hot[:, first : first + width] = jnp.where(here, 1.0, 0.0).astype(BF16)
+        places[kind, 1, rows, lanes] = other
+        turned = jnp.transpose(lane.astype(F32))
+        for s in range(SUBS):
+            first = ((kind * columns + rows.start + s) * slots + q) * LANES
+            here = turned[:, s : s + 1] == lane_of
+            hot[first : first + LANES, :] = jnp.where(here, 1.0, 0.0).astype(BF16)
 
 
 def force_kernel(slots, geometry, places, hot, mom_received, forces, pieces, values):
@@ -373,7 +364,7 @@
     groups = mom_received.shape[1] // 3
     for at, (kind, rows, q) in enumerate(contact_blocks(columns, slots)):
         lanes = slice(q * LANES, (q + 1) * LANES)
-        their_lane, their_group = split_index(places[kind, 2, rows, lanes])
+        their_lane, their_group = split_index(places[kind, 1, rows, lanes])
         their_bits = bits_of(their_group, groups)
         normal = [geometry[at, c] for c in range(3)]
         own = [geometry[at, 3 + c] for c in range(3)]
@@ -398,9 +389,7 @@
             values[:, first : first + width] = jnp.concatenate(
                 [jnp.where(here, pieces[kind, k, e : e + 1, :], 0.0) for k in range(9)], axis=0
             ).astype(BF16)
-    total = lax.dot_general(
-        values[...], hot[...], (((1,), (1,)), ((), ())), preferred_element_type=F32
-    )
+    total = jnp.dot(values[...], hot[...], preferred_element_type=F32)
     height = 3 * groups
     total = total[0:height] + total[height : 2 * height] + total[2 * height : 3 * height]
     for c in range(3):
@@ -499,20 +488,23 @@
     def in_hbm(*arrays):
         return [pltpu.with_memory_space_constraint(v, pltpu.HBM) for v in arrays]
 
-    inputs = in_hbm(positions, applied, suscept.reshape(1, count))
-    payload = call(
-        row_pack_kernel,
-        "row_pack",
-        shape(8 * groups, LANES),
-        *inputs,
-        specs=[HBM] * 3,
-        scratch=[pltpu.VMEM(v.shape, v.dtype) for v in inputs] + [pltpu.SemaphoreType.DMA((3,))],
-    )
     inputs = in_hbm(
+        positions,
+        applied,
+        suscept.reshape(1, count),
         velocity,
         owner.reshape(columns, slot_len),
         partner.reshape(columns, slot_len),
         contact_count.reshape(1, columns),
+    )
+    payload, *held = call(
+        row_pack_kernel,
+        "row_pack",
+        (shape(8 * groups, LANES),) + tuple(shape(*v.shape, dtype=v.dtype) for v in inputs[3:]),
+        *inputs,
+        specs=[HBM] * 7,
+        scratch=[pltpu.VMEM(v.shape, v.dtype) for v in inputs[:3]]
+        + [pltpu.SemaphoreType.DMA((7,))],
     )
     sent, table, listed = call(
         column_pack_kernel,
@@ -522,11 +514,8 @@
             shape(6 * groups, LANES),
             shape(2 * slots + 1, columns, LANES, dtype=jnp.int32),
         ),
-        *inputs,
+        *held,
         payload,
-        specs=[HBM] * 4 + [VMEM],
-        scratch=[pltpu.VMEM(v.shape, v.dtype) for v in inputs[:-1]]
-        + [pltpu.SMEM((1, columns), jnp.int32), pltpu.SemaphoreType.DMA((4,))],
     )
     paired = row_size > 1 and row_size & (row_size - 1) == 0
     rounds = (exchange if paired else others)(payload, "row", row_size)
@@ -569,8 +558,8 @@
         (
             shape(3, count),
             shape(len(contact_blocks(columns, slots)), 8, SUBS, LANES),
-            shape(2, 3, columns, slot_len, dtype=jnp.int32),
-            shape(LANES, 2 * columns * slot_len, dtype=BF16),
+            shape(2, 2, columns, slot_len, dtype=jnp.int32),
+            shape(2 * columns * slot_len, LANES, dtype=BF16),
         ),
         table,
         listed,

time: 38.6 us -> 38 us (0.984)
  Pallas kernels: 19 us -> 18.4 us
    pallas_call x9, Pallas kernels: 19 us -> 18.4 us  [call(): pl.pallas_call(kernel, out_shape=outs, in_specs=specs or [VMEM] * len(arg...]
    all_to_all x2, waiting for transfers between devices: 1.83 us -> 1.41 us  [to_columns(): lax.all_to_all(blocks, 'col', split_axis=0, concat_axis=0, axis_index_gro...]
  transfers between devices with their start and end apart: 7 -> 7, of which waited for: 4 -> 5; matrix products, arithmetic and copies ran while one was open for 0% -> 0% of each run, Pallas kernels for 43% -> 43%
where the time goes in v7:
time: 38 us; the launch traced here: 37.6 us
  Pallas kernels  18.4 us (48%)
  starting transfers between devices  15.6 us (41%)
  waiting for transfers between devices  2.83 us (7%)
  between operations  0.69 us (2%)
    pallas_call x9, Pallas kernels, call(): pl.pallas_call(kernel, out_shape=outs, in_specs=specs or [VMEM] * len(arg...  18.4 us
    all_to_all x2, starting transfers between devices, to_columns(): lax.all_to_all(blocks, 'col', split_axis=0, concat_axis=0, axis_index_gro...  12.8 us
    ppermute x5, starting transfers between devices, flip(): return lax.ppermute(blocks, axis, [(i, i ^ 1 << bit) for i in range(size)])  2.82 us
    ppermute x5, waiting for transfers between devices, flip(): return lax.ppermute(blocks, axis, [(i, i ^ 1 << bit) for i in range(size)])  1.42 us
    all_to_all x2, waiting for transfers between devices, to_columns(): lax.all_to_all(blocks, 'col', split_axis=0, concat_axis=0, axis_index_gro...  1.41 us
  transfers between devices with their start and end apart: 7, of which 5 were waited for; matrix products, arithmetic and copies ran while one was open for 0% of the time, Pallas kernels for 43%

profile of v7, /device:TPU:0, one launch (start us, length us, event | category | flops | bytes accessed | tf_op | source)
XLA Modules:
  0.0 37.6 jit_solution(94270106538193217)
XLA Ops:
  0.6 0.9 %row_pack.1 = (f32[64,128]{1,0:T(8,128)S(1)}, f32[3,1024]{1,0:T(4,128)S(1)}, s32[8,512]{1,0:T(8,128)S(1)}, s32[8,512]{1,0:T(8,128)S(1)}, s32[1,8]{1,0:T(1,128)S(1)}) custom-call(f32[3,1024]{1,0:T(4,128)} %refs_0_.1, f32[3,1024]{1,0:T(4,128)} %refs_1_.1, f32[1,1024]{1,0:T(1,128)} %bitcast.15, f32[3,1024]{1,0:T(4,128)} %refs_3_.1, s32[8,512]{1,0:T(8,128)} %bitcast.13, ...), custom_call_target="tpu_custom_call" | custom-call | tf_op jit(solution)/shard_map/row_pack/pallas_call | solution.py:403
  1.5 0.5 %collective-permute-start = (f32[1,64,128]{2,1,0:T(8,128)S(1)}, f32[1,64,128]{2,1,0:T(8,128)S(1)}, u32[]{:S(2)}, u32[]{:S(2)}) collective-permute-start(f32[1,64,128]{2,1,0:T(8,128)S(1)} %bitcast.6), channel_id=1, source_target_pairs={{0,8},{8,0},{16,24},{24,16},{1,9},{9,1},{17,25},{25,17},{2,10},{10... | collective-permute-start | bytes 98312 | tf_op jit(solution)/shard_map/ppermute | solution.py:419
  2.0 0.8 %column_pack.1 = (f32[8,64,128]{2,1,0:T(8,128)}, f32[48,128]{1,0:T(8,128)S(1)}, s32[9,8,128]{2,1,0:T(8,128)S(1)}) custom-call(f32[3,1024]{1,0:T(4,128)S(1)} %get-tuple-element.26.vel, s32[8,512]{1,0:T(8,128)S(1)} %get-tuple-element.27.owner, s32[8,512]{1,0:T(8,128)S(1)} %get-tuple-element.28.partner, s32[1,8]{1,0:T(1,128)S(1)} %get-tuple-element.29.counts, ...), custom_call_target="tpu_custom_call" | custom-call | tf_op jit(solution)/shard_map/column_pack/pallas_call | solution.py:403
  2.8 0.1 collective-permute-done.refs_2_
  2.9 7.7 %all-to-all-start = ((f32[8,64,128]{2,1,0:T(8,128)}), f32[8,64,128]{2,1,0:T(8,128)S(1)}, u32[]{:S(2)}, u32[]{:S(2)}) async-start(f32[8,64,128]{2,1,0:T(8,128)} %get-tuple-element.34), calls=%async_computation | async-start | bytes 524288 | tf_op jit(solution)/shard_map/all_to_all | solution.py:221
  10.6 1.6 %collective-permute-start.1 = (f32[2,64,128]{2,1,0:T(8,128)S(1)}, f32[2,64,128]{2,1,0:T(8,128)S(1)}, u32[]{:S(2)}, u32[]{:S(2)}) collective-permute-start(f32[2,64,128]{2,1,0:T(8,128)S(1)} %pad_maximum_fusion), channel_id=1, source_target_pairs={{0,16},{8,24},{16,0},{24,8},{1,17},{9,25},{17,1},{25,9},{2,18},{10... | collective-permute-start | bytes 196616 | tf_op jit(solution)/shard_map/ppermute | solution.py:419
  12.2 3.7 %field_sums.5 = (f32[48,1024]{1,0:T(8,128)S(1)}, bf16[2048,1024]{1,0:T(8,128)(2,1)S(1)}, bf16[2048,1024]{1,0:T(8,128)(2,1)S(1)}) custom-call(f32[64,128]{1,0:T(8,128)S(1)} %get-tuple-element.30.payload.refs_0_, f32[1,64,128]{2,1,0:T(8,128)S(1)} %bitcast.8, f32[1,64,128]{2,1,0:T(8,128)S(1)} %collective-permute-done.refs_2_), custom_call_target="tpu_custom_call" | custom-call | tf_op jit(solution)/shard_map/field_sums/pallas_call | solution.py:403
  15.9 0.0 collective-permute-done.1.refs_1_
  15.9 3.7 %field_sums.6 = (f32[24,128]{1,0:T(8,128)S(1)}, bf16[2048,1024]{1,0:T(8,128)(2,1)S(1)}, bf16[2048,1024]{1,0:T(8,128)(2,1)S(1)}) custom-call(f32[64,128]{1,0:T(8,128)S(1)} %get-tuple-element.30.payload.refs_0_, f32[2,64,128]{2,1,0:T(8,128)S(1)} %collective-permute-done.1.refs_1_, f32[48,1024]{1,0:T(8,128)S(1)} %get-tuple-element.36.refs_2_), custom_call_target="tpu_custom_call" | custom-call | tf_op jit(solution)/shard_map/field_sums/pallas_call | solution.py:403
  19.6 0.1 collective-permute-start.3
  19.7 0.6 %collective-permute-start.2 = (f32[1,24,128]{2,1,0:T(8,128)S(1)}, f32[1,24,128]{2,1,0:T(8,128)S(1)}, u32[]{:S(2)}, u32[]{:S(2)}) collective-permute-start(f32[1,24,128]{2,1,0:T(8,128)S(1)} %bitcast.11), channel_id=1, source_target_pairs={{0,16},{8,24},{16,0},{24,8},{1,17},{9,25},{17,1},{25,9},{2,18},{10... | collective-permute-start | bytes 36872 | tf_op jit(solution)/shard_map/ppermute | solution.py:419
  20.3 0.5 %collective-permute-done.3.refs_5_ = f32[1,24,128]{2,1,0:T(8,128)S(1)} collective-permute-done((f32[1,24,128]{2,1,0:T(8,128)S(1)}, f32[1,24,128]{2,1,0:T(8,128)S(1)}, u32[]{:S(2)}, u32[]{:S(2)}) %collective-permute-start.3) | collective-permute-done | bytes 12320 | tf_op jit(solution)/shard_map/ppermute | solution.py:419
  20.8 1.9 %field_sums.7.refs_6_ = f32[48,1024]{1,0:T(8,128)S(1)} custom-call(f32[64,128]{1,0:T(8,128)S(1)} %get-tuple-element.30.payload.refs_0_, f32[1,64,128]{2,1,0:T(8,128)S(1)} %bitcast.9, f32[1,64,128]{2,1,0:T(8,128)S(1)} %collective-permute-done.refs_2_, f32[24,128]{1,0:T(8,128)S(1)} %get-tuple-element.37.refs_3_.refs_2_, f32[1,24,128]{2,1,0:T(8,128)S(1)} %bitcast.12, ...), custom_call_target="tpu_custom_call" | custom-call | tf_op jit(solution)/shard_map/field_sums/pallas_call | solution.py:403
  22.7 0.7 %collective-permute-done.2.refs_3_ = f32[1,24,128]{2,1,0:T(8,128)S(1)} collective-permute-done((f32[1,24,128]{2,1,0:T(8,128)S(1)}, f32[1,24,128]{2,1,0:T(8,128)S(1)}, u32[]{:S(2)}, u32[]{:S(2)}) %collective-permute-start.2) | collective-permute-done | bytes 12320 | tf_op jit(solution)/shard_map/ppermute | solution.py:419
  23.4 0.0 collective-permute-start.4
  23.4 1.1 %field_sums.8.refs_6_ = f32[48,1024]{1,0:T(8,128)S(1)} custom-call(f32[64,128]{1,0:T(8,128)S(1)} %get-tuple-element.30.payload.refs_0_, f32[2,64,128]{2,1,0:T(8,128)S(1)} %collective-permute-done.1.refs_1_, f32[24,128]{1,0:T(8,128)S(1)} %get-tuple-element.37.refs_3_.refs_2_, f32[1,24,128]{2,1,0:T(8,128)S(1)} %collective-permute-done.2.refs_3_, ...), custom_call_target="tpu_custom_call" | custom-call | tf_op jit(solution)/shard_map/field_sums/pallas_call | solution.py:403
  24.5 0.1 collective-permute-done.4.refs_3_
  24.6 1.7 %field_sums.9 = (f32[24,128]{1,0:T(8,128)S(1)}, f32[8,24,128]{2,1,0:T(8,128)}) custom-call(f32[64,128]{1,0:T(8,128)S(1)} %get-tuple-element.30.payload.refs_0_, f32[2,64,128]{2,1,0:T(8,128)S(1)} %collective-permute-done.1.refs_1_, f32[24,128]{1,0:T(8,128)S(1)} %get-tuple-element.37.refs_3_.refs_2_, f32[1,24,128]{2,1,0:T(8,128)S(1)} %collective-permute-done.4.refs_3_, ...), custom_call_target="tpu_custom_call" | custom-call | tf_op jit(solution)/shard_map/field_sums/pallas_call | solution.py:403
  26.3 0.0 all-to-all-done.received
  26.3 5.1 %all-to-all-start.1 = ((f32[8,24,128]{2,1,0:T(8,128)}), f32[8,24,128]{2,1,0:T(8,128)S(1)}, u32[]{:S(2)}, u32[]{:S(2)}) async-start(f32[8,24,128]{2,1,0:T(8,128)} %get-tuple-element.49), calls=%async_computation.1 | async-start | bytes 196608 | tf_op jit(solution)/shard_map/all_to_all | solution.py:221
  31.4 3.4 %contact_geometry.1 = (f32[3,1024]{1,0:T(4,128)}, f32[8,8,8,128]{3,2,1,0:T(8,128)S(1)}, s32[2,2,8,512]{3,2,1,0:T(8,128)S(1)}, bf16[8192,128]{1,0:T(8,128)(2,1)S(1)}) custom-call(f32[48,128]{1,0:T(8,128)S(1)} %get-tuple-element.31.table, s32[9,8,128]{2,1,0:T(8,128)S(1)} %get-tuple-element.32.listed, f32[8,64,128]{2,1,0:T(8,128)S(1)} %all-to-all-done.received, ...), custom_call_target="tpu_custom_call" | custom-call | tf_op jit(solution)/shard_map/contact_geometry/pallas_call | solution.py:403
  34.7 1.4 %all-to-all-done.1.mom_received = f32[8,24,128]{2,1,0:T(8,128)S(1)} async-done(((f32[8,24,128]{2,1,0:T(8,128)}), f32[8,24,128]{2,1,0:T(8,128)S(1)}, u32[]{:S(2)}, u32[]{:S(2)}) %all-to-all-start.1) | async-done | bytes 98336 | tf_op jit(solution)/shard_map/all_to_all | solution.py:221
  36.2 1.4 %contact_force.1 = f32[3,1024]{1,0:T(4,128)} custom-call(f32[8,8,8,128]{3,2,1,0:T(8,128)S(1)} %get-tuple-element.46.geometry, s32[2,2,8,512]{3,2,1,0:T(8,128)S(1)} %get-tuple-element.47.places, bf16[8192,128]{1,0:T(8,128)(2,1)S(1)} %get-tuple-element.48.hot, f32[8,24,128]{2,1,0:T(8,128)S(1)} %all-to-all-done.1.mom_received), custom_call_target="tpu_custom_call" | custom-call | tf_op jit(solution)/shard_map/contact_force/pallas_call | solution.py:403
  (1 shorter events, 0.0 us)
Async XLA Ops:
  1.5 1.4 %collective-permute-start = (f32[1,64,128]{2,1,0:T(8,128)S(1)}, f32[1,64,128]{2,1,0:T(8,128)S(1)}, u32[]{:S(2)}, u32[]{:S(2)}) collective-permute-start(f32[1,64,128]{2,1,0:T(8,128)S(1)} %bitcast.6), channel_id=1, source_target_pairs={{0,8},{8,0},{16,24},{24,16},{1,9},{9,1},{17,25},{25,17},{2,10},{10... | collective-permute-start | bytes 98312 | tf_op jit(solution)/shard_map/ppermute | solution.py:419
  2.9 23.4 %all-to-all-start = ((f32[8,64,128]{2,1,0:T(8,128)}), f32[8,64,128]{2,1,0:T(8,128)S(1)}, u32[]{:S(2)}, u32[]{:S(2)}) async-start(f32[8,64,128]{2,1,0:T(8,128)} %get-tuple-element.34), calls=%async_computation | async-start | bytes 524288 | tf_op jit(solution)/shard_map/all_to_all | solution.py:221
  10.6 5.3 %collective-permute-start.1 = (f32[2,64,128]{2,1,0:T(8,128)S(1)}, f32[2,64,128]{2,1,0:T(8,128)S(1)}, u32[]{:S(2)}, u32[]{:S(2)}) collective-permute-start(f32[2,64,128]{2,1,0:T(8,128)S(1)} %pad_maximum_fusion), channel_id=1, source_target_pairs={{0,16},{8,24},{16,0},{24,8},{1,17},{9,25},{17,1},{25,9},{2,18},{10... | collective-permute-start | bytes 196616 | tf_op jit(solution)/shard_map/ppermute | solution.py:419
  19.6 1.2 %collective-permute-start.3 = (f32[1,24,128]{2,1,0:T(8,128)S(1)}, f32[1,24,128]{2,1,0:T(8,128)S(1)}, u32[]{:S(2)}, u32[]{:S(2)}) collective-permute-start(f32[1,24,128]{2,1,0:T(8,128)S(1)} %bitcast.10), channel_id=1, source_target_pairs={{0,8},{8,0},{16,24},{24,16},{1,9},{9,1},{17,25},{25,17},{2,10},{10... | collective-permute-start | bytes 36872 | tf_op jit(solution)/shard_map/ppermute | solution.py:419
  19.7 3.8 %collective-permute-start.2 = (f32[1,24,128]{2,1,0:T(8,128)S(1)}, f32[1,24,128]{2,1,0:T(8,128)S(1)}, u32[]{:S(2)}, u32[]{:S(2)}) collective-permute-start(f32[1,24,128]{2,1,0:T(8,128)S(1)} %bitcast.11), channel_id=1, source_target_pairs={{0,16},{8,24},{16,0},{24,8},{1,17},{9,25},{17,1},{25,9},{2,18},{10... | collective-permute-start | bytes 36872 | tf_op jit(solution)/shard_map/ppermute | solution.py:419
  23.4 1.2 %collective-permute-start.4 = (f32[1,24,128]{2,1,0:T(8,128)S(1)}, f32[1,24,128]{2,1,0:T(8,128)S(1)}, u32[]{:S(2)}, u32[]{:S(2)}) collective-permute-start(f32[1,24,128]{2,1,0:T(8,128)S(1)} %collective-permute-done.2.refs_3_), channel_id=1, source_target_pairs={{0,8},{8,0},{16,24},{24,16},{1,9},{9,1},{17,25},{25,17},{2,10},{10... | collective-permute-start | bytes 36872 | tf_op jit(solution)/shard_map/ppermute | solution.py:419
  26.3 9.9 %all-to-all-start.1 = ((f32[8,24,128]{2,1,0:T(8,128)}), f32[8,24,128]{2,1,0:T(8,128)S(1)}, u32[]{:S(2)}, u32[]{:S(2)}) async-start(f32[8,24,128]{2,1,0:T(8,128)} %get-tuple-element.49), calls=%async_computation.1 | async-start | bytes 196608 | tf_op jit(solution)/shard_map/all_to_all | solution.py:221

commit v8 on v7

--- a/solution.py
+++ b/solution.py
@@ -214,7 +214,8 @@
 
 
 def column_order(columns):
-    return [(k + columns // 2) % columns for k in range(columns)]
+    first = (columns // 2 + 1) % columns
+    return [first] + [k for k in range(columns) if k != first]
 
 
 def to_columns(blocks):
@@ -261,8 +262,7 @@
     for q in range(slots):
         lanes = slice(q * LANES, (q + 1) * LANES)
         for k, ref in enumerate((owner, partner)):
-            half = columns // 2
-            index = jnp.concatenate([ref[half:, lanes], ref[:half, lanes]], axis=0)
+            index = jnp.concatenate([ref[e : e + 1, lanes] for e in order], axis=0)
             send[:, 6 * groups + k * slots + q, :] = index.astype(F32)
             listed[k * slots + q] = index
 

time: 38 us -> 37.3 us (0.982)
  waiting for transfers between devices: 2.83 us -> 1.7 us
  starting transfers between devices: 15.6 us -> 16.1 us
    all_to_all x2, waiting for transfers between devices: 1.41 us -> 0.27 us  [to_columns(): lax.all_to_all(blocks, 'col', split_axis=0, concat_axis=0, axis_index_gro...]
    all_to_all x2, starting transfers between devices: 12.8 us -> 13.3 us  [to_columns(): lax.all_to_all(blocks, 'col', split_axis=0, concat_axis=0, axis_index_gro...]
  transfers between devices with their start and end apart: 7 -> 7, of which waited for: 5 -> 5; matrix products, arithmetic and copies ran while one was open for 0% -> 0% of each run, Pallas kernels for 43% -> 44%
where the time goes in v8:
time: 37.3 us; the launch traced here: 36.9 us
  Pallas kernels  18.4 us (49%)
  starting transfers between devices  16.1 us (43%)
  waiting for transfers between devices  1.7 us (5%)
  between operations  0.69 us (2%)
    pallas_call x9, Pallas kernels, call(): pl.pallas_call(kernel, out_shape=outs, in_specs=specs or [VMEM] * len(arg...  18.4 us
    all_to_all x2, starting transfers between devices, to_columns(): lax.all_to_all(blocks, 'col', split_axis=0, concat_axis=0, axis_index_gro...  13.3 us
    ppermute x5, starting transfers between devices, flip(): return lax.ppermute(blocks, axis, [(i, i ^ 1 << bit) for i in range(size)])  2.82 us
    ppermute x5, waiting for transfers between devices, flip(): return lax.ppermute(blocks, axis, [(i, i ^ 1 << bit) for i in range(size)])  1.43 us
  transfers between devices with their start and end apart: 7, of which 5 were waited for; matrix products, arithmetic and copies ran while one was open for 0% of the time, Pallas kernels for 44%

profile of v8, /device:TPU:0, one launch (start us, length us, event | category | flops | bytes accessed | tf_op | source)
XLA Modules:
  0.0 36.9 jit_solution(3737549843806125741)
XLA Ops:
  0.6 0.9 %row_pack.1 = (f32[64,128]{1,0:T(8,128)S(1)}, f32[3,1024]{1,0:T(4,128)S(1)}, s32[8,512]{1,0:T(8,128)S(1)}, s32[8,512]{1,0:T(8,128)S(1)}, s32[1,8]{1,0:T(1,128)S(1)}) custom-call(f32[3,1024]{1,0:T(4,128)} %refs_0_.1, f32[3,1024]{1,0:T(4,128)} %refs_1_.1, f32[1,1024]{1,0:T(1,128)} %bitcast.15, f32[3,1024]{1,0:T(4,128)} %refs_3_.1, s32[8,512]{1,0:T(8,128)} %bitcast.13, ...), custom_call_target="tpu_custom_call" | custom-call | tf_op jit(solution)/shard_map/row_pack/pallas_call | solution.py:403
  1.5 0.5 %collective-permute-start = (f32[1,64,128]{2,1,0:T(8,128)S(1)}, f32[1,64,128]{2,1,0:T(8,128)S(1)}, u32[]{:S(2)}, u32[]{:S(2)}) collective-permute-start(f32[1,64,128]{2,1,0:T(8,128)S(1)} %bitcast.6), channel_id=1, source_target_pairs={{0,8},{8,0},{16,24},{24,16},{1,9},{9,1},{17,25},{25,17},{2,10},{10... | collective-permute-start | bytes 98312 | tf_op jit(solution)/shard_map/ppermute | solution.py:419
  2.0 0.8 %column_pack.1 = (f32[8,64,128]{2,1,0:T(8,128)}, f32[48,128]{1,0:T(8,128)S(1)}, s32[9,8,128]{2,1,0:T(8,128)S(1)}) custom-call(f32[3,1024]{1,0:T(4,128)S(1)} %get-tuple-element.26.vel, s32[8,512]{1,0:T(8,128)S(1)} %get-tuple-element.27.owner, s32[8,512]{1,0:T(8,128)S(1)} %get-tuple-element.28.partner, s32[1,8]{1,0:T(1,128)S(1)} %get-tuple-element.29.counts, ...), custom_call_target="tpu_custom_call" | custom-call | tf_op jit(solution)/shard_map/column_pack/pallas_call | solution.py:403
  2.8 0.1 collective-permute-done.refs_2_
  2.9 8.2 %all-to-all-start = ((f32[8,64,128]{2,1,0:T(8,128)}), f32[8,64,128]{2,1,0:T(8,128)S(1)}, u32[]{:S(2)}, u32[]{:S(2)}) async-start(f32[8,64,128]{2,1,0:T(8,128)} %get-tuple-element.34), calls=%async_computation | async-start | bytes 524288 | tf_op jit(solution)/shard_map/all_to_all | solution.py:222
  11.1 1.6 %collective-permute-start.1 = (f32[2,64,128]{2,1,0:T(8,128)S(1)}, f32[2,64,128]{2,1,0:T(8,128)S(1)}, u32[]{:S(2)}, u32[]{:S(2)}) collective-permute-start(f32[2,64,128]{2,1,0:T(8,128)S(1)} %pad_maximum_fusion), channel_id=1, source_target_pairs={{0,16},{8,24},{16,0},{24,8},{1,17},{9,25},{17,1},{25,9},{2,18},{10... | collective-permute-start | bytes 196616 | tf_op jit(solution)/shard_map/ppermute | solution.py:419
  12.7 3.7 %field_sums.5 = (f32[48,1024]{1,0:T(8,128)S(1)}, bf16[2048,1024]{1,0:T(8,128)(2,1)S(1)}, bf16[2048,1024]{1,0:T(8,128)(2,1)S(1)}) custom-call(f32[64,128]{1,0:T(8,128)S(1)} %get-tuple-element.30.payload.refs_0_, f32[1,64,128]{2,1,0:T(8,128)S(1)} %bitcast.8, f32[1,64,128]{2,1,0:T(8,128)S(1)} %collective-permute-done.refs_2_), custom_call_target="tpu_custom_call" | custom-call | tf_op jit(solution)/shard_map/field_sums/pallas_call | solution.py:403
  16.3 0.0 collective-permute-done.1.refs_1_
  16.4 3.7 %field_sums.6 = (f32[24,128]{1,0:T(8,128)S(1)}, bf16[2048,1024]{1,0:T(8,128)(2,1)S(1)}, bf16[2048,1024]{1,0:T(8,128)(2,1)S(1)}) custom-call(f32[64,128]{1,0:T(8,128)S(1)} %get-tuple-element.30.payload.refs_0_, f32[2,64,128]{2,1,0:T(8,128)S(1)} %collective-permute-done.1.refs_1_, f32[48,1024]{1,0:T(8,128)S(1)} %get-tuple-element.36.refs_2_), custom_call_target="tpu_custom_call" | custom-call | tf_op jit(solution)/shard_map/field_sums/pallas_call | solution.py:403
  20.0 0.1 collective-permute-start.3
  20.1 0.6 %collective-permute-start.2 = (f32[1,24,128]{2,1,0:T(8,128)S(1)}, f32[1,24,128]{2,1,0:T(8,128)S(1)}, u32[]{:S(2)}, u32[]{:S(2)}) collective-permute-start(f32[1,24,128]{2,1,0:T(8,128)S(1)} %bitcast.11), channel_id=1, source_target_pairs={{0,16},{8,24},{16,0},{24,8},{1,17},{9,25},{17,1},{25,9},{2,18},{10... | collective-permute-start | bytes 36872 | tf_op jit(solution)/shard_map/ppermute | solution.py:419
  20.8 0.5 %collective-permute-done.3.refs_5_ = f32[1,24,128]{2,1,0:T(8,128)S(1)} collective-permute-done((f32[1,24,128]{2,1,0:T(8,128)S(1)}, f32[1,24,128]{2,1,0:T(8,128)S(1)}, u32[]{:S(2)}, u32[]{:S(2)}) %collective-permute-start.3) | collective-permute-done | bytes 12320 | tf_op jit(solution)/shard_map/ppermute | solution.py:419
  21.3 1.9 %field_sums.7.refs_6_ = f32[48,1024]{1,0:T(8,128)S(1)} custom-call(f32[64,128]{1,0:T(8,128)S(1)} %get-tuple-element.30.payload.refs_0_, f32[1,64,128]{2,1,0:T(8,128)S(1)} %bitcast.9, f32[1,64,128]{2,1,0:T(8,128)S(1)} %collective-permute-done.refs_2_, f32[24,128]{1,0:T(8,128)S(1)} %get-tuple-element.37.refs_3_.refs_2_, f32[1,24,128]{2,1,0:T(8,128)S(1)} %bitcast.12, ...), custom_call_target="tpu_custom_call" | custom-call | tf_op jit(solution)/shard_map/field_sums/pallas_call | solution.py:403
  23.2 0.7 %collective-permute-done.2.refs_3_ = f32[1,24,128]{2,1,0:T(8,128)S(1)} collective-permute-done((f32[1,24,128]{2,1,0:T(8,128)S(1)}, f32[1,24,128]{2,1,0:T(8,128)S(1)}, u32[]{:S(2)}, u32[]{:S(2)}) %collective-permute-start.2) | collective-permute-done | bytes 12320 | tf_op jit(solution)/shard_map/ppermute | solution.py:419
  23.9 0.0 collective-permute-start.4
  23.9 1.1 %field_sums.8.refs_6_ = f32[48,1024]{1,0:T(8,128)S(1)} custom-call(f32[64,128]{1,0:T(8,128)S(1)} %get-tuple-element.30.payload.refs_0_, f32[2,64,128]{2,1,0:T(8,128)S(1)} %collective-permute-done.1.refs_1_, f32[24,128]{1,0:T(8,128)S(1)} %get-tuple-element.37.refs_3_.refs_2_, f32[1,24,128]{2,1,0:T(8,128)S(1)} %collective-permute-done.2.refs_3_, ...), custom_call_target="tpu_custom_call" | custom-call | tf_op jit(solution)/shard_map/field_sums/pallas_call | solution.py:403
  25.0 0.1 collective-permute-done.4.refs_3_
  25.1 1.7 %field_sums.9 = (f32[24,128]{1,0:T(8,128)S(1)}, f32[8,24,128]{2,1,0:T(8,128)}) custom-call(f32[64,128]{1,0:T(8,128)S(1)} %get-tuple-element.30.payload.refs_0_, f32[2,64,128]{2,1,0:T(8,128)S(1)} %collective-permute-done.1.refs_1_, f32[24,128]{1,0:T(8,128)S(1)} %get-tuple-element.37.refs_3_.refs_2_, f32[1,24,128]{2,1,0:T(8,128)S(1)} %collective-permute-done.4.refs_3_, ...), custom_call_target="tpu_custom_call" | custom-call | tf_op jit(solution)/shard_map/field_sums/pallas_call | solution.py:403
  26.7 0.0 all-to-all-done.received
  26.8 5.1 %all-to-all-start.1 = ((f32[8,24,128]{2,1,0:T(8,128)}), f32[8,24,128]{2,1,0:T(8,128)S(1)}, u32[]{:S(2)}, u32[]{:S(2)}) async-start(f32[8,24,128]{2,1,0:T(8,128)} %get-tuple-element.49), calls=%async_computation.1 | async-start | bytes 196608 | tf_op jit(solution)/shard_map/all_to_all | solution.py:222
  31.9 3.4 %contact_geometry.1 = (f32[3,1024]{1,0:T(4,128)}, f32[8,8,8,128]{3,2,1,0:T(8,128)S(1)}, s32[2,2,8,512]{3,2,1,0:T(8,128)S(1)}, bf16[8192,128]{1,0:T(8,128)(2,1)S(1)}) custom-call(f32[48,128]{1,0:T(8,128)S(1)} %get-tuple-element.31.table, s32[9,8,128]{2,1,0:T(8,128)S(1)} %get-tuple-element.32.listed, f32[8,64,128]{2,1,0:T(8,128)S(1)} %all-to-all-done.received, ...), custom_call_target="tpu_custom_call" | custom-call | tf_op jit(solution)/shard_map/contact_geometry/pallas_call | solution.py:403
  35.2 0.3 all-to-all-done.1.mom_received
  35.5 1.4 %contact_force.1 = f32[3,1024]{1,0:T(4,128)} custom-call(f32[8,8,8,128]{3,2,1,0:T(8,128)S(1)} %get-tuple-element.46.geometry, s32[2,2,8,512]{3,2,1,0:T(8,128)S(1)} %get-tuple-element.47.places, bf16[8192,128]{1,0:T(8,128)(2,1)S(1)} %get-tuple-element.48.hot, f32[8,24,128]{2,1,0:T(8,128)S(1)} %all-to-all-done.1.mom_received), custom_call_target="tpu_custom_call" | custom-call | tf_op jit(solution)/shard_map/contact_force/pallas_call | solution.py:403
  (1 shorter events, 0.0 us)
Async XLA Ops:
  1.5 1.4 %collective-permute-start = (f32[1,64,128]{2,1,0:T(8,128)S(1)}, f32[1,64,128]{2,1,0:T(8,128)S(1)}, u32[]{:S(2)}, u32[]{:S(2)}) collective-permute-start(f32[1,64,128]{2,1,0:T(8,128)S(1)} %bitcast.6), channel_id=1, source_target_pairs={{0,8},{8,0},{16,24},{24,16},{1,9},{9,1},{17,25},{25,17},{2,10},{10... | collective-permute-start | bytes 98312 | tf_op jit(solution)/shard_map/ppermute | solution.py:419
  2.9 23.9 %all-to-all-start = ((f32[8,64,128]{2,1,0:T(8,128)}), f32[8,64,128]{2,1,0:T(8,128)S(1)}, u32[]{:S(2)}, u32[]{:S(2)}) async-start(f32[8,64,128]{2,1,0:T(8,128)} %get-tuple-element.34), calls=%async_computation | async-start | bytes 524288 | tf_op jit(solution)/shard_map/all_to_all | solution.py:222
  11.1 5.3 %collective-permute-start.1 = (f32[2,64,128]{2,1,0:T(8,128)S(1)}, f32[2,64,128]{2,1,0:T(8,128)S(1)}, u32[]{:S(2)}, u32[]{:S(2)}) collective-permute-start(f32[2,64,128]{2,1,0:T(8,128)S(1)} %pad_maximum_fusion), channel_id=1, source_target_pairs={{0,16},{8,24},{16,0},{24,8},{1,17},{9,25},{17,1},{25,9},{2,18},{10... | collective-permute-start | bytes 196616 | tf_op jit(solution)/shard_map/ppermute | solution.py:419
  20.0 1.2 %collective-permute-start.3 = (f32[1,24,128]{2,1,0:T(8,128)S(1)}, f32[1,24,128]{2,1,0:T(8,128)S(1)}, u32[]{:S(2)}, u32[]{:S(2)}) collective-permute-start(f32[1,24,128]{2,1,0:T(8,128)S(1)} %bitcast.10), channel_id=1, source_target_pairs={{0,8},{8,0},{16,24},{24,16},{1,9},{9,1},{17,25},{25,17},{2,10},{10... | collective-permute-start | bytes 36872 | tf_op jit(solution)/shard_map/ppermute | solution.py:419
  20.1 3.8 %collective-permute-start.2 = (f32[1,24,128]{2,1,0:T(8,128)S(1)}, f32[1,24,128]{2,1,0:T(8,128)S(1)}, u32[]{:S(2)}, u32[]{:S(2)}) collective-permute-start(f32[1,24,128]{2,1,0:T(8,128)S(1)} %bitcast.11), channel_id=1, source_target_pairs={{0,16},{8,24},{16,0},{24,8},{1,17},{9,25},{17,1},{25,9},{2,18},{10... | collective-permute-start | bytes 36872 | tf_op jit(solution)/shard_map/ppermute | solution.py:419
  23.9 1.2 %collective-permute-start.4 = (f32[1,24,128]{2,1,0:T(8,128)S(1)}, f32[1,24,128]{2,1,0:T(8,128)S(1)}, u32[]{:S(2)}, u32[]{:S(2)}) collective-permute-start(f32[1,24,128]{2,1,0:T(8,128)S(1)} %collective-permute-done.2.refs_3_), channel_id=1, source_target_pairs={{0,8},{8,0},{16,24},{24,16},{1,9},{9,1},{17,25},{25,17},{2,10},{10... | collective-permute-start | bytes 36872 | tf_op jit(solution)/shard_map/ppermute | solution.py:419
  26.8 8.7 %all-to-all-start.1 = ((f32[8,24,128]{2,1,0:T(8,128)}), f32[8,24,128]{2,1,0:T(8,128)S(1)}, u32[]{:S(2)}, u32[]{:S(2)}) async-start(f32[8,24,128]{2,1,0:T(8,128)} %get-tuple-element.49), calls=%async_computation.1 | async-start | bytes 196608 | tf_op jit(solution)/shard_map/all_to_all | solution.py:222

commit v9 on v8

--- a/solution.py
+++ b/solution.py
@@ -9,6 +9,7 @@
 from jax.sharding import PartitionSpec as P
 
 ITERS = 2
+PIECES = 2
 LANES = 128
 SUBS = 8
 FEATURES = 16
@@ -130,7 +131,8 @@
             refs.pop(0)
     kept = (refs.pop(0), refs.pop(0)) if has_kept else None
     before = refs.pop(0) if has_before else None
-    outs, (held, target, feats, sums) = refs[:-4], refs[-4:]
+    outs, (stages, target, feats, sums) = refs[:-4], refs[-4:]
+    held = stages.at[0]
     made = outs[1:3] if len(outs) == 3 else None
     groups = held.shape[1]
     count = groups * LANES
@@ -138,18 +140,23 @@
     center = [jnp.sum(p, keepdims=True) * (1.0 / count) for p in own_pos]
     pos = about(own_pos, center)
     if not has_kept:
-        target_rows(pos, held, target)
+        target_rows(pos, stages.at[1], target)
     sums[...] = before[...] if has_before else jnp.zeros_like(sums)
-    for k, there in enumerate(blocks):
+
+    def place(k):
+        their_pos = about(vectors_of(blocks[k], 0, groups), center)
+        source_rows(their_pos, stages.at[2 * k + 3], feats, k * count)
+
+    def weigh(k):
+        there = blocks[k]
         their_pos = about(vectors_of(there, 0, groups), center)
         if with_mom:
             their_mom = vectors_of(mom_blocks[k], 0, groups)
         else:
             chi = there[6 * groups : 7 * groups, :]
             their_mom = [chi * v for v in vectors_of(there, 3 * groups, groups)]
-        moment_rows(their_pos, their_mom, held, feats, k * count)
-        if not has_kept:
-            source_rows(their_pos, held, feats, k * count)
+        moment_rows(their_pos, their_mom, stages.at[2 * k + 2], feats, k * count)
+
     height, width = math.gcd(count, BLOCK), math.gcd(count, WIDTH)
     tiles = [
         (slice(a, a + height), slice(b, b + width))
@@ -171,21 +178,31 @@
             moments, low, preferred_element_type=F32
         )
 
+    each = len(tiles) // len(blocks)
     if has_kept:
+        for k in range(len(blocks)):
+            weigh(k)
         for a, b in tiles:
             k, at = divmod(a.start, count)
             rows = slice(picks[k] * count + at, picks[k] * count + at + height)
             add((a, b), kept[0][rows, b], kept[1][rows, b])
     else:
+        place(0)
         radius_sq, ready = radius_of(tiles[0]), None
+        weigh(0)
         for at, tile in enumerate(tiles):
+            k, step = at // each + 1, at % each
+            if k < len(blocks) and step == each // 4:
+                place(k)
+            if k < len(blocks) and step == each // 2:
+                weigh(k)
             following = radius_of(tiles[at + 1]) if at + 1 < len(tiles) else None
+            if ready is not None:
+                add(*ready)
             high, low = pair_coefficient(radius_sq)
             if made:
                 made[0][tile] = high
                 made[1][tile] = low
-            if ready is not None:
-                add(*ready)
             ready, radius_sq = (tile, high, low), following
         add(*ready)
     if not is_last:
@@ -362,36 +379,41 @@
 def force_kernel(slots, geometry, places, hot, mom_received, forces, pieces, values):
     columns = mom_received.shape[0]
     groups = mom_received.shape[1] // 3
-    for at, (kind, rows, q) in enumerate(contact_blocks(columns, slots)):
-        lanes = slice(q * LANES, (q + 1) * LANES)
-        their_lane, their_group = split_index(places[kind, 1, rows, lanes])
-        their_bits = bits_of(their_group, groups)
-        normal = [geometry[at, c] for c in range(3)]
-        own = [geometry[at, 3 + c] for c in range(3)]
-        along_own = geometry[at, 7]
-        their = [
-            look_up(their_tables(mom_received, rows, c * groups, groups), their_lane, their_bits)
-            for c in range(3)
-        ]
-        along_their = their[0] * normal[0] + their[1] * normal[1] + their[2] * normal[2]
-        product = own[0] * their[0] + own[1] * their[1] + own[2] * their[2]
-        radial = 3.0 * (product - 5.0 * along_own * along_their) + geometry[at, 6]
-        for c in range(3):
-            force = 3.0 * (along_own * their[c] + along_their * own[c]) + radial * normal[c]
-            for k, piece in enumerate(split3(force)):
-                pieces[kind, k * 3 + c, rows, lanes] = piece
     width = slots * LANES
+    height = 3 * groups
     row_of = lax.broadcasted_iota(jnp.int32, (groups, width), 0)
-    for kind in range(2):
-        for e in range(columns):
+    order = list(enumerate(contact_blocks(columns, slots)))
+    total = None
+    for first in range(0, len(order), slots):
+        for at, (kind, rows, q) in order[first : first + slots]:
+            lanes = slice(q * LANES, (q + 1) * LANES)
+            their_lane, their_group = split_index(places[kind, 1, rows, lanes])
+            their_bits = bits_of(their_group, groups)
+            normal = [geometry[at, c] for c in range(3)]
+            own = [geometry[at, 3 + c] for c in range(3)]
+            along_own = geometry[at, 7]
+            their = [
+                look_up(their_tables(mom_received, rows, c * groups, groups), their_lane, their_bits)
+                for c in range(3)
+            ]
+            along_their = their[0] * normal[0] + their[1] * normal[1] + their[2] * normal[2]
+            product = own[0] * their[0] + own[1] * their[1] + own[2] * their[2]
+            radial = 3.0 * (product - 5.0 * along_own * along_their) + geometry[at, 6]
+            for c in range(3):
+                force = 3.0 * (along_own * their[c] + along_their * own[c]) + radial * normal[c]
+                for k, piece in enumerate(split3(force)[:PIECES]):
+                    pieces[kind, k * 3 + c, rows, lanes] = piece
+        for e in range(rows.start, rows.stop):
             here = places[kind, 0, e : e + 1, :] == row_of
-            first = (kind * columns + e) * width
-            values[:, first : first + width] = jnp.concatenate(
-                [jnp.where(here, pieces[kind, k, e : e + 1, :], 0.0) for k in range(9)], axis=0
+            start = (kind * columns + e) * width
+            values[:, start : start + width] = jnp.concatenate(
+                [jnp.where(here, pieces[kind, k, e : e + 1, :], 0.0) for k in range(3 * PIECES)],
+                axis=0,
             ).astype(BF16)
-    total = jnp.dot(values[...], hot[...], preferred_element_type=F32)
-    height = 3 * groups
-    total = total[0:height] + total[height : 2 * height] + total[2 * height : 3 * height]
+        span = slice((kind * columns + rows.start) * width, (kind * columns + rows.stop) * width)
+        summed = jnp.dot(values[:, span], hot[span, :], preferred_element_type=F32)
+        total = summed if total is None else total + summed
+    total = sum(total[k * height : (k + 1) * height] for k in range(PIECES))
     for c in range(3):
         for g in range(groups):
             row = c * groups + g
@@ -469,7 +491,7 @@
             outs,
             *args,
             scratch=[
-                pltpu.VMEM((FEATURES, groups, LANES), F32),
+                pltpu.VMEM((2 * len(picks) + 2, FEATURES, groups, LANES), F32),
                 pltpu.VMEM((PAIR_ROWS, count), BF16),
                 pltpu.VMEM((3 * FEATURES + PAIR_ROWS, length), BF16),
                 pltpu.VMEM((3 * FEATURES, count), F32),
@@ -575,8 +597,8 @@
         hot,
         mom_received,
         scratch=[
-            pltpu.VMEM((2, 9, columns, slot_len), F32),
-            pltpu.VMEM((9 * groups, 2 * columns * slot_len), BF16),
+            pltpu.VMEM((2, 3 * PIECES, columns, slot_len), F32),
+            pltpu.VMEM((3 * PIECES * groups, 2 * columns * slot_len), BF16),
         ],
     )
     return (moments, forces)

time: 37.3 us -> 37.2 us (level)
  no operation moved by 1% of the time
where the time goes in v9:
time: 37.2 us; the launch traced here: 36.8 us
  Pallas kernels  18.4 us (49%)
  starting transfers between devices  16.1 us (43%)
  waiting for transfers between devices  1.62 us (4%)
  between operations  0.69 us (2%)
    pallas_call x9, Pallas kernels, call(): pl.pallas_call(kernel, out_shape=outs, in_specs=specs or [VMEM] * len(arg...  18.4 us
    all_to_all x2, starting transfers between devices, to_columns(): lax.all_to_all(blocks, 'col', split_axis=0, concat_axis=0, axis_index_gro...  13.3 us
    ppermute x5, starting transfers between devices, flip(): return lax.ppermute(blocks, axis, [(i, i ^ 1 << bit) for i in range(size)])  2.85 us
    ppermute x5, waiting for transfers between devices, flip(): return lax.ppermute(blocks, axis, [(i, i ^ 1 << bit) for i in range(size)])  1.35 us
  transfers between devices with their start and end apart: 7, of which 5 were waited for; matrix products, arithmetic and copies ran while one was open for 0% of the time, Pallas kernels for 44%

profile of v9, /device:TPU:0, one launch (start us, length us, event | category | flops | bytes accessed | tf_op | source)
XLA Modules:
  0.0 36.8 jit_solution(8541950000905473815)
XLA Ops:
  0.6 0.9 %row_pack.1 = (f32[64,128]{1,0:T(8,128)S(1)}, f32[3,1024]{1,0:T(4,128)S(1)}, s32[8,512]{1,0:T(8,128)S(1)}, s32[8,512]{1,0:T(8,128)S(1)}, s32[1,8]{1,0:T(1,128)S(1)}) custom-call(f32[3,1024]{1,0:T(4,128)} %refs_0_.1, f32[3,1024]{1,0:T(4,128)} %refs_1_.1, f32[1,1024]{1,0:T(1,128)} %bitcast.15, f32[3,1024]{1,0:T(4,128)} %refs_3_.1, s32[8,512]{1,0:T(8,128)} %bitcast.13, ...), custom_call_target="tpu_custom_call" | custom-call | tf_op jit(solution)/shard_map/row_pack/pallas_call | solution.py:425
  1.5 0.5 %collective-permute-start = (f32[1,64,128]{2,1,0:T(8,128)S(1)}, f32[1,64,128]{2,1,0:T(8,128)S(1)}, u32[]{:S(2)}, u32[]{:S(2)}) collective-permute-start(f32[1,64,128]{2,1,0:T(8,128)S(1)} %bitcast.6), channel_id=1, source_target_pairs={{0,8},{8,0},{16,24},{24,16},{1,9},{9,1},{17,25},{25,17},{2,10},{10... | collective-permute-start | bytes 98312 | tf_op jit(solution)/shard_map/ppermute | solution.py:441
  2.0 0.8 %column_pack.1 = (f32[8,64,128]{2,1,0:T(8,128)}, f32[48,128]{1,0:T(8,128)S(1)}, s32[9,8,128]{2,1,0:T(8,128)S(1)}) custom-call(f32[3,1024]{1,0:T(4,128)S(1)} %get-tuple-element.26.vel, s32[8,512]{1,0:T(8,128)S(1)} %get-tuple-element.27.owner, s32[8,512]{1,0:T(8,128)S(1)} %get-tuple-element.28.partner, s32[1,8]{1,0:T(1,128)S(1)} %get-tuple-element.29.counts, ...), custom_call_target="tpu_custom_call" | custom-call | tf_op jit(solution)/shard_map/column_pack/pallas_call | solution.py:425
  2.8 0.1 collective-permute-done.refs_2_
  2.9 8.2 %all-to-all-start = ((f32[8,64,128]{2,1,0:T(8,128)}), f32[8,64,128]{2,1,0:T(8,128)S(1)}, u32[]{:S(2)}, u32[]{:S(2)}) async-start(f32[8,64,128]{2,1,0:T(8,128)} %get-tuple-element.34), calls=%async_computation | async-start | bytes 524288 | tf_op jit(solution)/shard_map/all_to_all | solution.py:239
  11.1 1.6 %collective-permute-start.1 = (f32[2,64,128]{2,1,0:T(8,128)S(1)}, f32[2,64,128]{2,1,0:T(8,128)S(1)}, u32[]{:S(2)}, u32[]{:S(2)}) collective-permute-start(f32[2,64,128]{2,1,0:T(8,128)S(1)} %pad_maximum_fusion), channel_id=1, source_target_pairs={{0,16},{8,24},{16,0},{24,8},{1,17},{9,25},{17,1},{25,9},{2,18},{10... | collective-permute-start | bytes 196616 | tf_op jit(solution)/shard_map/ppermute | solution.py:441
  12.7 3.6 %field_sums.5 = (f32[48,1024]{1,0:T(8,128)S(1)}, bf16[2048,1024]{1,0:T(8,128)(2,1)S(1)}, bf16[2048,1024]{1,0:T(8,128)(2,1)S(1)}) custom-call(f32[64,128]{1,0:T(8,128)S(1)} %get-tuple-element.30.payload.refs_0_, f32[1,64,128]{2,1,0:T(8,128)S(1)} %bitcast.8, f32[1,64,128]{2,1,0:T(8,128)S(1)} %collective-permute-done.refs_2_), custom_call_target="tpu_custom_call" | custom-call | tf_op jit(solution)/shard_map/field_sums/pallas_call | solution.py:425
  16.3 0.0 collective-permute-done.1.refs_1_
  16.3 3.7 %field_sums.6 = (f32[24,128]{1,0:T(8,128)S(1)}, bf16[2048,1024]{1,0:T(8,128)(2,1)S(1)}, bf16[2048,1024]{1,0:T(8,128)(2,1)S(1)}) custom-call(f32[64,128]{1,0:T(8,128)S(1)} %get-tuple-element.30.payload.refs_0_, f32[2,64,128]{2,1,0:T(8,128)S(1)} %collective-permute-done.1.refs_1_, f32[48,1024]{1,0:T(8,128)S(1)} %get-tuple-element.36.refs_2_), custom_call_target="tpu_custom_call" | custom-call | tf_op jit(solution)/shard_map/field_sums/pallas_call | solution.py:425
  20.0 0.1 collective-permute-start.3
  20.1 0.7 %collective-permute-start.2 = (f32[1,24,128]{2,1,0:T(8,128)S(1)}, f32[1,24,128]{2,1,0:T(8,128)S(1)}, u32[]{:S(2)}, u32[]{:S(2)}) collective-permute-start(f32[1,24,128]{2,1,0:T(8,128)S(1)} %bitcast.11), channel_id=1, source_target_pairs={{0,16},{8,24},{16,0},{24,8},{1,17},{9,25},{17,1},{25,9},{2,18},{10... | collective-permute-start | bytes 36872 | tf_op jit(solution)/shard_map/ppermute | solution.py:441
  20.7 0.5 %collective-permute-done.3.refs_5_ = f32[1,24,128]{2,1,0:T(8,128)S(1)} collective-permute-done((f32[1,24,128]{2,1,0:T(8,128)S(1)}, f32[1,24,128]{2,1,0:T(8,128)S(1)}, u32[]{:S(2)}, u32[]{:S(2)}) %collective-permute-start.3) | collective-permute-done | bytes 12320 | tf_op jit(solution)/shard_map/ppermute | solution.py:441
  21.2 1.9 %field_sums.7.refs_6_ = f32[48,1024]{1,0:T(8,128)S(1)} custom-call(f32[64,128]{1,0:T(8,128)S(1)} %get-tuple-element.30.payload.refs_0_, f32[1,64,128]{2,1,0:T(8,128)S(1)} %bitcast.9, f32[1,64,128]{2,1,0:T(8,128)S(1)} %collective-permute-done.refs_2_, f32[24,128]{1,0:T(8,128)S(1)} %get-tuple-element.37.refs_3_.refs_2_, f32[1,24,128]{2,1,0:T(8,128)S(1)} %bitcast.12, ...), custom_call_target="tpu_custom_call" | custom-call | tf_op jit(solution)/shard_map/field_sums/pallas_call | solution.py:425
  23.2 0.7 %collective-permute-done.2.refs_3_ = f32[1,24,128]{2,1,0:T(8,128)S(1)} collective-permute-done((f32[1,24,128]{2,1,0:T(8,128)S(1)}, f32[1,24,128]{2,1,0:T(8,128)S(1)}, u32[]{:S(2)}, u32[]{:S(2)}) %collective-permute-start.2) | collective-permute-done | bytes 12320 | tf_op jit(solution)/shard_map/ppermute | solution.py:441
  23.8 0.0 collective-permute-start.4
  23.8 1.1 %field_sums.8.refs_6_ = f32[48,1024]{1,0:T(8,128)S(1)} custom-call(f32[64,128]{1,0:T(8,128)S(1)} %get-tuple-element.30.payload.refs_0_, f32[2,64,128]{2,1,0:T(8,128)S(1)} %collective-permute-done.1.refs_1_, f32[24,128]{1,0:T(8,128)S(1)} %get-tuple-element.37.refs_3_.refs_2_, f32[1,24,128]{2,1,0:T(8,128)S(1)} %collective-permute-done.2.refs_3_, ...), custom_call_target="tpu_custom_call" | custom-call | tf_op jit(solution)/shard_map/field_sums/pallas_call | solution.py:425
  24.9 0.1 collective-permute-done.4.refs_3_
  25.0 1.7 %field_sums.9 = (f32[24,128]{1,0:T(8,128)S(1)}, f32[8,24,128]{2,1,0:T(8,128)}) custom-call(f32[64,128]{1,0:T(8,128)S(1)} %get-tuple-element.30.payload.refs_0_, f32[2,64,128]{2,1,0:T(8,128)S(1)} %collective-permute-done.1.refs_1_, f32[24,128]{1,0:T(8,128)S(1)} %get-tuple-element.37.refs_3_.refs_2_, f32[1,24,128]{2,1,0:T(8,128)S(1)} %collective-permute-done.4.refs_3_, ...), custom_call_target="tpu_custom_call" | custom-call | tf_op jit(solution)/shard_map/field_sums/pallas_call | solution.py:425
  26.7 0.0 all-to-all-done.received
  26.7 5.1 %all-to-all-start.1 = ((f32[8,24,128]{2,1,0:T(8,128)}), f32[8,24,128]{2,1,0:T(8,128)S(1)}, u32[]{:S(2)}, u32[]{:S(2)}) async-start(f32[8,24,128]{2,1,0:T(8,128)} %get-tuple-element.49), calls=%async_computation.1 | async-start | bytes 196608 | tf_op jit(solution)/shard_map/all_to_all | solution.py:239
  31.8 3.4 %contact_geometry.1 = (f32[3,1024]{1,0:T(4,128)}, f32[8,8,8,128]{3,2,1,0:T(8,128)S(1)}, s32[2,2,8,512]{3,2,1,0:T(8,128)S(1)}, bf16[8192,128]{1,0:T(8,128)(2,1)S(1)}) custom-call(f32[48,128]{1,0:T(8,128)S(1)} %get-tuple-element.31.table, s32[9,8,128]{2,1,0:T(8,128)S(1)} %get-tuple-element.32.listed, f32[8,64,128]{2,1,0:T(8,128)S(1)} %all-to-all-done.received, ...), custom_call_target="tpu_custom_call" | custom-call | tf_op jit(solution)/shard_map/contact_geometry/pallas_call | solution.py:425
  35.2 0.3 all-to-all-done.1.mom_received
  35.4 1.4 %contact_force.1 = f32[3,1024]{1,0:T(4,128)} custom-call(f32[8,8,8,128]{3,2,1,0:T(8,128)S(1)} %get-tuple-element.46.geometry, s32[2,2,8,512]{3,2,1,0:T(8,128)S(1)} %get-tuple-element.47.places, bf16[8192,128]{1,0:T(8,128)(2,1)S(1)} %get-tuple-element.48.hot, f32[8,24,128]{2,1,0:T(8,128)S(1)} %all-to-all-done.1.mom_received), custom_call_target="tpu_custom_call" | custom-call | tf_op jit(solution)/shard_map/contact_force/pallas_call | solution.py:425
  (1 shorter events, 0.0 us)
Async XLA Ops:
  1.5 1.4 %collective-permute-start = (f32[1,64,128]{2,1,0:T(8,128)S(1)}, f32[1,64,128]{2,1,0:T(8,128)S(1)}, u32[]{:S(2)}, u32[]{:S(2)}) collective-permute-start(f32[1,64,128]{2,1,0:T(8,128)S(1)} %bitcast.6), channel_id=1, source_target_pairs={{0,8},{8,0},{16,24},{24,16},{1,9},{9,1},{17,25},{25,17},{2,10},{10... | collective-permute-start | bytes 98312 | tf_op jit(solution)/shard_map/ppermute | solution.py:441
  2.9 23.8 %all-to-all-start = ((f32[8,64,128]{2,1,0:T(8,128)}), f32[8,64,128]{2,1,0:T(8,128)S(1)}, u32[]{:S(2)}, u32[]{:S(2)}) async-start(f32[8,64,128]{2,1,0:T(8,128)} %get-tuple-element.34), calls=%async_computation | async-start | bytes 524288 | tf_op jit(solution)/shard_map/all_to_all | solution.py:239
  11.1 5.2 %collective-permute-start.1 = (f32[2,64,128]{2,1,0:T(8,128)S(1)}, f32[2,64,128]{2,1,0:T(8,128)S(1)}, u32[]{:S(2)}, u32[]{:S(2)}) collective-permute-start(f32[2,64,128]{2,1,0:T(8,128)S(1)} %pad_maximum_fusion), channel_id=1, source_target_pairs={{0,16},{8,24},{16,0},{24,8},{1,17},{9,25},{17,1},{25,9},{2,18},{10... | collective-permute-start | bytes 196616 | tf_op jit(solution)/shard_map/ppermute | solution.py:441
  20.0 1.2 %collective-permute-start.3 = (f32[1,24,128]{2,1,0:T(8,128)S(1)}, f32[1,24,128]{2,1,0:T(8,128)S(1)}, u32[]{:S(2)}, u32[]{:S(2)}) collective-permute-start(f32[1,24,128]{2,1,0:T(8,128)S(1)} %bitcast.10), channel_id=1, source_target_pairs={{0,8},{8,0},{16,24},{24,16},{1,9},{9,1},{17,25},{25,17},{2,10},{10... | collective-permute-start | bytes 36872 | tf_op jit(solution)/shard_map/ppermute | solution.py:441
  20.1 3.8 %collective-permute-start.2 = (f32[1,24,128]{2,1,0:T(8,128)S(1)}, f32[1,24,128]{2,1,0:T(8,128)S(1)}, u32[]{:S(2)}, u32[]{:S(2)}) collective-permute-start(f32[1,24,128]{2,1,0:T(8,128)S(1)} %bitcast.11), channel_id=1, source_target_pairs={{0,16},{8,24},{16,0},{24,8},{1,17},{9,25},{17,1},{25,9},{2,18},{10... | collective-permute-start | bytes 36872 | tf_op jit(solution)/shard_map/ppermute | solution.py:441
  23.8 1.2 %collective-permute-start.4 = (f32[1,24,128]{2,1,0:T(8,128)S(1)}, f32[1,24,128]{2,1,0:T(8,128)S(1)}, u32[]{:S(2)}, u32[]{:S(2)}) collective-permute-start(f32[1,24,128]{2,1,0:T(8,128)S(1)} %collective-permute-done.2.refs_3_), channel_id=1, source_target_pairs={{0,8},{8,0},{16,24},{24,16},{1,9},{9,1},{17,25},{25,17},{2,10},{10... | collective-permute-start | bytes 36872 | tf_op jit(solution)/shard_map/ppermute | solution.py:441
  26.7 8.7 %all-to-all-start.1 = ((f32[8,24,128]{2,1,0:T(8,128)}), f32[8,24,128]{2,1,0:T(8,128)S(1)}, u32[]{:S(2)}, u32[]{:S(2)}) async-start(f32[8,24,128]{2,1,0:T(8,128)} %get-tuple-element.49), calls=%async_computation.1 | async-start | bytes 196608 | tf_op jit(solution)/shard_map/all_to_all | solution.py:239

commit v10 on v9

--- a/solution.py
+++ b/solution.py
@@ -226,8 +226,7 @@
     ]
     for copy in copies:
         copy.start()
-    for copy in copies:
-        copy.wait()
+    return copies
 
 
 def column_order(columns):
@@ -248,7 +247,9 @@
 
 def row_pack_kernel(*refs):
     inputs, payload, held, (pos, field, chi, done) = refs[0:7], refs[7], refs[8:12], refs[12:]
-    copy_in(inputs, (pos, field, chi, *held), done)
+    copies = copy_in(inputs, (pos, field, chi, *held), done)
+    for copy in copies[:3]:
+        copy.wait()
     groups = pos.shape[1] // LANES
     for g in range(groups):
         lanes = slice(g * LANES, (g + 1) * LANES)
@@ -258,6 +259,8 @@
             payload[row : row + 1, :] = field[c : c + 1, lanes]
         payload[6 * groups + g : 6 * groups + g + 1, :] = chi[:, lanes]
     payload[7 * groups :, :] = jnp.zeros_like(payload[7 * groups :, :])
+    for copy in copies[3:]:
+        copy.wait()
 
 
 def column_pack_kernel(vel, owner, partner, counts, payload, send, table, listed):

time: 37.2 us -> 37.2 us (level)
  no operation moved by 1% of the time
where the time goes in v10:
time: 37.2 us; the launch traced here: 36.8 us
  Pallas kernels  18.4 us (49%)
  starting transfers between devices  16.1 us (43%)
  waiting for transfers between devices  1.63 us (4%)
  between operations  0.69 us (2%)
    pallas_call x9, Pallas kernels, call(): pl.pallas_call(kernel, out_shape=outs, in_specs=specs or [VMEM] * len(arg...  18.4 us
    all_to_all x2, starting transfers between devices, to_columns(): lax.all_to_all(blocks, 'col', split_axis=0, concat_axis=0, axis_index_gro...  13.3 us
    ppermute x5, starting transfers between devices, flip(): return lax.ppermute(blocks, axis, [(i, i ^ 1 << bit) for i in range(size)])  2.85 us
    ppermute x5, waiting for transfers between devices, flip(): return lax.ppermute(blocks, axis, [(i, i ^ 1 << bit) for i in range(size)])  1.36 us
  transfers between devices with their start and end apart: 7, of which 5 were waited for; matrix products, arithmetic and copies ran while one was open for 0% of the time, Pallas kernels for 44%

profile of v10, /device:TPU:0, one launch (start us, length us, event | category | flops | bytes accessed | tf_op | source)
XLA Modules:
  0.0 36.8 jit_solution(14831979629828946742)
XLA Ops:
  0.6 0.9 %row_pack.1 = (f32[64,128]{1,0:T(8,128)S(1)}, f32[3,1024]{1,0:T(4,128)S(1)}, s32[8,512]{1,0:T(8,128)S(1)}, s32[8,512]{1,0:T(8,128)S(1)}, s32[1,8]{1,0:T(1,128)S(1)}) custom-call(f32[3,1024]{1,0:T(4,128)} %refs_0_.1, f32[3,1024]{1,0:T(4,128)} %refs_1_.1, f32[1,1024]{1,0:T(1,128)} %bitcast.15, f32[3,1024]{1,0:T(4,128)} %refs_3_.1, s32[8,512]{1,0:T(8,128)} %bitcast.13, ...), custom_call_target="tpu_custom_call" | custom-call | tf_op jit(solution)/shard_map/row_pack/pallas_call | solution.py:428
  1.5 0.5 %collective-permute-start = (f32[1,64,128]{2,1,0:T(8,128)S(1)}, f32[1,64,128]{2,1,0:T(8,128)S(1)}, u32[]{:S(2)}, u32[]{:S(2)}) collective-permute-start(f32[1,64,128]{2,1,0:T(8,128)S(1)} %bitcast.6), channel_id=1, source_target_pairs={{0,8},{8,0},{16,24},{24,16},{1,9},{9,1},{17,25},{25,17},{2,10},{10... | collective-permute-start | bytes 98312 | tf_op jit(solution)/shard_map/ppermute | solution.py:444
  2.0 0.8 %column_pack.1 = (f32[8,64,128]{2,1,0:T(8,128)}, f32[48,128]{1,0:T(8,128)S(1)}, s32[9,8,128]{2,1,0:T(8,128)S(1)}) custom-call(f32[3,1024]{1,0:T(4,128)S(1)} %get-tuple-element.26.vel, s32[8,512]{1,0:T(8,128)S(1)} %get-tuple-element.27.owner, s32[8,512]{1,0:T(8,128)S(1)} %get-tuple-element.28.partner, s32[1,8]{1,0:T(1,128)S(1)} %get-tuple-element.29.counts, ...), custom_call_target="tpu_custom_call" | custom-call | tf_op jit(solution)/shard_map/column_pack/pallas_call | solution.py:428
  2.8 0.1 collective-permute-done.refs_2_
  2.9 8.2 %all-to-all-start = ((f32[8,64,128]{2,1,0:T(8,128)}), f32[8,64,128]{2,1,0:T(8,128)S(1)}, u32[]{:S(2)}, u32[]{:S(2)}) async-start(f32[8,64,128]{2,1,0:T(8,128)} %get-tuple-element.34), calls=%async_computation | async-start | bytes 524288 | tf_op jit(solution)/shard_map/all_to_all | solution.py:238
  11.1 1.6 %collective-permute-start.1 = (f32[2,64,128]{2,1,0:T(8,128)S(1)}, f32[2,64,128]{2,1,0:T(8,128)S(1)}, u32[]{:S(2)}, u32[]{:S(2)}) collective-permute-start(f32[2,64,128]{2,1,0:T(8,128)S(1)} %pad_maximum_fusion), channel_id=1, source_target_pairs={{0,16},{8,24},{16,0},{24,8},{1,17},{9,25},{17,1},{25,9},{2,18},{10... | collective-permute-start | bytes 196616 | tf_op jit(solution)/shard_map/ppermute | solution.py:444
  12.6 3.6 %field_sums.5 = (f32[48,1024]{1,0:T(8,128)S(1)}, bf16[2048,1024]{1,0:T(8,128)(2,1)S(1)}, bf16[2048,1024]{1,0:T(8,128)(2,1)S(1)}) custom-call(f32[64,128]{1,0:T(8,128)S(1)} %get-tuple-element.30.payload.refs_0_, f32[1,64,128]{2,1,0:T(8,128)S(1)} %bitcast.8, f32[1,64,128]{2,1,0:T(8,128)S(1)} %collective-permute-done.refs_2_), custom_call_target="tpu_custom_call" | custom-call | tf_op jit(solution)/shard_map/field_sums/pallas_call | solution.py:428
  16.3 0.0 collective-permute-done.1.refs_1_
  16.3 3.7 %field_sums.6 = (f32[24,128]{1,0:T(8,128)S(1)}, bf16[2048,1024]{1,0:T(8,128)(2,1)S(1)}, bf16[2048,1024]{1,0:T(8,128)(2,1)S(1)}) custom-call(f32[64,128]{1,0:T(8,128)S(1)} %get-tuple-element.30.payload.refs_0_, f32[2,64,128]{2,1,0:T(8,128)S(1)} %collective-permute-done.1.refs_1_, f32[48,1024]{1,0:T(8,128)S(1)} %get-tuple-element.36.refs_2_), custom_call_target="tpu_custom_call" | custom-call | tf_op jit(solution)/shard_map/field_sums/pallas_call | solution.py:428
  20.0 0.1 collective-permute-start.3
  20.1 0.7 %collective-permute-start.2 = (f32[1,24,128]{2,1,0:T(8,128)S(1)}, f32[1,24,128]{2,1,0:T(8,128)S(1)}, u32[]{:S(2)}, u32[]{:S(2)}) collective-permute-start(f32[1,24,128]{2,1,0:T(8,128)S(1)} %bitcast.11), channel_id=1, source_target_pairs={{0,16},{8,24},{16,0},{24,8},{1,17},{9,25},{17,1},{25,9},{2,18},{10... | collective-permute-start | bytes 36872 | tf_op jit(solution)/shard_map/ppermute | solution.py:444
  20.7 0.5 %collective-permute-done.3.refs_5_ = f32[1,24,128]{2,1,0:T(8,128)S(1)} collective-permute-done((f32[1,24,128]{2,1,0:T(8,128)S(1)}, f32[1,24,128]{2,1,0:T(8,128)S(1)}, u32[]{:S(2)}, u32[]{:S(2)}) %collective-permute-start.3) | collective-permute-done | bytes 12320 | tf_op jit(solution)/shard_map/ppermute | solution.py:444
  21.2 1.9 %field_sums.7.refs_6_ = f32[48,1024]{1,0:T(8,128)S(1)} custom-call(f32[64,128]{1,0:T(8,128)S(1)} %get-tuple-element.30.payload.refs_0_, f32[1,64,128]{2,1,0:T(8,128)S(1)} %bitcast.9, f32[1,64,128]{2,1,0:T(8,128)S(1)} %collective-permute-done.refs_2_, f32[24,128]{1,0:T(8,128)S(1)} %get-tuple-element.37.refs_3_.refs_2_, f32[1,24,128]{2,1,0:T(8,128)S(1)} %bitcast.12, ...), custom_call_target="tpu_custom_call" | custom-call | tf_op jit(solution)/shard_map/field_sums/pallas_call | solution.py:428
  23.1 0.7 %collective-permute-done.2.refs_3_ = f32[1,24,128]{2,1,0:T(8,128)S(1)} collective-permute-done((f32[1,24,128]{2,1,0:T(8,128)S(1)}, f32[1,24,128]{2,1,0:T(8,128)S(1)}, u32[]{:S(2)}, u32[]{:S(2)}) %collective-permute-start.2) | collective-permute-done | bytes 12320 | tf_op jit(solution)/shard_map/ppermute | solution.py:444
  23.8 0.0 collective-permute-start.4
  23.8 1.1 %field_sums.8.refs_6_ = f32[48,1024]{1,0:T(8,128)S(1)} custom-call(f32[64,128]{1,0:T(8,128)S(1)} %get-tuple-element.30.payload.refs_0_, f32[2,64,128]{2,1,0:T(8,128)S(1)} %collective-permute-done.1.refs_1_, f32[24,128]{1,0:T(8,128)S(1)} %get-tuple-element.37.refs_3_.refs_2_, f32[1,24,128]{2,1,0:T(8,128)S(1)} %collective-permute-done.2.refs_3_, ...), custom_call_target="tpu_custom_call" | custom-call | tf_op jit(solution)/shard_map/field_sums/pallas_call | solution.py:428
  24.9 0.1 collective-permute-done.4.refs_3_
  25.0 1.7 %field_sums.9 = (f32[24,128]{1,0:T(8,128)S(1)}, f32[8,24,128]{2,1,0:T(8,128)}) custom-call(f32[64,128]{1,0:T(8,128)S(1)} %get-tuple-element.30.payload.refs_0_, f32[2,64,128]{2,1,0:T(8,128)S(1)} %collective-permute-done.1.refs_1_, f32[24,128]{1,0:T(8,128)S(1)} %get-tuple-element.37.refs_3_.refs_2_, f32[1,24,128]{2,1,0:T(8,128)S(1)} %collective-permute-done.4.refs_3_, ...), custom_call_target="tpu_custom_call" | custom-call | tf_op jit(solution)/shard_map/field_sums/pallas_call | solution.py:428
  26.7 0.0 all-to-all-done.received
  26.7 5.1 %all-to-all-start.1 = ((f32[8,24,128]{2,1,0:T(8,128)}), f32[8,24,128]{2,1,0:T(8,128)S(1)}, u32[]{:S(2)}, u32[]{:S(2)}) async-start(f32[8,24,128]{2,1,0:T(8,128)} %get-tuple-element.49), calls=%async_computation.1 | async-start | bytes 196608 | tf_op jit(solution)/shard_map/all_to_all | solution.py:238
  31.8 3.4 %contact_geometry.1 = (f32[3,1024]{1,0:T(4,128)}, f32[8,8,8,128]{3,2,1,0:T(8,128)S(1)}, s32[2,2,8,512]{3,2,1,0:T(8,128)S(1)}, bf16[8192,128]{1,0:T(8,128)(2,1)S(1)}) custom-call(f32[48,128]{1,0:T(8,128)S(1)} %get-tuple-element.31.table, s32[9,8,128]{2,1,0:T(8,128)S(1)} %get-tuple-element.32.listed, f32[8,64,128]{2,1,0:T(8,128)S(1)} %all-to-all-done.received, ...), custom_call_target="tpu_custom_call" | custom-call | tf_op jit(solution)/shard_map/contact_geometry/pallas_call | solution.py:428
  35.1 0.3 all-to-all-done.1.mom_received
  35.4 1.4 %contact_force.1 = f32[3,1024]{1,0:T(4,128)} custom-call(f32[8,8,8,128]{3,2,1,0:T(8,128)S(1)} %get-tuple-element.46.geometry, s32[2,2,8,512]{3,2,1,0:T(8,128)S(1)} %get-tuple-element.47.places, bf16[8192,128]{1,0:T(8,128)(2,1)S(1)} %get-tuple-element.48.hot, f32[8,24,128]{2,1,0:T(8,128)S(1)} %all-to-all-done.1.mom_received), custom_call_target="tpu_custom_call" | custom-call | tf_op jit(solution)/shard_map/contact_force/pallas_call | solution.py:428
  (1 shorter events, 0.0 us)
Async XLA Ops:
  1.5 1.4 %collective-permute-start = (f32[1,64,128]{2,1,0:T(8,128)S(1)}, f32[1,64,128]{2,1,0:T(8,128)S(1)}, u32[]{:S(2)}, u32[]{:S(2)}) collective-permute-start(f32[1,64,128]{2,1,0:T(8,128)S(1)} %bitcast.6), channel_id=1, source_target_pairs={{0,8},{8,0},{16,24},{24,16},{1,9},{9,1},{17,25},{25,17},{2,10},{10... | collective-permute-start | bytes 98312 | tf_op jit(solution)/shard_map/ppermute | solution.py:444
  2.9 23.8 %all-to-all-start = ((f32[8,64,128]{2,1,0:T(8,128)}), f32[8,64,128]{2,1,0:T(8,128)S(1)}, u32[]{:S(2)}, u32[]{:S(2)}) async-start(f32[8,64,128]{2,1,0:T(8,128)} %get-tuple-element.34), calls=%async_computation | async-start | bytes 524288 | tf_op jit(solution)/shard_map/all_to_all | solution.py:238
  11.1 5.2 %collective-permute-start.1 = (f32[2,64,128]{2,1,0:T(8,128)S(1)}, f32[2,64,128]{2,1,0:T(8,128)S(1)}, u32[]{:S(2)}, u32[]{:S(2)}) collective-permute-start(f32[2,64,128]{2,1,0:T(8,128)S(1)} %pad_maximum_fusion), channel_id=1, source_target_pairs={{0,16},{8,24},{16,0},{24,8},{1,17},{9,25},{17,1},{25,9},{2,18},{10... | collective-permute-start | bytes 196616 | tf_op jit(solution)/shard_map/ppermute | solution.py:444
  20.0 1.2 %collective-permute-start.3 = (f32[1,24,128]{2,1,0:T(8,128)S(1)}, f32[1,24,128]{2,1,0:T(8,128)S(1)}, u32[]{:S(2)}, u32[]{:S(2)}) collective-permute-start(f32[1,24,128]{2,1,0:T(8,128)S(1)} %bitcast.10), channel_id=1, source_target_pairs={{0,8},{8,0},{16,24},{24,16},{1,9},{9,1},{17,25},{25,17},{2,10},{10... | collective-permute-start | bytes 36872 | tf_op jit(solution)/shard_map/ppermute | solution.py:444
  20.1 3.8 %collective-permute-start.2 = (f32[1,24,128]{2,1,0:T(8,128)S(1)}, f32[1,24,128]{2,1,0:T(8,128)S(1)}, u32[]{:S(2)}, u32[]{:S(2)}) collective-permute-start(f32[1,24,128]{2,1,0:T(8,128)S(1)} %bitcast.11), channel_id=1, source_target_pairs={{0,16},{8,24},{16,0},{24,8},{1,17},{9,25},{17,1},{25,9},{2,18},{10... | collective-permute-start | bytes 36872 | tf_op jit(solution)/shard_map/ppermute | solution.py:444
  23.8 1.2 %collective-permute-start.4 = (f32[1,24,128]{2,1,0:T(8,128)S(1)}, f32[1,24,128]{2,1,0:T(8,128)S(1)}, u32[]{:S(2)}, u32[]{:S(2)}) collective-permute-start(f32[1,24,128]{2,1,0:T(8,128)S(1)} %collective-permute-done.2.refs_3_), channel_id=1, source_target_pairs={{0,8},{8,0},{16,24},{24,16},{1,9},{9,1},{17,25},{25,17},{2,10},{10... | collective-permute-start | bytes 36872 | tf_op jit(solution)/shard_map/ppermute | solution.py:444
  26.7 8.7 %all-to-all-start.1 = ((f32[8,24,128]{2,1,0:T(8,128)}), f32[8,24,128]{2,1,0:T(8,128)S(1)}, u32[]{:S(2)}, u32[]{:S(2)}) async-start(f32[8,24,128]{2,1,0:T(8,128)} %get-tuple-element.49), calls=%async_computation.1 | async-start | bytes 196608 | tf_op jit(solution)/shard_map/all_to_all | solution.py:238
